TPU v7x, 32 devices: a whole 2x2x4 slice. The times are simulated.
32 devices in a mesh: dp: 8 (over z, core), fsdp: 4 (over y, x).
Axes of the slice: x: 2, y: 2, z: 4, core: 2. Of those that a mesh axis runs over, the one named last changes fastest.
Arguments:
- tokens: bfloat16 [32768, 768], P(('dp', 'fsdp')), may hold values from -6 to 6
- bucket: int32 [32], P(('dp', 'fsdp')), may hold values from 0 to 1, as said below
- lengths: int32 [32, 8], P(('dp', 'fsdp')), may hold values from 0 to 512, as said below
- cotangent: bfloat16 [32768, 768], P(('dp', 'fsdp')), may hold values from -6 to 6
- query_weight: bfloat16 [768, 768], P('dp', 'fsdp'), may hold values from -0.21875 to 0.21875
- query_bias: bfloat16 [768], P('fsdp'), may hold values from -3 to 3
- key_weight: bfloat16 [768, 768], P('dp', 'fsdp'), may hold values from -0.21875 to 0.21875
- value_weight: bfloat16 [768, 768], P('dp', 'fsdp'), may hold values from -0.21875 to 0.21875
- value_bias: bfloat16 [768], P('fsdp'), may hold values from -0.625 to 0.625
- out_weight: bfloat16 [768, 768], P('dp', 'fsdp'), may hold values from -2.5 to 2.5
- out_bias: bfloat16 [768], P('fsdp'), may hold values from -3 to 3
- norm1_gain: bfloat16 [768], P('fsdp'), may hold values from 0.5 to 1.5
- norm1_bias: bfloat16 [768], P('fsdp'), may hold values from -1.75 to 1.75
- up_weight: bfloat16 [768, 3072], P('dp', 'fsdp'), may hold values from -0.21875 to 0.21875
- up_bias: bfloat16 [3072], P('fsdp'), may hold values from -3 to 3
- down_weight: bfloat16 [3072, 768], P('dp', 'fsdp'), may hold values from -0.109375 to 0.109375
- down_bias: bfloat16 [768], P('fsdp'), may hold values from -3 to 3
- norm2_gain: bfloat16 [768], P('fsdp'), may hold values from 0.5 to 1.5
- norm2_bias: bfloat16 [768], P('fsdp'), may hold values from -1.75 to 1.75
Outputs:
- out_tokens: bfloat16 [32768, 768], P(('dp', 'fsdp'))
- pooled: float32 [256, 768], P(('dp', 'fsdp'))
- input_grad: float32 [32768, 768], P(('dp', 'fsdp'))
- grad_query_weight: float32 [768, 768], P('dp', 'fsdp')
- grad_query_bias: float32 [768], P('fsdp')
- grad_key_weight: float32 [768, 768], P('dp', 'fsdp')
- grad_value_weight: float32 [768, 768], P('dp', 'fsdp')
- grad_value_bias: float32 [768], P('fsdp')
- grad_out_weight: float32 [768, 768], P('dp', 'fsdp')
- grad_out_bias: float32 [768], P('fsdp')
- grad_norm1_gain: float32 [768], P('fsdp')
- grad_norm1_bias: float32 [768], P('fsdp')
- grad_up_weight: float32 [768, 3072], P('dp', 'fsdp')
- grad_up_bias: float32 [3072], P('fsdp')
- grad_down_weight: float32 [3072, 768], P('dp', 'fsdp')
- grad_down_bias: float32 [768], P('fsdp')
- grad_norm2_gain: float32 [768], P('fsdp')
- grad_norm2_bias: float32 [768], P('fsdp')
Inputs may be any that keep to these rules, and one draw needn't show every extreme that they name: `bucket`: both values occur. A device with 1 holds 2 passages of 512 rows, one with 0 holds 8 queries of 128 rows. `lengths`: entry j is the live length of the device's j-th sequence, 1 to 512 for passages and 1 to 128 for queries; entries j >= 2 of a passage device are 0. Some passage has 512 live tokens and some query 128.
All inputs are finite; a program needn't handle non-finite values.
Results may differ from a plain program's by a relative error of at most 0.02.
Values may be sent and summed in bfloat16 or wider, within the bound.
No kernel may reach another device: no remote copies, remote signals or barrier semaphores. Data moves between devices by JAX's collectives and lax.ppermute only.
A program may use at most 192 MiB of HBM per device.

v0:
```python
import functools

import jax
import jax.numpy as jnp
from jax import lax
from jax.experimental import pallas as pl
from jax.experimental.pallas import tpu as pltpu
from jax.sharding import PartitionSpec as P

H = 12
HD = 64
PLEN = 512
QLEN = 128
PAIR = 2 * HD
ROWS = 256
FEED_ROWS = 512

epsilon = 1e-06
masked_score = -1e30
f32 = jnp.float32
bf16 = jnp.bfloat16
LIMIT = 60 * 1024 * 1024
SMALL = 24 * 1024 * 1024


def dot(left, right):
    return jnp.dot(left, right, preferred_element_type=f32)


def dot_nt(left, right):
    return lax.dot_general(left, right, (((1,), (1,)), ((), ())), preferred_element_type=f32)


def dot_tn(left, right):
    return lax.dot_general(left, right, (((0,), (0,)), ((), ())), preferred_element_type=f32)


BIG = 16 * 1024


def far(v, least):
    if v.size * v.dtype.itemsize < least:
        return v
    return pltpu.with_memory_space_constraint(v, pltpu.HBM)


def call(
    kernel, name, grid, in_specs, out_specs, out_shape, scratch=(), prefetch=0, cost=None, limit=LIMIT, aliases={},
    least=BIG, free=pltpu.VMEM,
):
    several = isinstance(out_shape, list)
    shapes = [
        pltpu.HBM(v.shape, v.dtype)
        if isinstance(v, jax.ShapeDtypeStruct) and v.size * v.dtype.itemsize >= BIG else v
        for v in (out_shape if several else [out_shape])
    ]
    run = pl.pallas_call(
        kernel,
        name=name,
        grid_spec=pltpu.PrefetchScalarGridSpec(
            num_scalar_prefetch=prefetch,
            grid=grid,
            in_specs=in_specs,
            out_specs=out_specs,
            scratch_shapes=list(scratch),
        ),
        out_shape=shapes if several else shapes[0],
        input_output_aliases=aliases,
        compiler_params=pltpu.CompilerParams(
            vmem_limit_bytes=limit, dimension_semantics=("arbitrary",) * len(grid)
        ),
        cost_estimate=cost,
    )

    def run_far(*args):
        given = [
            v if spec.memory_space in (pltpu.VMEM, free) else far(v, least) for v, spec in zip(args[prefetch:], in_specs)
        ]
        return run(*args[:prefetch], *given)

    return run_far


def whole(shape):
    return pl.BlockSpec(shape, lambda *_: (0,) * len(shape))


def sds(shape, dtype):
    return jax.ShapeDtypeStruct(shape, dtype)


def held():
    return pl.BlockSpec(memory_space=pltpu.VMEM)


def guess(flops, nbytes):
    return pl.CostEstimate(flops=int(flops), bytes_accessed=int(nbytes), transcendentals=0)


def reverse(s, bits):
    return sum(((s >> b) & 1) << (bits - 1 - b) for b in range(bits))


def axis_facts():
    dp, fsdp = lax.axis_size("dp"), lax.axis_size("fsdp")
    return dp, fsdp, dp // 2, fsdp.bit_length() - 1


def along_z(hop):
    dp = lax.axis_size("dp")
    return [(d, (d + 2 * hop) % dp) for d in range(dp)]


def across_cores():
    return [(d, d ^ 1) for d in range(lax.axis_size("dp"))]


def along_bit(r):
    dp, fsdp, _, bits = axis_facts()
    pairs = []
    for d in range(dp):
        flip = 1 << (r if d % 2 == 0 else bits - 1 - r)
        pairs += [(d * fsdp + f, d * fsdp + (f ^ flip)) for f in range(fsdp)]
    return pairs


def select_core(even, odd):
    return jnp.where(lax.axis_index("dp") % 2 == 0, even, odd)


def gather_z(block):
    dp = lax.axis_size("dp")
    groups = [list(range(core, dp, 2)) for core in range(2)]
    return lax.all_gather(block, "dp", axis=0, axis_index_groups=groups)


class Gather:
    def __init__(self, along):
        self.held, self.round, self.blocks = along[None], 0, None

    def stage(self):
        bits = axis_facts()[3]
        if self.round < bits:
            return [(self.held, ("dp", "fsdp"), along_bit(self.round))]
        return [(v, "dp", across_cores()) for v in self.own]

    def take(self, got):
        bits = axis_facts()[3]
        if self.round < bits - 1:
            self.held = jnp.concatenate([self.held] + got)
        elif self.round < bits:
            self.own = [self.held] + got
        else:
            self.blocks = self.own + got
        self.round += 1

    def done(self):
        return self.blocks is not None


class Once:
    def __init__(self, sends):
        self.sends, self.got = sends, None

    def stage(self):
        return self.sends

    def take(self, got):
        self.got = got

    def done(self):
        return self.got is not None


def add(left, right):
    return (left.astype(f32) + right.astype(f32)).astype(bf16)


class Scatter:
    def __init__(self, keep, send):
        self.keep, self.send, self.round, self.total = keep, [send], axis_facts()[3], None

    def stage(self):
        _, _, depth, bits = axis_facts()
        if self.round == bits:
            return [(self.send[0], "dp", across_cores())]
        if self.round >= 0:
            return [(self.send[0], ("dp", "fsdp"), along_bit(self.round))]
        return [(self.send[s - 1], "dp", along_z(-s)) for s in range(1, depth)]

    def take(self, got):
        depth = axis_facts()[2]
        keep = self.keep
        if self.round > 0:
            half = keep.shape[0] // 2
            self.send = [add(keep[half:], got[0][half:])]
            self.keep = add(keep[:half], got[0][:half])
        elif self.round == 0:
            self.send = [add(keep[0, s], got[0][0, s]) for s in range(1, depth)]
            self.keep = keep[0, 0].astype(f32) + got[0][0, 0].astype(f32)
        else:
            for part in got:
                keep = keep + part.astype(f32)
            self.total = keep
        self.round -= 1

    def done(self):
        return self.total is not None


def beside(moves, compute=None, args=(), key=0, out=0):
    moves = [move for move in moves if not move.done()]
    stages = [move.stage() for move in moves]
    arrays = [[v for v, _, _ in stage] for stage in stages]
    args = list(args)
    results = ()
    if compute:
        args[key], arrays = lax.optimization_barrier((args[key], arrays))
        results = list(compute(*args))
    else:
        arrays = lax.optimization_barrier(arrays)
    got = [
        [lax.ppermute(v, axis, perm) for v, (_, axis, perm) in zip(sent, stage)]
        for sent, stage in zip(arrays, stages)
    ]
    if compute:
        results[out], got = lax.optimization_barrier((results[out], got))
    else:
        got = lax.optimization_barrier(got)
    for move, parts in zip(moves, got):
        move.take(parts)
    return results


def finish(move):
    while not move.done():
        beside([move])


def places():
    dp, fsdp, depth, bits = axis_facts()
    d, f = lax.axis_index("dp"), lax.axis_index("fsdp")
    z, core = d // 2, d % 2
    slot = jnp.arange(depth, dtype=jnp.int32)
    index = jnp.arange(fsdp, dtype=jnp.int32)
    mirror = sum((((index >> b) & 1) << (bits - 1 - b) for b in range(bits)), jnp.zeros_like(index))
    rows, slots, columns = [], [], []
    for n in range(2):
        there = core ^ n
        rows.append(2 * ((z - slot) % depth) + there)
        away = index ^ f
        mirrored = sum((((away >> b) & 1) << (bits - 1 - b) for b in range(bits)), jnp.zeros_like(index))
        slots.append(jnp.where(there == 0, away, mirrored))
        columns.append(f ^ jnp.where(there == 0, index, mirror))
    neighbours = [(f ^ s)[None] for s in range(fsdp)]
    return jnp.concatenate(rows + slots + columns + [core[None]] + neighbours).astype(jnp.int32)


def row_of(place, n, slot, depth):
    return place[n * depth + slot]


def slot_of(place, n, j, depth, fsdp):
    return place[2 * depth + n * fsdp + j]


def column_of(place, n, s, depth, fsdp):
    return place[2 * depth + 2 * fsdp + n * fsdp + s]


def core_of(place, depth, fsdp):
    return place[2 * depth + 4 * fsdp]


def neighbour_of(place, s, depth, fsdp):
    return place[2 * depth + 4 * fsdp + 1 + s]


def block_copies(place, arrays, target, sems):
    half, depth = arrays[0].shape[:2]
    fsdp = 2 * half
    copies = []
    for a, array in enumerate(arrays):
        core = lax.rem(core_of(place, depth, fsdp) + a // 2, 2)
        for q in range(half):
            j = column_of(place, a // 2, (a % 2) * half + q, depth, fsdp)
            copies.append(pltpu.make_async_copy(array.at[q], target(core, j), sems.at[len(copies)]))
    return copies


def assemble_kernel(place, own_low, own_high, other_low, other_high, weights, vectors, ub):
    step = pl.program_id(0)
    half, _, height, width = own_low.shape
    fsdp, depth, tall = 2 * half, pl.num_programs(0) // 2, height - 16
    narrow = width // 4

    def fill(n, low, high):
        pieces = []
        for j in range(fsdp):
            slot = slot_of(place, n, j, depth, fsdp)
            upper, q = slot >= half, lax.rem(slot, half)
            pieces.append(jnp.where(upper, high[q, 0].astype(f32), low[q, 0].astype(f32)))
        for m in range(4):
            row = jnp.concatenate([p[:, m * narrow:(m + 1) * narrow] for p in pieces], axis=1)
            weights[m] = row[:tall].astype(bf16)
            vectors[m] = row[tall:]
        for j in range(fsdp):
            ub[j] = pieces[j][tall:]

    @pl.when(step < depth)
    def _():
        fill(0, own_low, own_high)

    @pl.when(step >= depth)
    def _():
        fill(1, other_low, other_high)


def row_at(place, s, depth, fsdp):
    core = core_of(place, depth, fsdp)
    return 2 * lax.rem(s, depth) + lax.rem(core + s // depth, 2)


def assemble(place, arrays):
    half, depth, height, width = arrays[0].shape
    fsdp, tall, d = 2 * half, height - 16, half * width // 2
    own = pl.BlockSpec((half, 1, height, width), lambda s, place: (0, jnp.minimum(s, depth - 1), 0, 0))
    other = pl.BlockSpec((half, 1, height, width), lambda s, place: (0, jnp.maximum(s - depth, 0), 0, 0))
    return call(
        assemble_kernel, "assemble", (2 * depth,),
        [own, own, other, other],
        [pl.BlockSpec((4, tall, d), lambda s, place: (0, row_at(place, s, depth, fsdp), 0)), whole((4, 16, d)),
         whole((fsdp, 16, width))],
        [sds((4, 2 * depth * tall, d), bf16), sds((4, 16, d), f32), sds((fsdp, 16, width), f32)],
        prefetch=1, cost=guess(1e9, 11e6),
    )(place, *arrays)


def pack_kernel(place, gq, gk, gv, go, vectors, gub, send, keep):
    step = pl.program_id(0)
    fsdp, _, height, width = send.shape
    depth, tall, narrow = pl.num_programs(0) // 2, height - 16, width // 4

    def fill(n, out):
        for j in range(fsdp):
            slot = slot_of(place, n, j, depth, fsdp)
            columns = slice(j * narrow, (j + 1) * narrow)
            out[slot, 0, :tall, :] = jnp.concatenate(
                [g[:, columns].astype(f32) for g in (gq, gk, gv, go)], axis=1
            ).astype(bf16)
            slab = jnp.concatenate([vectors[m, :, columns] for m in range(4)], axis=1)
            third = lax.broadcasted_iota(jnp.int32, slab.shape, 0) == 2
            out[slot, 0, tall:, :] = jnp.where(third, gub[j], slab).astype(bf16)

    @pl.when(step < depth)
    def _():
        fill(1, send)

    @pl.when(step >= depth)
    def _():
        fill(0, keep)


def pack(place, grads, vectors, gub):
    d = grads[0].shape[0]
    dp, fsdp, depth, _ = axis_facts()
    tall, width = d // dp, 4 * d // fsdp
    rows = pl.BlockSpec((tall, d), lambda s, place: (place[(s + depth) % (2 * depth)], 0))
    sent = pl.BlockSpec((fsdp, 1, tall + 16, width), lambda s, place: (0, jnp.minimum(s, depth - 1), 0, 0))
    kept = pl.BlockSpec((fsdp, 1, tall + 16, width), lambda s, place: (0, jnp.maximum(s - depth, 0), 0, 0))
    return call(
        pack_kernel, "pack", (2 * depth,),
        [rows, rows, rows, rows, whole((4, 16, d)), whole((fsdp, 1, width))],
        [sent, kept],
        [sds((fsdp, depth, tall + 16, width), bf16)] * 2,
        prefetch=1, cost=guess(1e9, 11e6),
    )(place, *grads, vectors, gub)


def segment_lanes(bucket, lengths, queries_ext, keys_ext):
    row_count = queries_ext.shape[0]
    slots = lengths.shape[0]
    shape = (row_count, PAIR)
    row = lax.broadcasted_iota(jnp.int32, shape, 0)
    lane = lax.broadcasted_iota(jnp.int32, shape, 1) % HD
    passage = bucket[0] == 1
    segment = jnp.where(passage, row // PLEN, row // QLEN)
    position = jnp.where(passage, row % PLEN, row % QLEN)
    limit = jnp.zeros(shape, jnp.int32)
    for s in range(slots):
        limit = jnp.where(segment == s, lengths[s], limit)
    alive = position < limit
    same = segment == lane
    queries_ext[...] = jnp.where(same, 1.0, 0.0).astype(bf16)
    keys_ext[...] = jnp.where((lane < slots) & ~(same & alive), masked_score, 0.0).astype(bf16)


def attend_kernel(
    bucket, lengths, x, qw, kw, vw, qb, vb,
    q_out, k_out, v_out, context_out, lse_out,
    queries_ext, keys_ext, lse_all,
):
    pair = pl.program_id(0)
    row_count = x.shape[0]

    @pl.when(pair == 0)
    def _():
        segment_lanes(bucket, lengths, queries_ext, keys_ext)
        lse_all[...] = jnp.zeros_like(lse_all)

    weights = jnp.concatenate([qw[0], kw[0], vw[0]], axis=1)
    qb_row = qb[...]
    vb_row = vb[...]
    low_half = lax.broadcasted_iota(jnp.int32, (PLEN, PAIR), 1) < HD
    lane = lax.broadcasted_iota(jnp.int32, (PLEN, PAIR), 1)

    def block(b, carry):
        rows = pl.ds(pl.multiple_of(b * PLEN, PLEN), PLEN)
        qkv = dot(x[rows, :], weights)
        queries = ((qkv[:, :PAIR] + qb_row).astype(bf16).astype(f32) * HD ** (-0.5)).astype(bf16)
        keys = qkv[:, PAIR:2 * PAIR].astype(bf16)
        values = (qkv[:, 2 * PAIR:] + vb_row).astype(bf16)
        q_out[rows, :] = queries
        k_out[rows, :] = keys
        v_out[rows, :] = values
        q_ext = queries_ext[rows, :]
        k_ext = keys_ext[rows, :]
        ones = jnp.ones_like(values)
        sums, tops = [], []
        for half in range(2):
            mine = low_half if half == 0 else ~low_half
            scores = dot_nt(jnp.where(mine, queries, q_ext), jnp.where(mine, keys, k_ext))
            top = jnp.max(scores, axis=-1, keepdims=True)
            weight = jnp.exp(scores - top).astype(bf16)
            sums.append(dot(weight, jnp.where(mine, values, ones)))
            tops.append(top)
        numer = jnp.where(low_half, sums[0], sums[1])
        denom = pltpu.roll(jnp.where(low_half, sums[1], sums[0]), HD, 1)
        context_out[rows, :] = (numer / denom).astype(bf16)
        lse = jnp.where(low_half, tops[0], tops[1]) + jnp.log(denom)
        mine = (lane % HD) == pair
        lse_all[rows, :] = jnp.where(mine, lse, lse_all[rows, :])
        return carry

    lax.fori_loop(0, row_count // PLEN, block, 0)

    @pl.when(pair == pl.num_programs(0) - 1)
    def _():
        lse_out[...] = lse_all[...].T


def attend(bucket, lengths, x, weights, qb, vb):
    t, d = x.shape
    pairs = d // PAIR
    column = lambda m: pl.BlockSpec((1, d, PAIR), lambda p, *_: (m, 0, p))
    vector = pl.BlockSpec((1, PAIR), lambda p, *_: (0, p))
    tall = pl.BlockSpec((t, PAIR), lambda p, *_: (0, p))
    return call(
        attend_kernel, "attend", (pairs,),
        [whole((t, d)), column(0), column(1), column(2), vector, vector],
        [tall, tall, tall, tall, whole((PAIR, t))],
        [sds((t, d), bf16)] * 4 + [sds((PAIR, t), f32)],
        [pltpu.VMEM((t, PAIR), bf16), pltpu.VMEM((t, PAIR), bf16), pltpu.VMEM((t, PAIR), f32)],
        prefetch=2, cost=guess(15e9, 12e6),
    )(bucket, lengths, x, weights, weights, weights, qb, vb)


HEADS = 3
USED = 5 * PAIR


def block_kernel(q, k, v, o, *refs):
    *vectors, ub, out = refs
    tall = q.shape[0]
    out[:tall, :] = jnp.concatenate(
        [part.astype(f32) for part in (
            q[:, :PAIR], k[:, :PAIR], v[:, :PAIR], q[:, PAIR:], k[:, PAIR:], v[:, PAIR:], o[...]
        )], axis=1
    ).astype(bf16)
    each = [v[...].astype(f32)[None, :] for v in vectors]
    first, second = jnp.concatenate(each[:4], axis=1), jnp.concatenate(each[4:], axis=1)
    third = ub[...].astype(f32)[None, :]
    row = lax.broadcasted_iota(jnp.int32, (16, out.shape[1]), 0)
    out[tall:, :] = jnp.where(
        row == 0, first, jnp.where(row == 1, second, jnp.where(row == 2, third, 0.0))
    ).astype(bf16)


def make_block(q, k, v, o, *vectors):
    tall, narrow = q.shape
    out = (tall + 16, 4 * narrow)
    return call(
        block_kernel, "block", (1,), [whole(q.shape)] * 4 + [whole(u.shape) for u in vectors], whole(out),
        sds(out, bf16), cost=guess(1e6, 1e6), limit=SMALL, least=0,
    )(q, k, v, o, *vectors)


def unblock_kernel(total, *refs):
    got, (gq, gk, gv, go, *vectors) = refs[:-13], refs[-13:]
    tall, narrow = gq.shape
    block = total[...]
    for part in got:
        block = block + part[...].astype(f32)

    def split(v):
        return (
            jnp.concatenate([v[:, :PAIR], v[:, 3 * PAIR:3 * PAIR + HD]], axis=1),
            jnp.concatenate([v[:, PAIR:2 * PAIR], v[:, 3 * PAIR + HD:4 * PAIR]], axis=1),
            jnp.concatenate([v[:, 2 * PAIR:3 * PAIR], v[:, 4 * PAIR:4 * PAIR + HD]], axis=1),
            v[:, 4 * PAIR + HD:],
        )

    gq[...], gk[...], gv[...], go[...] = split(block[:tall])
    qb, _, vb, ob = split(block[tall:tall + 1])
    rest = [block[tall + r:tall + r + 1, m * narrow:(m + 1) * narrow] for r, m in ((1, 0), (1, 1), (1, 2), (1, 3), (2, 0))]
    for ref, row in zip(vectors, (qb, vb, ob, *rest, block[tall + 3:tall + 4])):
        ref[...] = row[0]


def unblock(total, got):
    height, width = total.shape
    tall, narrow = height - 16, width // 4
    shapes = [(tall, narrow)] * 4 + [(narrow,)] * 8 + [(width,)]
    return call(
        unblock_kernel, "unblock", (1,), [whole(total.shape)] * (1 + len(got)), [whole(v) for v in shapes],
        [sds(v, f32) for v in shapes], cost=guess(1e6, 1e6), limit=SMALL,
    )(total, *got)


def line_up_kernel(place, *refs):
    out = refs[-1]
    depth = len(refs) - 1
    for s in range(depth):
        out[row_of(place, 0, s, depth) // 2] = refs[s][...]


def line_up(place, parts):
    shape = parts[0].shape
    out = (len(parts), *shape)
    return call(
        line_up_kernel, "line_up", (1,), [whole(shape)] * len(parts), whole(out), sds(out, parts[0].dtype),
        prefetch=1, cost=guess(1e6, 1e6), limit=SMALL,
    )(place, *parts)


def attend_one_kernel(
    away, place, bucket, lengths, x, own, other, *refs,
):
    context_out, w_out, slab_out, kept, lse_out, queries_ext, keys_ext, weights_here, sems = refs[-9:]
    depth, _, tall, width = weights_here.shape
    step, fsdp = pl.program_id(0), w_out_fsdp(place, depth)
    core = core_of(place, depth, fsdp)
    j = neighbour_of(place, away, depth, fsdp)
    copies = [
        pltpu.make_async_copy(ref.at[:, :tall, :], weights_here.at[:, lax.rem(core + n, 2)], sems.at[n])
        for n, ref in enumerate((own, other))
    ]
    copies.append(pltpu.make_async_copy(own.at[0, tall:, :], slab_out.at[0], sems.at[2]))
    onward = pltpu.make_async_copy(weights_here, w_out.at[j], sems.at[3])

    @pl.when(step == 0)
    def _():
        for copy in copies:
            copy.start()
        segment_lanes(bucket, lengths, queries_ext, keys_ext)
        for copy in copies:
            copy.wait()
        onward.start()

    narrow = width // 4
    row = slab_out[0, 0:1, :].astype(f32)
    qb, vb = row[:, :narrow], row[:, narrow:2 * narrow]
    none = jnp.zeros((1, PAIR), f32)
    bias = jnp.concatenate(
        [qb[:, :PAIR], none, vb[:, :PAIR], qb[:, PAIR:], none[:, :HD], vb[:, PAIR:], none[:, :HD]], axis=1
    )
    lane = lax.broadcasted_iota(jnp.int32, (PLEN, PAIR), 1)
    low_half = lane < HD
    scale = HD ** (-0.5)

    rows = pl.ds(pl.multiple_of(step * PLEN, PLEN), PLEN)
    weights = weights_here[:, :, :, :USED].reshape(2 * depth * tall, USED)
    qkv = dot(x[...], weights) + bias
    tiles = [qkv[:, n * PAIR:(n + 1) * PAIR].astype(bf16) for n in range(5)]
    tiles[0] = tiles[0] * jnp.array(scale, bf16)
    tiles[3] = jnp.where(low_half, tiles[3] * jnp.array(scale, bf16), tiles[3])
    for n in range(5):
        kept[:, n * PAIR:(n + 1) * PAIR] = tiles[n]
    queries, keys, values, both, values_two = tiles
    keys_two = pltpu.roll(both.astype(f32), HD, 1).astype(bf16)
    q_ext, k_ext = queries_ext[rows, :], keys_ext[rows, :]
    ones = jnp.ones_like(values)

    def one(mine, q, k, v):
        scores = dot_nt(jnp.where(mine, q, q_ext), jnp.where(mine, k, k_ext))
        top = jnp.max(scores, axis=-1, keepdims=True)
        weight = jnp.exp(scores - top).astype(bf16)
        return top, dot(weight, jnp.where(mine, v, ones))

    top_a, sum_a = one(low_half, queries, keys, values)
    top_b, sum_b = one(~low_half, queries, keys, values)
    top_c, sum_c = one(low_half, both, keys_two, values_two)
    denom = pltpu.roll(jnp.where(low_half, sum_b, sum_a), HD, 1)
    denom_c = pltpu.roll(sum_c, HD, 1)
    context_out[0, :, :PAIR] = (jnp.where(low_half, sum_a, sum_b) / denom).astype(bf16)
    context_out[0, :, PAIR:] = (sum_c / denom_c)[:, :HD].astype(bf16)
    lse_ab = jnp.where(low_half, top_a, top_b) + jnp.log(denom)
    lse_c = top_c + jnp.log(denom_c)
    every = jnp.where((lane >= 32) & low_half, lse_c, lse_ab).T
    lse_out[0:1, :] = every[0:1]
    lse_out[1:2, :] = every[HD:HD + 1]
    lse_out[2:3, :] = every[32:33]

    @pl.when(step == pl.num_programs(0) - 1)
    def _():
        onward.wait()


def w_out_fsdp(place, depth):
    return (place.shape[0] - 2 * depth - 1) // 5


def attend_one(away, fsdp, place, bucket, lengths, x, own, other, shared):
    t, d = x.shape
    depth, height, width = own.shape
    tall, narrow = height - 16, d // fsdp
    shapes = [(fsdp, t, narrow), (fsdp, depth, 2, tall, width), (fsdp, 16, width)]
    j = lambda place: neighbour_of(place, away, depth, fsdp)
    any_space = pl.BlockSpec(memory_space=pl.ANY)
    return call(
        functools.partial(attend_one_kernel, away), "attend", (t // PLEN,),
        [pl.BlockSpec((PLEN, d), lambda s, *_: (s, 0)), any_space, any_space] + [any_space] * len(shared),
        [
            pl.BlockSpec((1, PLEN, narrow), lambda s, place, *_: (j(place), s, 0)), any_space,
            pl.BlockSpec((1, 16, width), lambda s, place, *_: (j(place), 0, 0)),
            pl.BlockSpec((PLEN, USED), lambda s, *_: (s, 0)), pl.BlockSpec((8, PLEN), lambda s, *_: (0, s)),
        ],
        [sds(shape, bf16) for shape in shapes] + [sds((t, USED), bf16), sds((8, t), f32)],
        [pltpu.VMEM((t, PAIR), bf16), pltpu.VMEM((t, PAIR), bf16), pltpu.VMEM((depth, 2, tall, width), bf16),
         pltpu.SemaphoreType.DMA((4,))],
        prefetch=3, cost=guess(5e9, 8e6), limit=SMALL, free=pl.ANY,
        aliases={6 + n: n for n in range(len(shared))},
    )(place, bucket, lengths, x, own, other, *shared)


def attend_back_one_kernel(
    away, place, bucket, lengths, x_t_far, kept, grad_context, lse, delta, gow_far, inner, outer, gub,
    send, keep, grads_out,
    queries_ext, keys_ext, grads, found, sums, x_t, gow, sems,
):
    depth, height, width = send.shape
    tall = height - 16
    step, steps = pl.program_id(0), pl.num_programs(0)
    fsdp = w_out_fsdp(place, depth)
    core, j = core_of(place, depth, fsdp), neighbour_of(place, away, depth, fsdp)
    copies = [
        pltpu.make_async_copy(source, target, sems.at[n])
        for n, (source, target) in enumerate(((x_t_far, x_t), (gow_far.at[j], gow)))
    ]

    @pl.when(step == 0)
    def _():
        for copy in copies:
            copy.start()
        segment_lanes(bucket, lengths, queries_ext, keys_ext)
        sums[...] = jnp.zeros_like(sums)

    lane = lax.broadcasted_iota(jnp.int32, (PLEN, PAIR), 1)
    low_half = lane < HD
    scale = HD ** (-0.5)

    rows = pl.ds(pl.multiple_of(step * PLEN, PLEN), PLEN)
    queries, keys, values, both, values_two = (kept[:, n * PAIR:(n + 1) * PAIR] for n in range(5))
    keys_two = pltpu.roll(both.astype(f32), HD, 1).astype(bf16)
    q_ext, k_ext = queries_ext[rows, :], keys_ext[rows, :]
    nothing = jnp.zeros_like(values)
    grad_two = jnp.concatenate([grad_context[0, :, PAIR:]] * 2, axis=1)

    def one(a, mine, q, k, v, grad_ctx):
        scores = dot_nt(jnp.where(mine, k, k_ext), jnp.where(mine, q, q_ext))
        probs = jnp.exp(scores - lse[a:a + 1, :])
        grad_probs = dot_nt(jnp.where(mine, v, nothing), grad_ctx)
        grad_scores = (probs * (grad_probs - delta[0, a:a + 1, :])).astype(bf16)
        grad_v = dot(probs.astype(bf16), grad_ctx)
        grad_k = dot(grad_scores, q)
        grad_q = dot_tn(grad_scores, k) * scale
        return grad_q, grad_k, grad_v

    grad_pair = grad_context[0, :, :PAIR]
    q_a, k_a, v_a = one(0, low_half, queries, keys, values, grad_pair)
    q_b, k_b, v_b = one(1, ~low_half, queries, keys, values, grad_pair)
    q_c, k_c, v_c = one(2, low_half, both, keys_two, values_two, grad_two)
    made = [
        jnp.where(low_half, q_a, q_b), jnp.where(low_half, k_a, k_b), jnp.where(low_half, v_a, v_b),
        jnp.where(low_half, q_c, pltpu.roll(k_c, HD, 1)), jnp.where(low_half, v_c, 0.0),
    ]
    for n in range(5):
        low = made[n].astype(bf16)
        lanes = slice(n * PAIR, (n + 1) * PAIR)
        grads[rows, lanes] = low
        grads_out[:, lanes] = low
        sums[0:1, lanes] += jnp.sum(low.astype(f32), axis=0, keepdims=True)

    @pl.when(step == steps - 1)
    def _():
        for copy in copies:
            copy.wait()
        columns = grads[...]
        product = dot(x_t[...], columns)
        found[:, :4 * PAIR] = product[:, :4 * PAIR].astype(bf16)
        found[:, 4 * PAIR:] = jnp.concatenate(
            [product[:, 4 * PAIR:4 * PAIR + HD], gow[...].astype(f32)], axis=1
        ).astype(bf16)
        narrow = width // 4
        none = jnp.zeros((1, 3 * narrow), f32)
        inner_rows, outer_rows = inner[0], outer[0]
        first = jnp.concatenate([sums[0:1, :4 * PAIR + HD], inner_rows[2:3]], axis=1)
        second = jnp.concatenate([inner_rows[0:1], inner_rows[1:2], outer_rows[0:1], outer_rows[1:2]], axis=1)
        third = jnp.concatenate([outer_rows[2:3], none], axis=1)
        row = lax.broadcasted_iota(jnp.int32, (16, width), 0)
        rest = jnp.where(row == 1, second, jnp.where(row == 2, third, jnp.where(row == 3, gub[0], 0.0)))
        below = jnp.where(row == 0, first, rest).astype(bf16)
        for n, target in ((1, send), (0, keep)):
            for z in range(depth):
                i = 2 * z + lax.rem(core + n, 2)
                target[z, :tall, :] = found[pl.ds(pl.multiple_of(i * tall, 16), tall), :]
                target[z, tall:, :] = below


def attend_back_one(
    away, fsdp, depth, place, bucket, lengths, x_t, kept, grad_context, lse, delta, gow, inner, outer, gub
):
    d, t = x_t.shape
    tall, narrow, width = d // (2 * depth), d // fsdp, 4 * d // fsdp
    j = lambda place: neighbour_of(place, away, depth, fsdp)
    any_space = pl.BlockSpec(memory_space=pl.ANY)
    small = lambda *shape: pl.BlockSpec((1, *shape), lambda s, place, *_: (j(place), 0, 0))
    sent = (depth, tall + 16, width)
    rows = pl.BlockSpec((PLEN, USED), lambda s, *_: (s, 0))
    return call(
        functools.partial(attend_back_one_kernel, away), "attend_back", (t // PLEN,),
        [any_space, rows, pl.BlockSpec((1, PLEN, narrow), lambda s, place, *_: (j(place), s, 0)),
         pl.BlockSpec((8, PLEN), lambda s, *_: (0, s)),
         pl.BlockSpec((1, 8, PLEN), lambda s, place, *_: (j(place), 0, s)), any_space,
         small(8, narrow), small(8, narrow), small(1, width)],
        [whole(sent), whole(sent), rows],
        [sds(sent, bf16)] * 2 + [sds((t, USED), bf16)],
        [pltpu.VMEM((t, PAIR), bf16), pltpu.VMEM((t, PAIR), bf16), pltpu.VMEM((t, USED), bf16),
         pltpu.VMEM((d, width), bf16), pltpu.VMEM((8, USED), f32), pltpu.VMEM((d, t), bf16),
         pltpu.VMEM((d, narrow), bf16), pltpu.SemaphoreType.DMA((2,))],
        prefetch=3, cost=guess(10e9, 12e6), limit=SMALL,
    )(place, bucket, lengths, x_t, kept, grad_context, lse, delta, gow, inner, outer, gub)


def input_grad_kernel(place, inner, *refs):
    grads, weights, out = refs[:-2], refs[-2], refs[-1]
    fsdp, depth, _, tall, _ = weights.shape
    total = inner[...]
    for away, columns in enumerate(grads):
        held_weights = weights[neighbour_of(place, away, depth, fsdp)][:, :, :, :USED]
        total += dot_nt(columns[...], held_weights.reshape(2 * depth * tall, USED))
    out[...] = total


def make_input_grad(place, inner, grads, weights):
    t, d = inner.shape
    rows = pl.BlockSpec((ROWS, d), lambda r, *_: (r, 0))
    return [call(
        input_grad_kernel, "input_grad", (t // ROWS,),
        [rows] + [pl.BlockSpec((ROWS, USED), lambda r, *_: (r, 0))] * len(grads) + [whole(weights.shape)],
        rows, sds((t, d), f32), prefetch=1, cost=guess(5e9, 15e6), limit=SMALL,
    )(place, inner, *grads, weights)]


def attend_back_kernel(
    bucket, lengths, x_t, q, k, v, grad_context, lse, delta, qw, kw, vw, grad_inner,
    gqw, gkw, gvw, gqb, gvb, input_grad,
    queries_ext, keys_ext, grads,
):
    pair = pl.program_id(0)
    row_count = q.shape[0]

    @pl.when(pair == 0)
    def _():
        segment_lanes(bucket, lengths, queries_ext, keys_ext)

    low_half = lax.broadcasted_iota(jnp.int32, (PLEN, PAIR), 1) < HD

    def block(b, carry):
        rows = pl.ds(pl.multiple_of(b * PLEN, PLEN), PLEN)
        queries, keys, values, grad_ctx = q[rows, :], k[rows, :], v[rows, :], grad_context[rows, :]
        q_ext, k_ext = queries_ext[rows, :], keys_ext[rows, :]
        nothing = jnp.zeros_like(values)
        got = []
        for half in range(2):
            mine = low_half if half == 0 else ~low_half
            lse_row = lse[pl.ds(half * HD + pair, 1), rows]
            delta_row = delta[pl.ds(half * HD + pair, 1), rows]
            scores = dot_nt(jnp.where(mine, keys, k_ext), jnp.where(mine, queries, q_ext))
            probs = jnp.exp(scores - lse_row)
            grad_probs = dot_nt(jnp.where(mine, values, nothing), grad_ctx)
            grad_scores = (probs * (grad_probs - delta_row)).astype(bf16)
            grad_v = dot(probs.astype(bf16), grad_ctx)
            grad_k = dot(grad_scores, queries)
            grad_q = dot_tn(grad_scores, keys)
            got.append((grad_q, grad_k, grad_v))
        gq = (jnp.where(low_half, got[0][0], got[1][0]) * HD ** (-0.5)).astype(bf16)
        gk = jnp.where(low_half, got[0][1], got[1][1]).astype(bf16)
        gv = jnp.where(low_half, got[0][2], got[1][2]).astype(bf16)
        grads[rows, :PAIR] = gq
        grads[rows, PAIR:2 * PAIR] = gk
        grads[rows, 2 * PAIR:] = gv
        sum_q = jnp.sum(gq.astype(f32), axis=0, keepdims=True)
        sum_v = jnp.sum(gv.astype(f32), axis=0, keepdims=True)
        return (carry[0] + sum_q, carry[1] + sum_v)

    start = jnp.zeros((1, PAIR), f32)
    gqb[...], gvb[...] = lax.fori_loop(0, row_count // PLEN, block, (start, start))

    columns = grads[...]
    weight_grads = dot(x_t[...], columns)
    gqw[...] = weight_grads[:, :PAIR].astype(gqw.dtype)
    gkw[...] = weight_grads[:, PAIR:2 * PAIR].astype(gkw.dtype)
    gvw[...] = weight_grads[:, 2 * PAIR:].astype(gvw.dtype)

    @pl.when(pair == 0)
    def _():
        input_grad[...] = grad_inner[...]

    weights = jnp.concatenate([qw[0], kw[0], vw[0]], axis=1)
    input_grad[...] += dot_nt(columns, weights)


def attend_back(bucket, lengths, x_t, q, k, v, grad_context, lse, delta, weights, grad_inner):
    t, d = q.shape
    pairs = d // PAIR
    column = lambda m: pl.BlockSpec((1, d, PAIR), lambda p, *_: (m, 0, p))
    vector = pl.BlockSpec((1, PAIR), lambda p, *_: (0, p))
    tall = pl.BlockSpec((t, PAIR), lambda p, *_: (0, p))
    made = pl.BlockSpec((d, PAIR), lambda p, *_: (0, p))
    return call(
        attend_back_kernel, "attend_back", (pairs,),
        [whole((d, t)), tall, tall, tall, tall, whole((PAIR, t)), whole((PAIR, t)),
         column(0), column(1), column(2), whole((t, d))],
        [made, made, made, vector, vector, whole((t, d))],
        [sds((d, d), bf16)] * 3 + [sds((1, d), f32)] * 2 + [sds((t, d), f32)],
        [pltpu.VMEM((t, PAIR), bf16), pltpu.VMEM((t, PAIR), bf16), pltpu.VMEM((t, 3 * PAIR), bf16)],
        prefetch=2, cost=guess(30e9, 25e6),
    )(bucket, lengths, x_t, q, k, v, grad_context, lse, delta, weights, weights, weights, grad_inner)


def normed(v):
    centred = v - jnp.mean(v, axis=-1, keepdims=True)
    r = lax.rsqrt(jnp.mean(centred * centred, axis=-1, keepdims=True) + epsilon)
    return centred * r, r


def norm_back(dy, n, r, gain):
    dn = dy * gain
    return r * (dn - jnp.mean(dn, axis=-1, keepdims=True) - n * jnp.mean(dn * n, axis=-1, keepdims=True))


def gelu_parts(u):
    phi = 0.5 + 0.5 * lax.erf(u * 0.5 ** 0.5)
    bell = jnp.exp2(u * u * -0.7213475204444817)
    return u * phi, phi + u * (bell * 0.3989422804014327)


VECTORS = ((0, 2), (0, 3), (1, 0), (1, 1), (1, 2), (1, 3))


def attended_kernel(x, context, ow, slabs, n1_out, r1_out, low_out, low_t, ow_out, vectors):
    rows = pl.ds(pl.multiple_of(pl.program_id(0) * ROWS, ROWS), ROWS)
    parts, _, narrow = context.shape

    @pl.when(pl.program_id(0) == 0)
    def _():
        ow_out[...] = jnp.concatenate([ow[j][:, ow.shape[2] - narrow:] for j in range(parts)], axis=1)
        cuts, _, width = slabs.shape
        piece = width // 4
        held_slabs = [slabs[j].astype(f32) for j in range(cuts)]
        for n, (r, m) in enumerate(VECTORS):
            vectors[n:n + 1, :] = jnp.concatenate(
                [v[r:r + 1, m * piece:(m + 1) * piece] for v in held_slabs], axis=1
            )

    joined = jnp.concatenate([context[j] for j in range(parts)], axis=1)
    ob, g1, b1 = (vectors[n:n + 1, :] for n in range(3))
    attended = dot(joined, ow_out[...]) + ob
    n1, r1 = normed(x[...].astype(f32) + attended)
    n1_out[rows, :] = n1
    r1_out[rows, :] = jnp.broadcast_to(r1, (ROWS, r1_out.shape[1]))
    low = (n1 * g1 + b1).astype(bf16)
    low_out[rows, :] = low
    low_t[:, rows] = low.T


def attended(x, context, ow, last, slabs):
    t, d = x.shape
    parts, _, narrow = context.shape
    wide = ow.shape[2] // (last + 1)
    rows = pl.BlockSpec((ROWS, d), lambda r: (r, 0))
    return call(
        attended_kernel, "attended", (t // ROWS,),
        [rows, pl.BlockSpec((parts, ROWS, narrow), lambda r: (0, r, 0)),
         pl.BlockSpec((parts, d, wide), lambda r: (0, 0, last)), whole(slabs.shape)],
        [held()] * 5 + [whole((8, d))],
        [pltpu.VMEM((t, d), f32), pltpu.VMEM((t, 128), f32), pltpu.VMEM((t, d), bf16), pltpu.VMEM((d, t), bf16),
         pltpu.VMEM((d, d), bf16), sds((8, d), f32)],
        cost=guess(3e9, 10e6), limit=SMALL,
    )(x, context, ow, slabs)


def up_tiles(tile, uw, slabs, act_out, slope_out):
    count, depth, _, tall, columns = uw.shape
    for j in range(act_out.shape[0]):
        hidden = dot(tile, uw[j].reshape(2 * depth * tall, columns)) + slabs[j, 2:3, :].astype(f32)
        active, slope = gelu_parts(hidden)
        act_out[j] = active.astype(bf16)
        slope_out[j] = slope.astype(bf16)


def up_kernel(place, low, slabs, u0, u1, u2, u3, act_out, slope_out, uw, sems):
    rows = pl.ds(pl.multiple_of(pl.program_id(0) * ROWS, ROWS), ROWS)
    copies = block_copies(place, (u0, u1, u2, u3), lambda core, j: uw.at[j, :, core], sems)

    @pl.when(pl.program_id(0) == 0)
    def _():
        for copy in copies:
            copy.start()
        for copy in copies:
            copy.wait()

    up_tiles(low[rows, :], uw, slabs, act_out, slope_out)


def up_rest_kernel(place, low, slabs, uw, act_in, slope_in, act_out, slope_out):
    rows = pl.ds(pl.multiple_of(pl.program_id(0) * ROWS, ROWS), ROWS)
    up_tiles(low[rows, :], uw, slabs, act_out, slope_out)


def up(place, low, slabs, blocks):
    t, d = low.shape
    half, depth, tall, wide = blocks[0].shape
    f = 2 * half
    high = pl.BlockSpec((half, ROWS, wide), lambda r, *_: (0, r, 0))
    return call(
        up_kernel, "up", (t // ROWS,),
        [held(), whole((half, 16, wide))] + [pl.BlockSpec(memory_space=pl.ANY)] * 4,
        [high, high, whole((f, depth, 2, tall, wide))],
        [sds((f, t, wide), bf16), sds((f, t, wide), bf16), sds((f, depth, 2, tall, wide), bf16)],
        [pltpu.SemaphoreType.DMA((2 * f,))],
        prefetch=1, cost=guess(6e9, 20e6), limit=SMALL, free=pl.ANY,
    )(place, low, slabs, *blocks)


def up_rest(place, low, slabs, uw, act, slope):
    t, d = low.shape
    f, depth, _, tall, wide = uw.shape
    half = f // 2
    high = pl.BlockSpec((half, ROWS, wide), lambda r, *_: (1, r, 0))
    any_space = pl.BlockSpec(memory_space=pl.ANY)
    return call(
        up_rest_kernel, "up_rest", (t // ROWS,),
        [held(), pl.BlockSpec((half, 16, wide), lambda r, *_: (1, 0, 0)),
         pl.BlockSpec((half, depth, 2, tall, wide), lambda r, *_: (1, 0, 0, 0, 0)),
         any_space, any_space],
        [high, high],
        [sds((f, t, wide), bf16), sds((f, t, wide), bf16)],
        prefetch=1, cost=guess(6e9, 16e6), limit=SMALL, aliases={4: 0, 5: 1},
    )(place, low, slabs, uw, act, slope)


def down_kernel(
    place, bucket, lengths, act_rows, n1, given, cotangent, act_part, d0, d1, d2, d3,
    out, pooled, mixed_out, branch_out, vectors, send, keep, dw,
    branch_t, counts, sums, found, sems,
):
    step = pl.program_id(0)
    tiles = branch_t.shape[1] // ROWS
    f, _, tall, narrow = send.shape
    depth = (place.shape[0] - 1 - 5 * f) // 2
    shared = f == depth

    def target(core, j):
        rows = pl.ds(pl.multiple_of(j * tall, 16), tall)
        if shared:
            return dw.at[:, rows, pl.ds(pl.multiple_of(core * narrow, narrow), narrow)]
        return dw.at[:, core, rows, :]

    copies = block_copies(place, (d0, d1, d2, d3), target, sems)

    @pl.when(step == 0)
    def _():
        for copy in copies:
            copy.start()
        pooled[...] = jnp.zeros_like(pooled)
        counts[...] = jnp.zeros_like(counts)
        sums[...] = jnp.zeros_like(sums)
        for copy in copies:
            copy.wait()

    @pl.when(step < tiles)
    def _():
        rows = pl.ds(pl.multiple_of(step * ROWS, ROWS), ROWS)
        if shared:
            parts = [dot_nt(act_rows[row_of(place, 0, s, depth) // 2], dw[s]) for s in range(f)]
        else:
            parts = [dot_nt(act_rows[i], dw[i // 2, i % 2]) for i in range(f)]
        branch = sum(parts[1:], parts[0])
        g1, b1, db, g2, b2 = (given[n:n + 1, :] for n in range(1, 6))
        residual = n1[rows, :] * g1 + b1 + (branch + db)
        n2, r2 = normed(residual)
        result = n2 * g2 + b2
        out[...] = result.astype(bf16)
        passage = bucket[0] == 1
        for part in range(ROWS // QLEN):
            start = step * ROWS + part * QLEN
            segment = jnp.where(passage, start // PLEN, start // QLEN)
            position = jnp.where(passage, lax.rem(start, PLEN), 0)
            alive = jnp.clip(lengths[segment] - position, 0, QLEN)
            row = lax.broadcasted_iota(jnp.int32, (QLEN, 1), 0)
            picked = jnp.where(row < alive, result[part * QLEN:(part + 1) * QLEN], 0.0)
            pooled[pl.ds(segment, 1), :] += jnp.sum(picked, axis=0, keepdims=True)
            counts[pl.ds(segment, 1), :] += jnp.full((1, 128), 1.0, f32) * alive.astype(f32)
        dy = cotangent[...].astype(f32)
        sums[1:2, :] += jnp.sum(dy * n2, axis=0, keepdims=True)
        sums[2:3, :] += jnp.sum(dy, axis=0, keepdims=True)
        mixed = norm_back(dy, n2, r2, g2)
        mixed_out[rows, :] = mixed
        low = mixed.astype(bf16)
        branch_out[rows, :] = low
        sums[0:1, :] += jnp.sum(low.astype(f32), axis=0, keepdims=True)
        branch_t[:, rows] = low.T

    @pl.when(step == tiles - 1)
    def _():
        pooled[...] = pooled[...] / jnp.maximum(counts[...], 1.0)[:, :1]
        for j in range(vectors.shape[0]):
            vectors[j] = sums[:, j * vectors.shape[2]:(j + 1) * vectors.shape[2]]

    if shared:
        @pl.when(step >= tiles)
        def _():
            core = core_of(place, depth, f)
            found[...] = dot(branch_t[...], act_part[0]).astype(bf16)
            for n, made in ((1, send), (0, keep)):
                lanes = pl.ds(pl.multiple_of(lax.rem(core + n, 2) * narrow, narrow), narrow)
                for j in range(f):
                    made[slot_of(place, n, j, depth, f), 0] = found[j * tall:(j + 1) * tall, lanes]
    else:
        def part(n, made):
            part_found = dot(branch_t[...], act_part[0]).astype(bf16)
            for j in range(f):
                made[slot_of(place, n, j, depth, f), 0] = part_found[j * tall:(j + 1) * tall]

        @pl.when((step >= tiles) & (step < tiles + depth))
        def _():
            part(1, send)

        @pl.when(step >= tiles + depth)
        def _():
            part(0, keep)


def down(cuts, place, bucket, lengths, active, n1, given, cotangent, blocks):
    f, t, wide = active.shape
    d = n1.shape[1]
    tiles = t // ROWS
    slots = lengths.shape[0]
    _, depth, tall, narrow = blocks[0].shape
    shared = f == depth
    parts = f
    weights = (f, d, wide) if shared else (depth, 2, d, narrow)
    early = lambda s: jnp.minimum(s, tiles - 1)
    if shared:
        late = lambda s, place: place[jnp.maximum(s - tiles, 0)] // 2
    else:
        late = lambda s, place: place[(jnp.maximum(s - tiles, 0) + depth) % parts]
    made = lambda first: pl.BlockSpec(
        (f, 1, tall, narrow), lambda s, *_: (0, jnp.clip(s - tiles - first, 0, depth - 1), 0, 0)
    )
    rows = pl.BlockSpec((ROWS, d), lambda s, *_: (early(s), 0))
    return call(
        down_kernel, "down", (tiles + parts,),
        [pl.BlockSpec((f, ROWS, wide), lambda s, *_: (0, early(s), 0)), held(), whole((8, d)), rows, pl.BlockSpec((1, t, wide), lambda s, place, *_: (late(s, place), 0, 0))]
        + [pl.BlockSpec(memory_space=pl.ANY)] * 4,
        [rows, whole((slots, d)), held(), held(), whole((cuts, 8, d // cuts)), made(0), made(0 if shared else depth),
         whole(weights)],
        [sds((t, d), bf16), sds((slots, d), f32), pltpu.VMEM((t, d), f32), pltpu.VMEM((t, d), bf16)]
        + [sds((cuts, 8, d // cuts), f32)] + [sds((f, depth, tall, narrow), bf16)] * 2
        + [sds(weights, bf16)],
        [pltpu.VMEM((d, t), bf16), pltpu.VMEM((slots, 128), f32), pltpu.VMEM((8, d), f32),
         pltpu.VMEM((d, wide), bf16), pltpu.SemaphoreType.DMA((2 * f,))],
        prefetch=3, cost=guess(12e9, 35e6), limit=SMALL, free=pl.ANY,
    )(place, bucket, lengths, active, n1, given, cotangent, active, *blocks)


def feed_back_kernel(
    place, branch, slope, dw, uw, low_t, mixed, *refs,
):
    send, keep, gub, grad_normed, hidden, found = refs[-6:]
    j = pl.program_id(0)
    _, depth, tall, _ = send.shape
    _, t, wide = slope.shape
    tiles = t // FEED_ROWS

    def gelu_rows(r, sums):
        rows = pl.ds(pl.multiple_of(r * FEED_ROWS, FEED_ROWS), FEED_ROWS)
        grad = (slope[0, rows, :].astype(f32) * dot(branch[rows, :], dw[0])).astype(bf16)
        hidden[rows, :] = grad
        return sums + jnp.sum(grad.astype(f32), axis=0, keepdims=True)

    gub[0] = lax.fori_loop(0, tiles, gelu_rows, jnp.zeros((1, wide), f32))
    found[...] = dot(low_t[...], hidden[...]).astype(bf16)
    for n, target in ((1, send), (0, keep)):
        for slot in range(depth):
            i = row_of(place, n, slot, depth)
            target[0, slot] = found[pl.ds(pl.multiple_of(i * tall, 16), tall), :]

    @pl.when(j == 0)
    def _():
        grad_normed[...] = mixed[...]

    def normed_rows(r, carry):
        rows = pl.ds(pl.multiple_of(r * FEED_ROWS, FEED_ROWS), FEED_ROWS)
        grad_normed[rows, :] += dot_nt(hidden[rows, :], uw[0])
        return carry

    lax.fori_loop(0, tiles, normed_rows, 0)


def feed_back(first, count, place, branch, slope, dw, uw, low_t, mixed, shared):
    t = slope.shape[1]
    f, d, wide = uw.shape
    dp, _, depth, _ = axis_facts()
    tall = d // dp
    made = lambda n: pl.BlockSpec(
        (1, depth, tall, wide), lambda j, place: (slot_of(place, n, first + j, depth, f), 0, 0, 0)
    )
    part = lambda *shape: pl.BlockSpec((1, *shape), lambda j, *_: (first + j, 0, 0))
    slot = lambda j, place: row_of(place, 0, first + j, depth) // 2 if f == depth else first + j
    any_space = pl.BlockSpec(memory_space=pl.ANY)
    return call(
        feed_back_kernel, "feed_back", (count,),
        [held(), part(t, wide), pl.BlockSpec((1, d, wide), lambda j, place: (slot(j, place), 0, 0)), part(d, wide),
         held(), held()] + [any_space] * len(shared),
        [made(1), made(0), part(1, wide), held()],
        [sds((f, depth, tall, wide), bf16)] * 2 + [pltpu.HBM((f, 1, wide), f32), pltpu.VMEM((t, d), f32)],
        [pltpu.VMEM((t, wide), bf16), pltpu.VMEM((d, wide), bf16)],
        prefetch=1, cost=guess(15e9, 35e6), limit=SMALL, least=0, aliases={7 + n: n for n in range(len(shared))},
    )(place, branch, slope, dw, uw, low_t, mixed, *shared)


def inner_kernel(
    head_of, grad_normed, n1, r1, given, context, ow,
    inner_out, vectors, gow, grad_context, delta_out,
    weight_grad, sums,
):
    step = pl.program_id(0)
    d = n1.shape[1]
    parts, _, narrow = context.shape

    @pl.when(step == 0)
    def _():
        weight_grad[...] = jnp.zeros_like(weight_grad)
        sums[...] = jnp.zeros_like(sums)

    shape = (delta_out.shape[0], d)
    head = head_of(lax.broadcasted_iota(jnp.int32, shape, 0))
    pick = jnp.where(lax.broadcasted_iota(jnp.int32, shape, 1) // HD == head, 1.0, 0.0).astype(bf16)
    rows = pl.ds(pl.multiple_of(step * ROWS, ROWS), ROWS)
    dy, n = grad_normed[rows, :], n1[rows, :]
    inner = norm_back(dy, n, r1[rows, :1], given[1:2, :])
    inner_out[...] = inner
    low = inner.astype(bf16)
    grad_ctx = dot_nt(low, ow[...]).astype(bf16)
    for j in range(parts):
        grad_context[j] = grad_ctx[:, j * narrow:(j + 1) * narrow]
    joined = jnp.concatenate([context[j] for j in range(parts)], axis=1)
    both = grad_ctx.astype(f32) * joined.astype(f32)
    high = both.astype(bf16)
    rest = (both - high.astype(f32)).astype(bf16)
    delta_out[...] = dot_nt(pick, high) + dot_nt(pick, rest)
    sums[0:1, :] += jnp.sum(dy * n, axis=0, keepdims=True)
    sums[1:2, :] += jnp.sum(dy, axis=0, keepdims=True)
    sums[2:3, :] += jnp.sum(low.astype(f32), axis=0, keepdims=True)
    weight_grad[...] += dot_tn(joined, low)

    @pl.when(step == pl.num_programs(0) - 1)
    def _():
        for j in range(parts):
            columns = slice(j * narrow, (j + 1) * narrow)
            gow[j] = weight_grad[:, columns].astype(bf16)
            vectors[j] = sums[:, columns]


def inner_back(count, head_of, grad_normed, n1, r1, given, context, ow):
    t, d = n1.shape
    parts, _, narrow = context.shape
    tile = pl.BlockSpec((parts, ROWS, narrow), lambda r: (0, r, 0))
    return call(
        functools.partial(inner_kernel, head_of), "inner_back", (t // ROWS,),
        [held(), held(), held(), whole((8, d)), tile, held()],
        [pl.BlockSpec((ROWS, d), lambda r: (r, 0)), whole((parts, 8, narrow)), whole((parts, d, narrow)), tile,
         pl.BlockSpec((count, ROWS), lambda r: (0, r))],
        [sds((t, d), f32), sds((parts, 8, narrow), f32), sds((parts, d, narrow), bf16), sds((parts, t, narrow), bf16),
         sds((count, t), f32)],
        [pltpu.VMEM((d, d), f32), pltpu.VMEM((8, d), f32)],
        cost=guess(4e9, 10e6), limit=SMALL,
    )(grad_normed, n1, r1, given, context, ow)


def shards(
    tokens, bucket, lengths, cotangent,
    query_weight, query_bias, key_weight, value_weight, value_bias, out_weight, out_bias,
    norm1_gain, norm1_bias, up_weight, up_bias, down_weight, down_bias, norm2_gain, norm2_bias,
):
    t, d = tokens.shape
    dp, fsdp = lax.axis_size("dp"), lax.axis_size("fsdp")
    lengths = lengths[0]

    place = places()
    depth = dp // 2
    tall, narrow = d // dp, d // fsdp
    width = 4 * narrow
    by_head = narrow == HEADS * HD and fsdp == 4
    down_t = down_weight.T

    if by_head:
        block = make_block(
            query_weight, key_weight, value_weight, out_weight, query_bias, value_bias, out_bias, norm1_gain,
            norm1_bias, down_bias, norm2_gain, norm2_bias, up_bias,
        )
        along = Once([(block, "dp", along_z(s)) for s in range(1, depth)])
        x_t, = beside([along], lambda x: (x.T,), (tokens,))
        own = [block] + along.got
        own = line_up(place, own)
        swap = lambda v: (v, "dp", across_cores())
        in_plane = lambda v, s: (v, "fsdp", [(f, f ^ s) for f in range(fsdp)])
        paired = Once([swap(own)])
        beside([paired])
        pair_0 = paired.got[0]
        ups = Once([(up_weight, "dp", along_z(s)) for s in range(1, depth)])
        sides = Once([in_plane(own, 1), in_plane(own, 2)])
        one = lambda away: functools.partial(attend_one, away, fsdp)
        run = (bucket, lengths, tokens)
        *shared, kept_0, lse_0 = beside([sides, ups], one(0), (place, *run, own, pair_0, []), out=3)
        own_x, own_y = sides.got
        to_u = Gather(line_up(place, [up_weight] + ups.got))
        paired = Once([swap(own_x), swap(own_y)])
        corner = Once([(select_core(own_y, own_x), ("dp", "fsdp"), along_bit(0))])
        beside([paired])
        pair_x, pair_y = paired.got
        downs = Once([(down_t, "dp", along_z(s)) for s in range(1, depth)])
        *shared, kept_1, lse_1 = beside([corner, to_u, downs], one(1), (place, *run, own_x, pair_x, shared), out=3)
        own_c = corner.got[0]
        to_d = Gather(jnp.stack([down_t] + downs.got))
        paired = Once([swap(own_c)])
        *shared, kept_2, lse_2 = beside([paired, to_u], one(2), (place, *run, own_y, pair_y, shared), out=3)
        *shared, kept_3, lse_3 = beside([to_u, to_d], one(3), (place, *run, own_c, paired.got[0], shared), out=3)
        context, weights, slabs = shared
        ow, last = weights.reshape(fsdp, d, width), 2
        count, head_of = 8 * fsdp, lambda r: jnp.where(r % 8 < HEADS, r // 8 * HEADS + r % 8, -1)
    else:
        block = jnp.concatenate([
            jnp.concatenate([query_weight, key_weight, value_weight, out_weight], axis=1),
            jnp.concatenate([query_bias, value_bias, out_bias, norm1_gain])[None],
            jnp.concatenate([norm1_bias, down_bias, norm2_gain, norm2_bias])[None],
            up_bias[None],
            jnp.zeros((13, width), bf16),
        ])
        to_a, to_u, to_d = Gather(gather_z(block)), Gather(gather_z(up_weight)), Gather(gather_z(down_t))
        finish(to_a)
        weights, vectors, slabs = assemble(place, to_a.blocks)
        qb, vb = (vectors[m, 0:1] for m in range(2))
        q, k, v, context, lse = attend(bucket, lengths, tokens, weights, qb, vb)
        context, ow, last = context[None], weights[3:], 0
        count, head_of = PAIR, lambda r: 2 * (r % HD) + r // HD

    finish(to_u)

    def attended_up(place, *args):
        normal = attended(*args)
        return [*normal, *up(place, normal[2], slabs, to_u.blocks)]

    n1, r1, low, low_t, ow, given, active, slope, uw = beside(
        [to_d], attended_up, (place, tokens, context, ow, last, slabs), key=5, out=6
    )
    active, slope = beside([to_d], up_rest, (place, low, slabs, uw, active, slope))
    finish(to_d)
    cuts = context.shape[0]
    out, pooled, mixed, branch, down_vectors, send_d, keep_d, dw = down(
        cuts, place, bucket, lengths, active, n1, given, cotangent, to_d.blocks
    )
    of_d = Scatter(keep_d, send_d)
    dw, uw = dw.reshape(fsdp, d, -1), uw.reshape(fsdp, d, -1)
    part = fsdp // 2
    *shared, so_far = beside(
        [of_d], functools.partial(feed_back, 0, part), (place, branch, slope, dw, uw, low_t, mixed, [])
    )
    send_u, keep_u, gub, grad_normed = beside(
        [of_d], functools.partial(feed_back, part, fsdp - part),
        (place, branch, slope, dw, uw, low_t, so_far, shared),
    )
    of_u = Scatter(keep_u, send_u)
    inner, inner_vectors, gow, grad_context, delta = beside(
        [of_d, of_u], functools.partial(inner_back, count, head_of), (grad_normed, n1, r1, given, context, ow),
        key=3, out=2
    )

    if by_head:
        delta = delta.reshape(fsdp, 8, t)

        def back(away, moves, kept, lse):
            args = (place, bucket, lengths, x_t, kept, grad_context, lse, delta, gow, inner_vectors, down_vectors, gub)
            return beside(moves, functools.partial(attend_back_one, away, fsdp, depth), args)

        send_3, keep_3, grads_3 = back(3, [of_d, of_u], kept_3, lse_3)
        swap_3 = Once([swap(send_3)])
        send_1, keep_1, grads_1 = back(1, [swap_3, of_u], kept_1, lse_1)
        corner = Once([(add(keep_3, swap_3.got[0]), ("dp", "fsdp"), along_bit(0))])
        send_2, keep_2, grads_2 = back(2, [corner, of_u], kept_2, lse_2)
        sums = Once([swap(send_1), swap(send_2)])
        beside([sums])
        add_both = lambda *v: sum(u.astype(f32) for u in v)
        through = corner.got[0]
        sum_1 = add_both(keep_1, sums.got[0]) + select_core(jnp.zeros_like(through), through).astype(f32)
        sum_2 = add_both(keep_2, sums.got[1]) + select_core(through, jnp.zeros_like(through)).astype(f32)
        sides = Once([in_plane(sum_1.astype(bf16), 1), in_plane(sum_2.astype(bf16), 2)])
        send_0, keep_0, grads_0 = back(0, [sides, of_u], kept_0, lse_0)
        sums = Once([swap(send_0)])
        beside([sums, of_u])
        total = add_both(keep_0, sums.got[0], *sides.got)
        z = lax.axis_index("dp") // 2
        at = lambda s: lax.dynamic_index_in_dim(total, (z - s) % depth, 0, keepdims=False)
        along = Once([(at(s).astype(bf16), "dp", along_z(-s)) for s in range(1, depth)])
        input_grad, = beside(
            [along, of_u], make_input_grad, (place, inner, (grads_0, grads_1, grads_2, grads_3), weights)
        )
        *made, gqb, gvb, gob, gg1, gb1, gdb, gg2, gb2, gub = unblock(at(0), along.got)
        vectors = (gqb, gvb, gob, gg1, gb1, gdb, gg2, gb2)
        finish(of_d)
        finish(of_u)
    else:
        gg1, gb1, gob = (inner_vectors[0, n:n + 1] for n in range(3))
        gdb, gg2, gb2 = (down_vectors[0, n:n + 1] for n in range(3))
        gqw, gkw, gvw, gqb, gvb, input_grad = attend_back(
            bucket, lengths, tokens.T, q, k, v, grad_context[0], lse, delta, weights, inner
        )
        firsts = jnp.stack([gqb, gvb, gob, gg1])
        seconds = jnp.stack([gb1, gdb, gg2, gb2])
        vectors = jnp.concatenate([firsts, seconds, jnp.zeros((4, 14, d), f32)], axis=1)
        of_a = Scatter(*reversed(pack(place, (gqw, gkw, gvw, gow[0]), vectors, gub)))
        while not (of_a.done() and of_u.done() and of_d.done()):
            beside([of_a, of_u, of_d])
        made_a = of_a.total
        made = [made_a[:tall, m * narrow:(m + 1) * narrow] for m in range(4)]
        vectors = [made_a[tall + n, m * narrow:(m + 1) * narrow] for n in range(2) for m in range(4)]
        gub = made_a[tall + 2]
    return (
        out, pooled, input_grad, made[0], vectors[0], made[1], made[2], vectors[1], made[3], vectors[2], vectors[3],
        vectors[4], of_u.total, gub, of_d.total.T, vectors[5], vectors[6], vectors[7],
    )


def solution(mesh):
    tall, square, vector = P(("dp", "fsdp"), None), P("dp", "fsdp"), P("fsdp")
    in_specs = (
        tall, P(("dp", "fsdp")), tall, tall, square, vector, square, square, vector, square, vector,
        vector, vector, square, vector, square, vector, vector, vector,
    )
    out_specs = (
        tall, tall, tall, square, vector, square, square, vector, square, vector, vector, vector,
        square, vector, square, vector, vector, vector,
    )
    return jax.shard_map(shards, mesh=mesh, in_specs=in_specs, out_specs=out_specs, check_vma=False)
```

profile of v0, /device:TPU:0, one launch (start us, length us, event | category | flops | bytes accessed | tf_op | source)
XLA Modules:
  0.0 282.1 jit_solution(972554912270101568)
XLA Ops:
  0.7 1.7 block.1.refs_0_
  2.4 3.0 %collective-permute-start = (bf16[112,768]{1,0:T(8,128)(2,1)}, bf16[112,768]{1,0:T(8,128)(2,1)S(1)}, u32[]{:S(2)}, u32[]{:S(2)}) collective-permute-start(bf16[112,768]{1,0:T(8,128)(2,1)} %block.1.refs_0_), channel_id=1, source_target_pairs={{0,8},{4,12},{8,16},{12,20},{16,24},{20,28},{24,0},{28,4},{1,9},{5... | collective-permute-start | bytes 516104 | tf_op jit(solution)/shard_map/ppermute | solution.py:223
  5.4 2.6 collective-permute-start.1
  9.3 2.6 copy.51
  12.9 6.5 %collective-permute-done.1.refs_2_ = bf16[112,768]{1,0:T(8,128)(2,1)S(1)} collective-permute-done((bf16[112,768]{1,0:T(8,128)(2,1)}, bf16[112,768]{1,0:T(8,128)(2,1)S(1)}, u32[]{:S(2)}, u32[]{:S(2)}) %collective-permute-start.1) | collective-permute-done | bytes 172064 | tf_op jit(solution)/shard_map/ppermute | solution.py:223
  20.2 2.6 line_up.2.own
  22.8 1.5 collective-permute-start.4
  24.3 1.5 collective-permute-start.5
  26.5 4.2 %collective-permute-start.6 = (bf16[96,768]{1,0:T(8,128)(2,1)S(1)}, bf16[96,768]{1,0:T(8,128)(2,1)S(1)}, u32[]{:S(2)}, u32[]{:S(2)}) collective-permute-start(bf16[96,768]{1,0:T(8,128)(2,1)S(1)} %copy-done.18), channel_id=1, source_target_pairs={{0,8},{4,12},{8,16},{12,20},{16,24},{20,28},{24,0},{28,4},{1,9},{5... | collective-permute-start | bytes 442376 | tf_op jit(solution)/shard_map/ppermute | solution.py:223
  30.7 1.7 collective-permute-start.7
  34.2 8.1 %attend.4 = (bf16[4,1024,192]{2,1,0:T(8,128)(2,1)}, bf16[4,4,2,96,768]{4,3,2,1,0:T(8,128)(2,1)}, bf16[4,16,768]{2,1,0:T(8,128)(2,1)}, bf16[1024,640]{1,0:T(8,128)(2,1)}, f32[8,1024]{1,0:T(8,128)}) custom-call(s32[29]{0:T(128)S(1)} %concatenate.9.place, s32[1]{0:T(128)S(6)} %copy.66.bucket, s32[8]{0:T(128)S(1)} %bitcast.55, bf16[1024,768]{1,0:T(8,128)(2,1)} %x.9, ...), custom_call_target="tpu_custom_call" | custom-call | flops 5000000000 | bytes 8000000 | tf_op jit(solution)/shard_map/attend/pallas_call | solution.py:79
  43.1 2.5 line_up.3
  47.8 3.6 %collective-permute-start.13 = (bf16[192,384]{1,0:T(8,128)(2,1)S(1)}, bf16[192,384]{1,0:T(8,128)(2,1)S(1)}, u32[]{:S(2)}, u32[]{:S(2)}) collective-permute-start(bf16[192,384]{1,0:T(8,128)(2,1)S(1)} %bitcast.70), channel_id=1, source_target_pairs={{0,8},{4,12},{8,16},{12,20},{16,24},{20,28},{24,0},{28,4},{1,9},{5... | collective-permute-start | bytes 442376 | tf_op jit(solution)/shard_map/ppermute | solution.py:223
  51.4 1.7 collective-permute-start.14
  54.3 8.1 %attend.5 = (bf16[4,1024,192]{2,1,0:T(8,128)(2,1)}, bf16[4,4,2,96,768]{4,3,2,1,0:T(8,128)(2,1)}, bf16[4,16,768]{2,1,0:T(8,128)(2,1)}, bf16[1024,640]{1,0:T(8,128)(2,1)}, f32[8,1024]{1,0:T(8,128)}) custom-call(s32[29]{0:T(128)S(1)} %concatenate.9.place, s32[1]{0:T(128)S(6)} %copy.66.bucket, ...), custom_call_target="tpu_custom_call", output_to_operand_aliasing={{0}: (6, {}), {1}: (7, {}), {2}: (8, {})} | custom-call | flops 5000000000 | bytes 8000000 | tf_op jit(solution)/shard_map/attend/pallas_call | solution.py:79
  64.3 8.1 %attend.6 = (bf16[4,1024,192]{2,1,0:T(8,128)(2,1)}, bf16[4,4,2,96,768]{4,3,2,1,0:T(8,128)(2,1)}, bf16[4,16,768]{2,1,0:T(8,128)(2,1)}, bf16[1024,640]{1,0:T(8,128)(2,1)}, f32[8,1024]{1,0:T(8,128)}) custom-call(s32[29]{0:T(128)S(1)} %concatenate.9.place, s32[1]{0:T(128)S(6)} %copy.66.bucket, ...), custom_call_target="tpu_custom_call", output_to_operand_aliasing={{0}: (6, {}), {1}: (7, {}), {2}: (8, {})} | custom-call | flops 5000000000 | bytes 8000000 | tf_op jit(solution)/shard_map/attend/pallas_call | solution.py:79
  72.5 7.0 %collective-permute-done.17.u1 = bf16[2,4,96,768]{3,2,1,0:T(8,128)(2,1)S(1)} collective-permute-done((bf16[2,4,96,768]{3,2,1,0:T(8,128)(2,1)S(1)}, bf16[2,4,96,768]{3,2,1,0:T(8,128)(2,1)S(1)}, u32[]{:S(2)}, u32[]{:S(2)}) %collective-permute-start.17) | collective-permute-done | bytes 1179680 | tf_op jit(solution)/shard_map/ppermute | solution.py:223
  80.6 8.1 %attend.7 = (bf16[4,1024,192]{2,1,0:T(8,128)(2,1)}, bf16[4,4,2,96,768]{4,3,2,1,0:T(8,128)(2,1)}, bf16[4,16,768]{2,1,0:T(8,128)(2,1)}, bf16[1024,640]{1,0:T(8,128)(2,1)}, f32[8,1024]{1,0:T(8,128)}) custom-call(s32[29]{0:T(128)S(1)} %concatenate.9.place, s32[1]{0:T(128)S(6)} %copy.66.bucket, ...), custom_call_target="tpu_custom_call", output_to_operand_aliasing={{0}: (6, {}), {1}: (7, {}), {2}: (8, {})} | custom-call | flops 5000000000 | bytes 8000000 | tf_op jit(solution)/shard_map/attend/pallas_call | solution.py:79
  91.0 5.7 %attended.1 = (f32[1024,768]{1,0:T(8,128)S(1)}, f32[1024,128]{1,0:T(8,128)S(1)}, bf16[1024,768]{1,0:T(8,128)(2,1)S(1)}, bf16[768,1024]{1,0:T(8,128)(2,1)S(1)}, b...) custom-call(bf16[1024,768]{1,0:T(8,128)(2,1)} %x.9, bf16[4,1024,192]{2,1,0:T(8,128)(2,1)} %get-tuple-element.269.context, ...), custom_call_target="tpu_custom_call" | custom-call | flops 3000000000 | bytes 10000000 | tf_op jit(solution)/shard_map/attended/pallas_call | solution.py:79
  96.8 9.3 %up.1 = (bf16[4,1024,768]{2,1,0:T(8,128)(2,1)}, bf16[4,1024,768]{2,1,0:T(8,128)(2,1)}, bf16[4,4,2,96,768]{4,3,2,1,0:T(8,128)(2,1)}) custom-call(s32[29]{0:T(128)S(1)} %concatenate.9.place, bf16[1024,768]{1,0:T(8,128)(2,1)S(1)} %get-tuple-element.273.low, bf16[4,16,768]{2,1,0:T(8,128)(2,1)} %get-tuple-element.272.slabs, ...), custom_call_target="tpu_custom_call" | custom-call | flops 6000000000 | bytes 20000000 | tf_op jit(solution)/shard_map/up/pallas_call | solution.py:79
  106.8 8.3 %up_rest.1 = (bf16[4,1024,768]{2,1,0:T(8,128)(2,1)}, bf16[4,1024,768]{2,1,0:T(8,128)(2,1)}) custom-call(s32[29]{0:T(128)S(1)} %concatenate.9.place, bf16[1024,768]{1,0:T(8,128)(2,1)S(1)} %get-tuple-element.273.low, bf16[4,16,768]{2,1,0:T(8,128)(2,1)} %get-tuple-element.272.slabs, ...), custom_call_target="tpu_custom_call", output_to_operand_aliasing={{0}: (4, {}), {1}: (5, {})} | custom-call | flops 6000000000 | bytes 16000000 | tf_op jit(solution)/shard_map/up_rest/pallas_call | solution.py:79
  115.1 21.8 %down.1 = (bf16[1024,768]{1,0:T(8,128)(2,1)}, f32[8,768]{1,0:T(8,128)}, f32[1024,768]{1,0:T(8,128)S(1)}, bf16[1024,768]{1,0:T(8,128)(2,1)S(1)}, f32[4,8,192]{2,1...) custom-call(s32[29]{0:T(128)S(1)} %concatenate.9.place, ...), custom_call_target="tpu_custom_call" | custom-call | flops 12000000000 | bytes 35000000 | tf_op jit(solution)/shard_map/down/pallas_call | solution.py:79
  137.0 13.7 %feed_back.2 = (bf16[4,4,96,768]{3,2,1,0:T(8,128)(2,1)}, bf16[4,4,96,768]{3,2,1,0:T(8,128)(2,1)}, f32[4,1,768]{2,1,0:T(1,128)}, f32[1024,768]{1,0:T(8,128)S(1)}) custom-call(s32[29]{0:T(128)S(1)} %concatenate.9.place, bf16[1024,768]{1,0:T(8,128)(2,1)S(1)} %get-tuple-element.296.branch, bf16[4,1024,768]{2,1,0:T(8,128)(2,1)} %get-tuple-element.297.slope, ...), custom_call_target="tpu_custom_call" | custom-call | flops 15000000512 | bytes 35000000 | tf_op jit(solution)/shard_map/feed_back/pallas_call | solution.py:79
  152.4 13.6 %feed_back.3 = (bf16[4,4,96,768]{3,2,1,0:T(8,128)(2,1)}, bf16[4,4,96,768]{3,2,1,0:T(8,128)(2,1)}, f32[4,1,768]{2,1,0:T(1,128)}, f32[1024,768]{1,0:T(8,128)S(1)}) custom-call(s32[29]{0:T(128)S(1)} %concatenate.9.place, bf16[1024,768]{1,0:T(8,128)(2,1)S(1)} %get-tuple-element.296.branch, ...), custom_call_target="tpu_custom_call", output_to_operand_aliasing={{0}: (7, {}), {1}: (8, {}), {2}: (9, {})} | custom-call | flops 15000000512 | bytes 35000000 | tf_op jit(solution)/shard_map/feed_back/pallas_call | solution.py:79
  165.9 1.7 collective-permute-done.25
  167.9 1.4 copy-done.26
  169.9 9.8 %inner_back.1 = (f32[1024,768]{1,0:T(8,128)}, f32[4,8,192]{2,1,0:T(8,128)}, bf16[4,768,192]{2,1,0:T(8,128)(2,1)}, bf16[4,1024,192]{2,1,0:T(8,128)(2,1)}, f32[32,1024]{1,0:T(8,128)}) custom-call(f32[1024,768]{1,0:T(8,128)S(1)} %get-tuple-element.312.grad_normed, f32[1024,768]{1,0:T(8,128)S(1)} %get-tuple-element.287.n1, ...), custom_call_target="tpu_custom_call" | custom-call | flops 4000000000 | bytes 10000000 | tf_op jit(solution)/shard_map/inner_back/pallas_call | solution.py:79
  181.9 4.9 %collective-permute-start.28 = (bf16[192,384]{1,0:T(8,128)(2,1)S(1)}, bf16[192,384]{1,0:T(8,128)(2,1)S(1)}, u32[]{:S(2)}, u32[]{:S(2)}) collective-permute-start(bf16[192,384]{1,0:T(8,128)(2,1)S(1)} %get-tuple-element.334), channel_id=1, source_target_pairs={{0,24},{4,28},{8,0},{12,4},{16,8},{20,12},{24,16},{28,20},{1,25},{... | collective-permute-start | bytes 442376 | tf_op jit(solution)/shard_map/ppermute | solution.py:223
  187.4 9.9 %attend_back.4 = (bf16[4,112,768]{2,1,0:T(8,128)(2,1)}, bf16[4,112,768]{2,1,0:T(8,128)(2,1)}, bf16[1024,640]{1,0:T(8,128)(2,1)}) custom-call(s32[29]{0:T(128)S(1)} %concatenate.9.place, s32[1]{0:T(128)S(6)} %copy.66.bucket, s32[8]{0:T(128)S(1)} %bitcast.60, bf16[768,1024]{1,0:T(8,128)(2,1)} %bitcast.66, bf16[1024,640]{1,0:T(8,128)(2,1)} %get-tuple-element.325.kept, ...), custom_call_target="tpu_custom_call" | custom-call | flops 10000000000 | bytes 12000000 | tf_op jit(solution)/shard_map/attend_back/pallas_call | solution.py:79
  197.3 3.0 %collective-permute-done.29 = bf16[192,384]{1,0:T(8,128)(2,1)S(1)} collective-permute-done((bf16[192,384]{1,0:T(8,128)(2,1)S(1)}, bf16[192,384]{1,0:T(8,128)(2,1)S(1)}, u32[]{:S(2)}, u32[]{:S(2)}) %collective-permute-start.29) | collective-permute-done | bytes 147488 | tf_op jit(solution)/shard_map/ppermute | solution.py:223
  202.1 1.5 collective-permute-start.33
  203.6 9.9 %attend_back.5 = (bf16[4,112,768]{2,1,0:T(8,128)(2,1)}, bf16[4,112,768]{2,1,0:T(8,128)(2,1)}, bf16[1024,640]{1,0:T(8,128)(2,1)}) custom-call(s32[29]{0:T(128)S(1)} %concatenate.9.place, s32[1]{0:T(128)S(6)} %copy.66.bucket, s32[8]{0:T(128)S(1)} %bitcast.61, bf16[768,1024]{1,0:T(8,128)(2,1)} %bitcast.67, bf16[1024,640]{1,0:T(8,128)(2,1)} %get-tuple-element.341.kept, ...), custom_call_target="tpu_custom_call" | custom-call | flops 10000000000 | bytes 12000000 | tf_op jit(solution)/shard_map/attend_back/pallas_call | solution.py:79
  217.7 1.9 collective-permute-start.37
  219.6 10.0 %attend_back.6 = (bf16[4,112,768]{2,1,0:T(8,128)(2,1)}, bf16[4,112,768]{2,1,0:T(8,128)(2,1)}, bf16[1024,640]{1,0:T(8,128)(2,1)}) custom-call(s32[29]{0:T(128)S(1)} %concatenate.9.place, s32[1]{0:T(128)S(6)} %copy.66.bucket, s32[8]{0:T(128)S(1)} %bitcast.62, bf16[768,1024]{1,0:T(8,128)(2,1)} %bitcast.68, bf16[1024,640]{1,0:T(8,128)(2,1)} %get-tuple-element.352.kept, ...), custom_call_target="tpu_custom_call" | custom-call | flops 10000000000 | bytes 12000000 | tf_op jit(solution)/shard_map/attend_back/pallas_call | solution.py:79
  229.6 1.4 collective-permute-done.36
  231.6 1.8 collective-permute-done.38
  234.5 1.7 add_convert_fusion.4
  236.2 1.6 collective-permute-start.40
  238.7 9.9 %attend_back.7 = (bf16[4,112,768]{2,1,0:T(8,128)(2,1)}, bf16[4,112,768]{2,1,0:T(8,128)(2,1)}, bf16[1024,640]{1,0:T(8,128)(2,1)}) custom-call(s32[29]{0:T(128)S(1)} %concatenate.9.place, s32[1]{0:T(128)S(6)} %copy.66.bucket, s32[8]{0:T(128)S(1)} %bitcast.63, bf16[768,1024]{1,0:T(8,128)(2,1)} %bitcast.69, bf16[1024,640]{1,0:T(8,128)(2,1)} %get-tuple-element.367.kept, ...), custom_call_target="tpu_custom_call" | custom-call | flops 10000000000 | bytes 12000000 | tf_op jit(solution)/shard_map/attend_back/pallas_call | solution.py:79
  248.6 5.1 %collective-permute-done.40 = bf16[4,112,768]{2,1,0:T(8,128)(2,1)S(1)} collective-permute-done((bf16[4,112,768]{2,1,0:T(8,128)(2,1)S(1)}, bf16[4,112,768]{2,1,0:T(8,128)(2,1)S(1)}, u32[]{:S(2)}, u32[]{:S(2)}) %collective-permute-start.40) | collective-permute-done | bytes 688160 | tf_op jit(solution)/shard_map/ppermute | solution.py:223
  254.9 1.8 fusion.2
  256.7 1.9 fusion.4
  258.7 1.4 convert_add_fusion
  260.7 1.4 collective-permute-start.44
  262.2 1.9 collective-permute-start.45
  264.1 10.8 %input_grad.1 = f32[1024,768]{1,0:T(8,128)} custom-call(s32[29]{0:T(128)S(1)} %concatenate.9.place, f32[1024,768]{1,0:T(8,128)} %get-tuple-element.377.inner, bf16[1024,640]{1,0:T(8,128)(2,1)} %get-tuple-element.378.refs_0_, bf16[1024,640]{1,0:T(8,128)(2,1)} %get-tuple-element.379.refs_1_, bf16[1024,640]{1,0:T(8,128)(2,1)} %get-tuple-element.380.refs_2_, ...), custom_call_target="tpu_custom_call" | custom-call | flops 5000000000 | bytes 15000000 | tf_op jit(solution)/shard_map/input_grad/pallas_call | solution.py:79
  275.7 2.5 collective-permute-done.44.refs_1_
  279.5 2.1 unblock.1
  (144 shorter events, 32.9 us)
Async XLA Ops:
  2.4 10.6 %collective-permute-start = (bf16[112,768]{1,0:T(8,128)(2,1)}, bf16[112,768]{1,0:T(8,128)(2,1)S(1)}, u32[]{:S(2)}, u32[]{:S(2)}) collective-permute-start(bf16[112,768]{1,0:T(8,128)(2,1)} %block.1.refs_0_), channel_id=1, source_target_pairs={{0,8},{4,12},{8,16},{12,20},{16,24},{20,28},{24,0},{28,4},{1,9},{5... | collective-permute-start | bytes 516104 | tf_op jit(solution)/shard_map/ppermute | solution.py:223
  5.4 14.1 %collective-permute-start.1 = (bf16[112,768]{1,0:T(8,128)(2,1)}, bf16[112,768]{1,0:T(8,128)(2,1)S(1)}, u32[]{:S(2)}, u32[]{:S(2)}) collective-permute-start(bf16[112,768]{1,0:T(8,128)(2,1)} %block.1.refs_0_), channel_id=1, source_target_pairs={{0,16},{4,20},{8,24},{12,28},{16,0},{20,4},{24,8},{28,12},{1,17},{... | collective-permute-start | bytes 516104 | tf_op jit(solution)/shard_map/ppermute | solution.py:223
  8.0 11.5 %collective-permute-start.2 = (bf16[112,768]{1,0:T(8,128)(2,1)}, bf16[112,768]{1,0:T(8,128)(2,1)S(1)}, u32[]{:S(2)}, u32[]{:S(2)}) collective-permute-start(bf16[112,768]{1,0:T(8,128)(2,1)} %block.1.refs_0_), channel_id=1, source_target_pairs={{0,24},{4,28},{8,0},{12,4},{16,8},{20,12},{24,16},{28,20},{1,25},{... | collective-permute-start | bytes 516104 | tf_op jit(solution)/shard_map/ppermute | solution.py:223
  11.9 21.2 %copy-start.1 = (s32[1,8]{1,0:T(1,128)S(1)}, s32[1,8]{1,0:T(1,128)}, u32[]{:S(2)}) copy-start(s32[1,8]{1,0:T(1,128)} %param.21) | copy-start | bytes 100
  22.8 9.5 %collective-permute-start.3 = (bf16[4,112,768]{2,1,0:T(8,128)(2,1)}, bf16[4,112,768]{2,1,0:T(8,128)(2,1)S(1)}, u32[]{:S(2)}, u32[]{:S(2)}) collective-permute-start(bf16[4,112,768]{2,1,0:T(8,128)(2,1)} %line_up.2.own), channel_id=1, source_target_pairs={{0,4},{4,0},{8,12},{12,8},{16,20},{20,16},{24,28},{28,24},{1,5},{5... | collective-permute-start | bytes 2064392 | tf_op jit(solution)/shard_map/ppermute | solution.py:223
  22.8 19.6 %collective-permute-start.4 = (bf16[4,112,768]{2,1,0:T(8,128)(2,1)}, bf16[4,112,768]{2,1,0:T(8,128)(2,1)S(1)}, u32[]{:S(2)}, u32[]{:S(2)}) collective-permute-start(bf16[4,112,768]{2,1,0:T(8,128)(2,1)} %line_up.2.own), channel_id=1, source_target_pairs={{0,1},{1,0},{2,3},{3,2},{4,5},{5,4},{6,7},{7,6},{8,9},{9,8},{10,11... | collective-permute-start | bytes 2064392 | tf_op jit(solution)/shard_map/ppermute | solution.py:223
  24.3 18.1 %collective-permute-start.5 = (bf16[4,112,768]{2,1,0:T(8,128)(2,1)}, bf16[4,112,768]{2,1,0:T(8,128)(2,1)S(1)}, u32[]{:S(2)}, u32[]{:S(2)}) collective-permute-start(bf16[4,112,768]{2,1,0:T(8,128)(2,1)} %line_up.2.own), channel_id=1, source_target_pairs={{0,2},{1,3},{2,0},{3,1},{4,6},{5,7},{6,4},{7,5},{8,10},{9,11},{10,... | collective-permute-start | bytes 2064392 | tf_op jit(solution)/shard_map/ppermute | solution.py:223
  26.5 15.8 %collective-permute-start.6 = (bf16[96,768]{1,0:T(8,128)(2,1)S(1)}, bf16[96,768]{1,0:T(8,128)(2,1)S(1)}, u32[]{:S(2)}, u32[]{:S(2)}) collective-permute-start(bf16[96,768]{1,0:T(8,128)(2,1)S(1)} %copy-done.18), channel_id=1, source_target_pairs={{0,8},{4,12},{8,16},{12,20},{16,24},{20,28},{24,0},{28,4},{1,9},{5... | collective-permute-start | bytes 442376 | tf_op jit(solution)/shard_map/ppermute | solution.py:223
  30.7 11.7 %collective-permute-start.7 = (bf16[96,768]{1,0:T(8,128)(2,1)S(1)}, bf16[96,768]{1,0:T(8,128)(2,1)S(1)}, u32[]{:S(2)}, u32[]{:S(2)}) collective-permute-start(bf16[96,768]{1,0:T(8,128)(2,1)S(1)} %copy-done.18), channel_id=1, source_target_pairs={{0,16},{4,20},{8,24},{12,28},{16,0},{20,4},{24,8},{28,12},{1,17},{... | collective-permute-start | bytes 442376 | tf_op jit(solution)/shard_map/ppermute | solution.py:223
  32.3 10.0 %collective-permute-start.8 = (bf16[96,768]{1,0:T(8,128)(2,1)S(1)}, bf16[96,768]{1,0:T(8,128)(2,1)S(1)}, u32[]{:S(2)}, u32[]{:S(2)}) collective-permute-start(bf16[96,768]{1,0:T(8,128)(2,1)S(1)} %copy-done.18), channel_id=1, source_target_pairs={{0,24},{4,28},{8,0},{12,4},{16,8},{20,12},{24,16},{28,20},{1,25},{... | collective-permute-start | bytes 442376 | tf_op jit(solution)/shard_map/ppermute | solution.py:223
  42.4 9.0 %collective-permute-start.10 = (bf16[4,112,768]{2,1,0:T(8,128)(2,1)S(1)}, bf16[4,112,768]{2,1,0:T(8,128)(2,1)S(1)}, u32[]{:S(2)}, u32[]{:S(2)}) collective-permute-start(bf16[4,112,768]{2,1,0:T(8,128)(2,1)S(1)} %collective-permute-done.5.own), channel_id=1, source_target_pairs={{0,4},{4,0},{8,12},{12,8},{16,20},{20,16},{24,28},{28,24},{1,5},{5... | collective-permute-start | bytes 2064392 | tf_op jit(solution)/shard_map/ppermute | solution.py:223
  42.5 10.6 %collective-permute-start.9 = (bf16[4,112,768]{2,1,0:T(8,128)(2,1)S(1)}, bf16[4,112,768]{2,1,0:T(8,128)(2,1)S(1)}, u32[]{:S(2)}, u32[]{:S(2)}) collective-permute-start(bf16[4,112,768]{2,1,0:T(8,128)(2,1)S(1)} %collective-permute-done.4.own), channel_id=1, source_target_pairs={{0,4},{4,0},{8,12},{12,8},{16,20},{20,16},{24,28},{28,24},{1,5},{5... | collective-permute-start | bytes 2064392 | tf_op jit(solution)/shard_map/ppermute | solution.py:223
  45.7 17.4 %collective-permute-start.11 = (bf16[4,112,768]{2,1,0:T(8,128)(2,1)S(1)}, bf16[4,112,768]{2,1,0:T(8,128)(2,1)S(1)}, u32[]{:S(2)}, u32[]{:S(2)}) collective-permute-start(bf16[4,112,768]{2,1,0:T(8,128)(2,1)S(1)} %broadcast_select_fusion), channel_id=1, source_target_pairs={{0,1},{1,0},{2,3},{3,2},{4,6},{5,7},{6,4},{7,5},{8,9},{9,8},{10,11... | collective-permute-start | bytes 2064392 | tf_op jit(solution)/shard_map/ppermute | solution.py:223
  46.7 16.4 %collective-permute-start.12 = (bf16[1,4,96,768]{3,2,1,0:T(8,128)(2,1)S(1)}, bf16[1,4,96,768]{3,2,1,0:T(8,128)(2,1)S(1)}, u32[]{:S(2)}, u32[]{:S(2)}) collective-permute-start(bf16[1,4,96,768]{3,2,1,0:T(8,128)(2,1)S(1)} %bitcast.64), channel_id=1, source_target_pairs={{0,1},{1,0},{2,3},{3,2},{4,6},{5,7},{6,4},{7,5},{8,9},{9,8},{10,11... | collective-permute-start | bytes 1769480 | tf_op jit(solution)/shard_map/ppermute | solution.py:223
  47.8 14.6 %collective-permute-start.13 = (bf16[192,384]{1,0:T(8,128)(2,1)S(1)}, bf16[192,384]{1,0:T(8,128)(2,1)S(1)}, u32[]{:S(2)}, u32[]{:S(2)}) collective-permute-start(bf16[192,384]{1,0:T(8,128)(2,1)S(1)} %bitcast.70), channel_id=1, source_target_pairs={{0,8},{4,12},{8,16},{12,20},{16,24},{20,28},{24,0},{28,4},{1,9},{5... | collective-permute-start | bytes 442376 | tf_op jit(solution)/shard_map/ppermute | solution.py:223
  51.4 11.7 %collective-permute-start.14 = (bf16[192,384]{1,0:T(8,128)(2,1)S(1)}, bf16[192,384]{1,0:T(8,128)(2,1)S(1)}, u32[]{:S(2)}, u32[]{:S(2)}) collective-permute-start(bf16[192,384]{1,0:T(8,128)(2,1)S(1)} %bitcast.71), channel_id=1, source_target_pairs={{0,16},{4,20},{8,24},{12,28},{16,0},{20,4},{24,8},{28,12},{1,17},{... | collective-permute-start | bytes 442376 | tf_op jit(solution)/shard_map/ppermute | solution.py:223
  53.1 10.0 %collective-permute-start.15 = (bf16[192,384]{1,0:T(8,128)(2,1)S(1)}, bf16[192,384]{1,0:T(8,128)(2,1)S(1)}, u32[]{:S(2)}, u32[]{:S(2)}) collective-permute-start(bf16[192,384]{1,0:T(8,128)(2,1)S(1)} %bitcast.72), channel_id=1, source_target_pairs={{0,24},{4,28},{8,0},{12,4},{16,8},{20,12},{24,16},{28,20},{1,25},{... | collective-permute-start | bytes 442376 | tf_op jit(solution)/shard_map/ppermute | solution.py:223
  63.2 16.3 %collective-permute-start.17 = (bf16[2,4,96,768]{3,2,1,0:T(8,128)(2,1)S(1)}, bf16[2,4,96,768]{3,2,1,0:T(8,128)(2,1)S(1)}, u32[]{:S(2)}, u32[]{:S(2)}) collective-permute-start(bf16[2,4,96,768]{3,2,1,0:T(8,128)(2,1)S(1)} %pad_maximum_fusion.u0), channel_id=1, source_target_pairs={{0,2},{1,3},{2,0},{3,1},{4,5},{5,4},{6,7},{7,6},{8,10},{9,11},{10,... | collective-permute-start | bytes 3538952 | tf_op jit(solution)/shard_map/ppermute | solution.py:223
  64.2 8.2 %collective-permute-start.16 = (bf16[4,112,768]{2,1,0:T(8,128)(2,1)S(1)}, bf16[4,112,768]{2,1,0:T(8,128)(2,1)S(1)}, u32[]{:S(2)}, u32[]{:S(2)}) collective-permute-start(bf16[4,112,768]{2,1,0:T(8,128)(2,1)S(1)} %collective-permute-done.11.own), channel_id=1, source_target_pairs={{0,4},{4,0},{8,12},{12,8},{16,20},{20,16},{24,28},{28,24},{1,5},{5... | collective-permute-start | bytes 2064392 | tf_op jit(solution)/shard_map/ppermute | solution.py:223
  79.5 10.4 %collective-permute-start.18 = (bf16[2,4,96,768]{3,2,1,0:T(8,128)(2,1)S(1)}, bf16[2,4,96,768]{3,2,1,0:T(8,128)(2,1)S(1)}, u32[]{:S(2)}, u32[]{:S(2)}) collective-permute-start(bf16[2,4,96,768]{3,2,1,0:T(8,128)(2,1)S(1)} %pad_maximum_fusion.u0), channel_id=1, source_target_pairs={{0,4},{4,0},{8,12},{12,8},{16,20},{20,16},{24,28},{28,24},{1,5},{5... | collective-permute-start | bytes 3538952 | tf_op jit(solution)/shard_map/ppermute | solution.py:223
  79.5 10.4 %collective-permute-start.19 = (bf16[2,4,96,768]{3,2,1,0:T(8,128)(2,1)S(1)}, bf16[2,4,96,768]{3,2,1,0:T(8,128)(2,1)S(1)}, u32[]{:S(2)}, u32[]{:S(2)}) collective-permute-start(bf16[2,4,96,768]{3,2,1,0:T(8,128)(2,1)S(1)} %collective-permute-done.17.u1), channel_id=1, source_target_pairs={{0,4},{4,0},{8,12},{12,8},{16,20},{20,16},{24,28},{28,24},{1,5},{5... | collective-permute-start | bytes 3538952 | tf_op jit(solution)/shard_map/ppermute | solution.py:223
  80.0 9.9 %collective-permute-start.20 = (bf16[1,4,192,384]{3,2,1,0:T(8,128)(2,1)S(1)}, bf16[1,4,192,384]{3,2,1,0:T(8,128)(2,1)S(1)}, u32[]{:S(2)}, u32[]{:S(2)}) collective-permute-start(bf16[1,4,192,384]{3,2,1,0:T(8,128)(2,1)S(1)} %maximum_bitcast_fusion), channel_id=1, source_target_pairs={{0,1},{1,0},{2,3},{3,2},{4,6},{5,7},{6,4},{7,5},{8,9},{9,8},{10,11... | collective-permute-start | bytes 1769480 | tf_op jit(solution)/shard_map/ppermute | solution.py:223
  90.0 16.3 %collective-permute-start.21 = (bf16[2,4,192,384]{3,2,1,0:T(8,128)(2,1)S(1)}, bf16[2,4,192,384]{3,2,1,0:T(8,128)(2,1)S(1)}, u32[]{:S(2)}, u32[]{:S(2)}) collective-permute-start(bf16[2,4,192,384]{3,2,1,0:T(8,128)(2,1)S(1)} %pad_maximum_fusion.1.d0), channel_id=1, source_target_pairs={{0,2},{1,3},{2,0},{3,1},{4,5},{5,4},{6,7},{7,6},{8,10},{9,11},{10,... | collective-permute-start | bytes 3538952 | tf_op jit(solution)/shard_map/ppermute | solution.py:223
  106.3 8.8 %collective-permute-start.22 = (bf16[2,4,192,384]{3,2,1,0:T(8,128)(2,1)S(1)}, bf16[2,4,192,384]{3,2,1,0:T(8,128)(2,1)S(1)}, u32[]{:S(2)}, u32[]{:S(2)}) collective-permute-start(bf16[2,4,192,384]{3,2,1,0:T(8,128)(2,1)S(1)} %pad_maximum_fusion.1.d0), channel_id=1, source_target_pairs={{0,4},{4,0},{8,12},{12,8},{16,20},{20,16},{24,28},{28,24},{1,5},{5... | collective-permute-start | bytes 3538952 | tf_op jit(solution)/shard_map/ppermute | solution.py:223
  106.3 8.8 %collective-permute-start.23 = (bf16[2,4,192,384]{3,2,1,0:T(8,128)(2,1)S(1)}, bf16[2,4,192,384]{3,2,1,0:T(8,128)(2,1)S(1)}, u32[]{:S(2)}, u32[]{:S(2)}) collective-permute-start(bf16[2,4,192,384]{3,2,1,0:T(8,128)(2,1)S(1)} %collective-permute-done.21.d1), channel_id=1, source_target_pairs={{0,4},{4,0},{8,12},{12,8},{16,20},{20,16},{24,28},{28,24},{1,5},{5... | collective-permute-start | bytes 3538952 | tf_op jit(solution)/shard_map/ppermute | solution.py:223
  136.9 13.8 %collective-permute-start.24 = (bf16[4,4,192,384]{3,2,1,0:T(8,128)(2,1)}, bf16[4,4,192,384]{3,2,1,0:T(8,128)(2,1)S(1)}, u32[]{:S(2)}, u32[]{:S(2)}) collective-permute-start(bf16[4,4,192,384]{3,2,1,0:T(8,128)(2,1)} %get-tuple-element.302), channel_id=1, source_target_pairs={{0,4},{4,0},{8,12},{12,8},{16,20},{20,16},{24,28},{28,24},{1,5},{5... | collective-permute-start | bytes 7077896 | tf_op jit(solution)/shard_map/ppermute | solution.py:223
  151.4 16.3 %collective-permute-start.25 = (bf16[2,4,192,384]{3,2,1,0:T(8,128)(2,1)S(1)}, bf16[2,4,192,384]{3,2,1,0:T(8,128)(2,1)S(1)}, u32[]{:S(2)}, u32[]{:S(2)}) collective-permute-start(bf16[2,4,192,384]{3,2,1,0:T(8,128)(2,1)S(1)} %get-tuple-element.310), channel_id=1, source_target_pairs={{0,2},{1,3},{2,0},{3,1},{4,5},{5,4},{6,7},{7,6},{8,10},{9,11},{10,... | collective-permute-start | bytes 3538952 | tf_op jit(solution)/shard_map/ppermute | solution.py:223
  169.3 10.5 %collective-permute-start.27 = (bf16[4,4,96,768]{3,2,1,0:T(8,128)(2,1)S(1)}, bf16[4,4,96,768]{3,2,1,0:T(8,128)(2,1)S(1)}, u32[]{:S(2)}, u32[]{:S(2)}) collective-permute-start(bf16[4,4,96,768]{3,2,1,0:T(8,128)(2,1)S(1)} %copy-done.26), channel_id=1, source_target_pairs={{0,4},{4,0},{8,12},{12,8},{16,20},{20,16},{24,28},{28,24},{1,5},{5... | collective-permute-start | bytes 7077896 | tf_op jit(solution)/shard_map/ppermute | solution.py:223
  169.3 10.4 %collective-permute-start.26 = (bf16[1,4,192,384]{3,2,1,0:T(8,128)(2,1)S(1)}, bf16[1,4,192,384]{3,2,1,0:T(8,128)(2,1)S(1)}, u32[]{:S(2)}, u32[]{:S(2)}) collective-permute-start(bf16[1,4,192,384]{3,2,1,0:T(8,128)(2,1)S(1)} %get-tuple-element.318), channel_id=1, source_target_pairs={{0,1},{1,0},{2,3},{3,2},{4,6},{5,7},{6,4},{7,5},{8,9},{9,8},{10,11... | collective-permute-start | bytes 1769480 | tf_op jit(solution)/shard_map/ppermute | solution.py:223
  180.8 19.6 %collective-permute-start.31 = (bf16[2,4,96,768]{3,2,1,0:T(8,128)(2,1)S(1)}, bf16[2,4,96,768]{3,2,1,0:T(8,128)(2,1)S(1)}, u32[]{:S(2)}, u32[]{:S(2)}) collective-permute-start(bf16[2,4,96,768]{3,2,1,0:T(8,128)(2,1)S(1)} %get-tuple-element.337), channel_id=1, source_target_pairs={{0,2},{1,3},{2,0},{3,1},{4,5},{5,4},{6,7},{7,6},{8,10},{9,11},{10,... | collective-permute-start | bytes 3538952 | tf_op jit(solution)/shard_map/ppermute | solution.py:223
  181.9 15.4 %collective-permute-start.28 = (bf16[192,384]{1,0:T(8,128)(2,1)S(1)}, bf16[192,384]{1,0:T(8,128)(2,1)S(1)}, u32[]{:S(2)}, u32[]{:S(2)}) collective-permute-start(bf16[192,384]{1,0:T(8,128)(2,1)S(1)} %get-tuple-element.334), channel_id=1, source_target_pairs={{0,24},{4,28},{8,0},{12,4},{16,8},{20,12},{24,16},{28,20},{1,25},{... | collective-permute-start | bytes 442376 | tf_op jit(solution)/shard_map/ppermute | solution.py:223
  186.8 13.5 %collective-permute-start.29 = (bf16[192,384]{1,0:T(8,128)(2,1)S(1)}, bf16[192,384]{1,0:T(8,128)(2,1)S(1)}, u32[]{:S(2)}, u32[]{:S(2)}) collective-permute-start(bf16[192,384]{1,0:T(8,128)(2,1)S(1)} %get-tuple-element.335), channel_id=1, source_target_pairs={{0,16},{4,20},{8,24},{12,28},{16,0},{20,4},{24,8},{28,12},{1,17},{... | collective-permute-start | bytes 442376 | tf_op jit(solution)/shard_map/ppermute | solution.py:223
  187.2 13.2 %collective-permute-start.30 = (bf16[192,384]{1,0:T(8,128)(2,1)S(1)}, bf16[192,384]{1,0:T(8,128)(2,1)S(1)}, u32[]{:S(2)}, u32[]{:S(2)}) collective-permute-start(bf16[192,384]{1,0:T(8,128)(2,1)S(1)} %get-tuple-element.336), channel_id=1, source_target_pairs={{0,8},{4,12},{8,16},{12,20},{16,24},{20,28},{24,0},{28,4},{1,9},{5... | collective-permute-start | bytes 442376 | tf_op jit(solution)/shard_map/ppermute | solution.py:223
  202.1 11.5 %collective-permute-start.32 = (bf16[4,112,768]{2,1,0:T(8,128)(2,1)S(1)}, bf16[4,112,768]{2,1,0:T(8,128)(2,1)S(1)}, u32[]{:S(2)}, u32[]{:S(2)}) collective-permute-start(bf16[4,112,768]{2,1,0:T(8,128)(2,1)S(1)} %copy-done.28), channel_id=1, source_target_pairs={{0,4},{4,0},{8,12},{12,8},{16,20},{20,16},{24,28},{28,24},{1,5},{5... | collective-permute-start | bytes 2064392 | tf_op jit(solution)/shard_map/ppermute | solution.py:223
  202.1 11.4 %collective-permute-start.33 = (bf16[1,4,96,768]{3,2,1,0:T(8,128)(2,1)S(1)}, bf16[1,4,96,768]{3,2,1,0:T(8,128)(2,1)S(1)}, u32[]{:S(2)}, u32[]{:S(2)}) collective-permute-start(bf16[1,4,96,768]{3,2,1,0:T(8,128)(2,1)S(1)} %get-tuple-element.346), channel_id=1, source_target_pairs={{0,1},{1,0},{2,3},{3,2},{4,6},{5,7},{6,4},{7,5},{8,9},{9,8},{10,11... | collective-permute-start | bytes 1769480 | tf_op jit(solution)/shard_map/ppermute | solution.py:223
  215.0 16.0 %collective-permute-start.34 = (bf16[4,112,768]{2,1,0:T(8,128)(2,1)S(1)}, bf16[4,112,768]{2,1,0:T(8,128)(2,1)S(1)}, u32[]{:S(2)}, u32[]{:S(2)}) collective-permute-start(bf16[4,112,768]{2,1,0:T(8,128)(2,1)S(1)} %add_convert_fusion.6), channel_id=1, source_target_pairs={{0,1},{1,0},{2,3},{3,2},{4,6},{5,7},{6,4},{7,5},{8,9},{9,8},{10,11... | collective-permute-start | bytes 2064392 | tf_op jit(solution)/shard_map/ppermute | solution.py:223
  215.6 14.0 %collective-permute-start.35 = (bf16[96,768]{1,0:T(8,128)(2,1)S(1)}, bf16[96,768]{1,0:T(8,128)(2,1)S(1)}, u32[]{:S(2)}, u32[]{:S(2)}) collective-permute-start(bf16[96,768]{1,0:T(8,128)(2,1)S(1)} %get-tuple-element.356), channel_id=1, source_target_pairs={{0,24},{4,28},{8,0},{12,4},{16,8},{20,12},{24,16},{28,20},{1,25},{... | collective-permute-start | bytes 442376 | tf_op jit(solution)/shard_map/ppermute | solution.py:223
  216.8 14.2 %collective-permute-start.36 = (bf16[96,768]{1,0:T(8,128)(2,1)S(1)}, bf16[96,768]{1,0:T(8,128)(2,1)S(1)}, u32[]{:S(2)}, u32[]{:S(2)}) collective-permute-start(bf16[96,768]{1,0:T(8,128)(2,1)S(1)} %get-tuple-element.357), channel_id=1, source_target_pairs={{0,16},{4,20},{8,24},{12,28},{16,0},{20,4},{24,8},{28,12},{1,17},{... | collective-permute-start | bytes 442376 | tf_op jit(solution)/shard_map/ppermute | solution.py:223
  217.7 13.4 %collective-permute-start.37 = (bf16[96,768]{1,0:T(8,128)(2,1)S(1)}, bf16[96,768]{1,0:T(8,128)(2,1)S(1)}, u32[]{:S(2)}, u32[]{:S(2)}) collective-permute-start(bf16[96,768]{1,0:T(8,128)(2,1)S(1)} %get-tuple-element.358), channel_id=1, source_target_pairs={{0,8},{4,12},{8,16},{12,20},{16,24},{20,28},{24,0},{28,4},{1,9},{5... | collective-permute-start | bytes 442376 | tf_op jit(solution)/shard_map/ppermute | solution.py:223
  219.6 14.8 %copy-start.6 = (bf16[4,112,768]{2,1,0:T(8,128)(2,1)S(1)}, bf16[4,112,768]{2,1,0:T(8,128)(2,1)}, u32[]{:S(2)}) copy-start(bf16[4,112,768]{2,1,0:T(8,128)(2,1)} %get-tuple-element.343) | copy-start | bytes 2064388
  231.1 2.4 collective-permute-start.38
  231.1 3.3 %collective-permute-start.39 = (bf16[4,112,768]{2,1,0:T(8,128)(2,1)}, bf16[4,112,768]{2,1,0:T(8,128)(2,1)S(1)}, u32[]{:S(2)}, u32[]{:S(2)}) collective-permute-start(bf16[4,112,768]{2,1,0:T(8,128)(2,1)} %get-tuple-element.361), channel_id=1, source_target_pairs={{0,4},{4,0},{8,12},{12,8},{16,20},{20,16},{24,28},{28,24},{1,5},{5... | collective-permute-start | bytes 2064392 | tf_op jit(solution)/shard_map/ppermute | solution.py:223
  236.2 17.5 %collective-permute-start.40 = (bf16[4,112,768]{2,1,0:T(8,128)(2,1)S(1)}, bf16[4,112,768]{2,1,0:T(8,128)(2,1)S(1)}, u32[]{:S(2)}, u32[]{:S(2)}) collective-permute-start(bf16[4,112,768]{2,1,0:T(8,128)(2,1)S(1)} %get-tuple-element.371), channel_id=1, source_target_pairs={{0,1},{1,0},{2,3},{3,2},{4,5},{5,4},{6,7},{7,6},{8,9},{9,8},{10,11... | collective-permute-start | bytes 2064392 | tf_op jit(solution)/shard_map/ppermute | solution.py:223
  237.7 17.2 %collective-permute-start.41 = (bf16[4,112,768]{2,1,0:T(8,128)(2,1)S(1)}, bf16[4,112,768]{2,1,0:T(8,128)(2,1)S(1)}, u32[]{:S(2)}, u32[]{:S(2)}) collective-permute-start(bf16[4,112,768]{2,1,0:T(8,128)(2,1)S(1)} %get-tuple-element.372), channel_id=1, source_target_pairs={{0,2},{1,3},{2,0},{3,1},{4,6},{5,7},{6,4},{7,5},{8,10},{9,11},{10,... | collective-permute-start | bytes 2064392 | tf_op jit(solution)/shard_map/ppermute | solution.py:223
  254.9 3.8 %collective-permute-start.42 = (bf16[4,112,768]{2,1,0:T(8,128)(2,1)}, bf16[4,112,768]{2,1,0:T(8,128)(2,1)}, u32[]{:S(2)}, u32[]{:S(2)}) collective-permute-start(bf16[4,112,768]{2,1,0:T(8,128)(2,1)} %get-tuple-element.373), channel_id=1, source_target_pairs={{0,4},{4,0},{8,12},{12,8},{16,20},{20,16},{24,28},{28,24},{1,5},{5... | collective-permute-start | bytes 2064392 | tf_op jit(solution)/shard_map/ppermute | solution.py:223
  260.2 15.5 %collective-permute-start.43 = (bf16[112,768]{1,0:T(8,128)(2,1)S(1)}, bf16[112,768]{1,0:T(8,128)(2,1)S(1)}, u32[]{:S(2)}, u32[]{:S(2)}) collective-permute-start(bf16[112,768]{1,0:T(8,128)(2,1)S(1)} %get-tuple-element.382), channel_id=1, source_target_pairs={{0,24},{4,28},{8,0},{12,4},{16,8},{20,12},{24,16},{28,20},{1,25},{... | collective-permute-start | bytes 516104 | tf_op jit(solution)/shard_map/ppermute | solution.py:223
  260.7 17.5 %collective-permute-start.44 = (bf16[112,768]{1,0:T(8,128)(2,1)S(1)}, bf16[112,768]{1,0:T(8,128)(2,1)S(1)}, u32[]{:S(2)}, u32[]{:S(2)}) collective-permute-start(bf16[112,768]{1,0:T(8,128)(2,1)S(1)} %get-tuple-element.383), channel_id=1, source_target_pairs={{0,16},{4,20},{8,24},{12,28},{16,0},{20,4},{24,8},{28,12},{1,17},{... | collective-permute-start | bytes 516104 | tf_op jit(solution)/shard_map/ppermute | solution.py:223
  262.2 16.0 %collective-permute-start.45 = (bf16[112,768]{1,0:T(8,128)(2,1)S(1)}, bf16[112,768]{1,0:T(8,128)(2,1)S(1)}, u32[]{:S(2)}, u32[]{:S(2)}) collective-permute-start(bf16[112,768]{1,0:T(8,128)(2,1)S(1)} %get-tuple-element.384), channel_id=1, source_target_pairs={{0,8},{4,12},{8,16},{12,20},{16,24},{20,28},{24,0},{28,4},{1,9},{5... | collective-permute-start | bytes 516104 | tf_op jit(solution)/shard_map/ppermute | solution.py:223
  (27 other events, 112.5 us)
where the time goes:
time: 287 us; the launch traced here: 282 us
  Pallas kernels  174 us (61%)
  starting transfers between devices  50.4 us (18%)
  waiting for transfers between devices  34.6 us (12%)
  local copies, waits for them, and re-layouts  11.2 us (4%)
  other arithmetic  9.73 us (3%)
    pallas_call x20, Pallas kernels, run_far(): return run(*args[:prefetch], *given)  174 us
    ppermute x46, starting transfers between devices, beside(): lax.ppermute(v, axis, perm)  50.4 us
    ppermute x46, waiting for transfers between devices, beside(): lax.ppermute(v, axis, perm)  34.6 us
    unnamed x58, local copies, waits for them, and re-layouts  7.74 us
  transfers between devices with their start and end apart: 46, of which 14 were waited for; matrix products, arithmetic and copies ran while one was open for 3% of the time, Pallas kernels for 52%

commit v1 on v0

--- a/solution.py
+++ b/solution.py
@@ -179,6 +179,7 @@
 class Scatter:
     def __init__(self, keep, send):
         self.keep, self.send, self.round, self.total = keep, [send], axis_facts()[3], None
+        self.joined = False
 
     def stage(self):
         _, _, depth, bits = axis_facts()
@@ -205,7 +206,7 @@
         self.round -= 1
 
     def done(self):
-        return self.total is not None
+        return self.total is not None or (self.joined and self.round < 0)
 
 
 def beside(moves, compute=None, args=(), key=0, out=0):
@@ -470,9 +471,8 @@
 
 
 def block_kernel(q, k, v, o, *refs):
-    *vectors, ub, out = refs
-    tall = q.shape[0]
-    out[:tall, :] = jnp.concatenate(
+    *vectors, ub, out, slab = refs
+    out[...] = jnp.concatenate(
         [part.astype(f32) for part in (
             q[:, :PAIR], k[:, :PAIR], v[:, :PAIR], q[:, PAIR:], k[:, PAIR:], v[:, PAIR:], o[...]
         )], axis=1
@@ -481,18 +481,39 @@
     first, second = jnp.concatenate(each[:4], axis=1), jnp.concatenate(each[4:], axis=1)
     third = ub[...].astype(f32)[None, :]
     row = lax.broadcasted_iota(jnp.int32, (16, out.shape[1]), 0)
-    out[tall:, :] = jnp.where(
+    slab[...] = jnp.where(
         row == 0, first, jnp.where(row == 1, second, jnp.where(row == 2, third, 0.0))
     ).astype(bf16)
 
 
 def make_block(q, k, v, o, *vectors):
     tall, narrow = q.shape
-    out = (tall + 16, 4 * narrow)
-    return call(
-        block_kernel, "block", (1,), [whole(q.shape)] * 4 + [whole(u.shape) for u in vectors], whole(out),
-        sds(out, bf16), cost=guess(1e6, 1e6), limit=SMALL, least=0,
+    shapes = [(tall, 4 * narrow), (16, 4 * narrow)]
+    return call(
+        block_kernel, "block", (1,), [whole(q.shape)] * 4 + [whole(u.shape) for u in vectors],
+        [whole(v) for v in shapes], [sds(v, bf16) for v in shapes], cost=guess(1e6, 1e6), limit=SMALL, least=0,
     )(q, k, v, o, *vectors)
+
+
+def total_kernel(place, *refs):
+    parts, first, others = refs[:4], refs[4], refs[5:]
+    depth = parts[0].shape[0]
+    for s in range(depth):
+        z = row_of(place, 0, s, depth) // 2
+        total = sum((part[z].astype(f32) for part in parts[1:]), parts[0][z].astype(f32))
+        if s:
+            others[s - 1][...] = total.astype(bf16)
+        else:
+            first[...] = total
+
+
+def make_total(place, parts):
+    depth, height, width = parts[0].shape
+    out = (height, width)
+    return call(
+        total_kernel, "total", (1,), [whole(parts[0].shape)] * 4, [whole(out)] * depth,
+        [sds(out, f32)] + [sds(out, bf16)] * (depth - 1), prefetch=1, cost=guess(1e6, 4e6), limit=SMALL,
+    )(place, *parts)
 
 
 def unblock_kernel(total, *refs):
@@ -543,26 +564,50 @@
     )(place, *parts)
 
 
+def line_up_rows_kernel(place, *refs):
+    *parts, slab, out = refs
+    depth, tall = len(parts), parts[0].shape[0]
+    for s in range(depth):
+        z = row_of(place, 0, s, depth) // 2
+        out[pl.ds(pl.multiple_of(z * tall, 16), tall), :] = parts[s][...]
+    out[depth * tall:, :] = slab[...]
+
+
+def line_up_rows(place, parts, slab):
+    tall, width = parts[0].shape
+    out = (len(parts) * tall + 16, width)
+    return call(
+        line_up_rows_kernel, "line_up_rows", (1,), [whole((tall, width))] * len(parts) + [whole(slab.shape)],
+        whole(out), sds(out, bf16), prefetch=1, cost=guess(1e6, 1e6), limit=SMALL,
+    )(place, *parts, slab)
+
+
 def attend_one_kernel(
     away, place, bucket, lengths, x, own, other, *refs,
 ):
-    context_out, w_out, slab_out, kept, lse_out, queries_ext, keys_ext, weights_here, sems = refs[-9:]
+    *given, context_out, w_out, slab_out, kept, lse_out, queries_ext, keys_ext, weights_here, sems = refs
+    if away:
+        queries_ext, keys_ext = given[:2]
     depth, _, tall, width = weights_here.shape
     step, fsdp = pl.program_id(0), w_out_fsdp(place, depth)
     core = core_of(place, depth, fsdp)
     j = neighbour_of(place, away, depth, fsdp)
     copies = [
-        pltpu.make_async_copy(ref.at[:, :tall, :], weights_here.at[:, lax.rem(core + n, 2)], sems.at[n])
+        pltpu.make_async_copy(
+            ref.at[pl.ds(0, depth * tall), :].reshape(depth, tall, width), weights_here.at[:, lax.rem(core + n, 2)],
+            sems.at[n],
+        )
         for n, ref in enumerate((own, other))
     ]
-    copies.append(pltpu.make_async_copy(own.at[0, tall:, :], slab_out.at[0], sems.at[2]))
+    copies.append(pltpu.make_async_copy(own.at[pl.ds(depth * tall, 16), :], slab_out.at[0], sems.at[2]))
     onward = pltpu.make_async_copy(weights_here, w_out.at[j], sems.at[3])
 
     @pl.when(step == 0)
     def _():
         for copy in copies:
             copy.start()
-        segment_lanes(bucket, lengths, queries_ext, keys_ext)
+        if not away:
+            segment_lanes(bucket, lengths, queries_ext, keys_ext)
         for copy in copies:
             copy.wait()
         onward.start()
@@ -620,33 +665,36 @@
     return (place.shape[0] - 2 * depth - 1) // 5
 
 
-def attend_one(away, fsdp, place, bucket, lengths, x, own, other, shared):
+def attend_one(away, fsdp, place, bucket, lengths, x, own, other, ext, shared):
     t, d = x.shape
-    depth, height, width = own.shape
-    tall, narrow = height - 16, d // fsdp
+    depth = axis_facts()[2]
+    height, width = own.shape
+    tall, narrow = (height - 16) // depth, d // fsdp
     shapes = [(fsdp, t, narrow), (fsdp, depth, 2, tall, width), (fsdp, 16, width)]
     j = lambda place: neighbour_of(place, away, depth, fsdp)
     any_space = pl.BlockSpec(memory_space=pl.ANY)
     return call(
         functools.partial(attend_one_kernel, away), "attend", (t // PLEN,),
-        [pl.BlockSpec((PLEN, d), lambda s, *_: (s, 0)), any_space, any_space] + [any_space] * len(shared),
+        [pl.BlockSpec((PLEN, d), lambda s, *_: (s, 0)), any_space, any_space] + [held()] * len(ext)
+        + [any_space] * len(shared),
         [
             pl.BlockSpec((1, PLEN, narrow), lambda s, place, *_: (j(place), s, 0)), any_space,
             pl.BlockSpec((1, 16, width), lambda s, place, *_: (j(place), 0, 0)),
             pl.BlockSpec((PLEN, USED), lambda s, *_: (s, 0)), pl.BlockSpec((8, PLEN), lambda s, *_: (0, s)),
-        ],
-        [sds(shape, bf16) for shape in shapes] + [sds((t, USED), bf16), sds((8, t), f32)],
-        [pltpu.VMEM((t, PAIR), bf16), pltpu.VMEM((t, PAIR), bf16), pltpu.VMEM((depth, 2, tall, width), bf16),
-         pltpu.SemaphoreType.DMA((4,))],
+        ] + ([] if away else [held()] * 2),
+        [sds(shape, bf16) for shape in shapes] + [sds((t, USED), bf16), sds((8, t), f32)]
+        + ([] if away else [pltpu.VMEM((t, PAIR), bf16)] * 2),
+        ([pltpu.VMEM((8, PAIR), bf16)] * 2 if away else [])
+        + [pltpu.VMEM((depth, 2, tall, width), bf16), pltpu.SemaphoreType.DMA((4,))],
         prefetch=3, cost=guess(5e9, 8e6), limit=SMALL, free=pl.ANY,
-        aliases={6 + n: n for n in range(len(shared))},
-    )(place, bucket, lengths, x, own, other, *shared)
+        aliases={6 + len(ext) + n: n for n in range(len(shared))},
+    )(place, bucket, lengths, x, own, other, *ext, *shared)
 
 
 def attend_back_one_kernel(
-    away, place, bucket, lengths, x_t_far, kept, grad_context, lse, delta, gow_far, inner, outer, gub,
+    away, place, x_t_far, kept, grad_context, lse, delta, gow_far, inner, outer, gub, queries_ext, keys_ext,
     send, keep, grads_out,
-    queries_ext, keys_ext, grads, found, sums, x_t, gow, sems,
+    grads, found, sums, x_t, gow, sems,
 ):
     depth, height, width = send.shape
     tall = height - 16
@@ -662,7 +710,6 @@
     def _():
         for copy in copies:
             copy.start()
-        segment_lanes(bucket, lengths, queries_ext, keys_ext)
         sums[...] = jnp.zeros_like(sums)
 
     lane = lax.broadcasted_iota(jnp.int32, (PLEN, PAIR), 1)
@@ -728,7 +775,7 @@
 
 
 def attend_back_one(
-    away, fsdp, depth, place, bucket, lengths, x_t, kept, grad_context, lse, delta, gow, inner, outer, gub
+    away, fsdp, depth, place, x_t, kept, grad_context, lse, delta, gow, inner, outer, gub, q_ext, k_ext
 ):
     d, t = x_t.shape
     tall, narrow, width = d // (2 * depth), d // fsdp, 4 * d // fsdp
@@ -742,14 +789,13 @@
         [any_space, rows, pl.BlockSpec((1, PLEN, narrow), lambda s, place, *_: (j(place), s, 0)),
          pl.BlockSpec((8, PLEN), lambda s, *_: (0, s)),
          pl.BlockSpec((1, 8, PLEN), lambda s, place, *_: (j(place), 0, s)), any_space,
-         small(8, narrow), small(8, narrow), small(1, width)],
+         small(8, narrow), small(8, narrow), small(1, width), held(), held()],
         [whole(sent), whole(sent), rows],
         [sds(sent, bf16)] * 2 + [sds((t, USED), bf16)],
-        [pltpu.VMEM((t, PAIR), bf16), pltpu.VMEM((t, PAIR), bf16), pltpu.VMEM((t, USED), bf16),
-         pltpu.VMEM((d, width), bf16), pltpu.VMEM((8, USED), f32), pltpu.VMEM((d, t), bf16),
+        [pltpu.VMEM((t, USED), bf16), pltpu.VMEM((d, width), bf16), pltpu.VMEM((8, USED), f32), pltpu.VMEM((d, t), bf16),
          pltpu.VMEM((d, narrow), bf16), pltpu.SemaphoreType.DMA((2,))],
-        prefetch=3, cost=guess(10e9, 12e6), limit=SMALL,
-    )(place, bucket, lengths, x_t, kept, grad_context, lse, delta, gow, inner, outer, gub)
+        prefetch=1, cost=guess(10e9, 12e6), limit=SMALL,
+    )(place, x_t, kept, grad_context, lse, delta, gow, inner, outer, gub, q_ext, k_ext)
 
 
 def input_grad_kernel(place, inner, *refs):
@@ -978,7 +1024,9 @@
 ):
     step = pl.program_id(0)
     tiles = branch_t.shape[1] // ROWS
-    f, _, tall, narrow = send.shape
+    f, _, height, width = send.shape
+    each = d0.shape[2] // height
+    tall, narrow = height * each, width // each
     depth = (place.shape[0] - 1 - 5 * f) // 2
     shared = f == depth
 
@@ -1047,7 +1095,10 @@
             for n, made in ((1, send), (0, keep)):
                 lanes = pl.ds(pl.multiple_of(lax.rem(core + n, 2) * narrow, narrow), narrow)
                 for j in range(f):
-                    made[slot_of(place, n, j, depth, f), 0] = found[j * tall:(j + 1) * tall, lanes]
+                    slot = slot_of(place, n, j, depth, f)
+                    for r in range(each):
+                        top = j * tall + r * height
+                        made[slot, 0, :, r * narrow:(r + 1) * narrow] = found[top:top + height, lanes]
     else:
         def part(n, made):
             part_found = dot(branch_t[...], act_part[0]).astype(bf16)
@@ -1072,13 +1123,14 @@
     shared = f == depth
     parts = f
     weights = (f, d, wide) if shared else (depth, 2, d, narrow)
+    each = wide // narrow
     early = lambda s: jnp.minimum(s, tiles - 1)
     if shared:
         late = lambda s, place: place[jnp.maximum(s - tiles, 0)] // 2
     else:
         late = lambda s, place: place[(jnp.maximum(s - tiles, 0) + depth) % parts]
     made = lambda first: pl.BlockSpec(
-        (f, 1, tall, narrow), lambda s, *_: (0, jnp.clip(s - tiles - first, 0, depth - 1), 0, 0)
+        (f, 1, tall // each, narrow * each), lambda s, *_: (0, jnp.clip(s - tiles - first, 0, depth - 1), 0, 0)
     )
     rows = pl.BlockSpec((ROWS, d), lambda s, *_: (early(s), 0))
     return call(
@@ -1088,7 +1140,7 @@
         [rows, whole((slots, d)), held(), held(), whole((cuts, 8, d // cuts)), made(0), made(0 if shared else depth),
          whole(weights)],
         [sds((t, d), bf16), sds((slots, d), f32), pltpu.VMEM((t, d), f32), pltpu.VMEM((t, d), bf16)]
-        + [sds((cuts, 8, d // cuts), f32)] + [sds((f, depth, tall, narrow), bf16)] * 2
+        + [sds((cuts, 8, d // cuts), f32)] + [sds((f, depth, tall // each, narrow * each), bf16)] * 2
         + [sds(weights, bf16)],
         [pltpu.VMEM((d, t), bf16), pltpu.VMEM((slots, 128), f32), pltpu.VMEM((8, d), f32),
          pltpu.VMEM((d, wide), bf16), pltpu.SemaphoreType.DMA((2 * f,))],
@@ -1228,14 +1280,14 @@
     down_t = down_weight.T
 
     if by_head:
-        block = make_block(
+        block, slab = make_block(
             query_weight, key_weight, value_weight, out_weight, query_bias, value_bias, out_bias, norm1_gain,
             norm1_bias, down_bias, norm2_gain, norm2_bias, up_bias,
         )
         along = Once([(block, "dp", along_z(s)) for s in range(1, depth)])
         x_t, = beside([along], lambda x: (x.T,), (tokens,))
         own = [block] + along.got
-        own = line_up(place, own)
+        own = line_up_rows(place, own, slab)
         swap = lambda v: (v, "dp", across_cores())
         in_plane = lambda v, s: (v, "fsdp", [(f, f ^ s) for f in range(fsdp)])
         paired = Once([swap(own)])
@@ -1245,7 +1297,10 @@
         sides = Once([in_plane(own, 1), in_plane(own, 2)])
         one = lambda away: functools.partial(attend_one, away, fsdp)
         run = (bucket, lengths, tokens)
-        *shared, kept_0, lse_0 = beside([sides, ups], one(0), (place, *run, own, pair_0, []), out=3)
+        *shared, kept_0, lse_0, q_ext, k_ext = beside(
+            [sides, ups], one(0), (place, *run, own, pair_0, [], []), out=3
+        )
+        ext = [q_ext, k_ext]
         own_x, own_y = sides.got
         to_u = Gather(line_up(place, [up_weight] + ups.got))
         paired = Once([swap(own_x), swap(own_y)])
@@ -1253,12 +1308,17 @@
         beside([paired])
         pair_x, pair_y = paired.got
         downs = Once([(down_t, "dp", along_z(s)) for s in range(1, depth)])
-        *shared, kept_1, lse_1 = beside([corner, to_u, downs], one(1), (place, *run, own_x, pair_x, shared), out=3)
+        *shared, kept_1, lse_1 = beside([corner, to_u, downs], one(1), (place, *run, own_x, pair_x, ext, shared), out=3)
         own_c = corner.got[0]
         to_d = Gather(jnp.stack([down_t] + downs.got))
-        paired = Once([swap(own_c)])
-        *shared, kept_2, lse_2 = beside([paired, to_u], one(2), (place, *run, own_y, pair_y, shared), out=3)
-        *shared, kept_3, lse_3 = beside([to_u, to_d], one(3), (place, *run, own_c, paired.got[0], shared), out=3)
+
+        def last_two(place, own_c):
+            pair_c = lax.ppermute(own_c, "dp", across_cores())
+            *part, kept_2, lse_2 = one(2)(place, *run, own_y, pair_y, ext, shared)
+            *part, kept_3, lse_3 = one(3)(place, *run, own_c, pair_c, ext, part)
+            return [*part, kept_2, lse_2, kept_3, lse_3]
+
+        *shared, kept_2, lse_2, kept_3, lse_3 = beside([to_u], last_two, (place, own_c), out=5)
         context, weights, slabs = shared
         ow, last = weights.reshape(fsdp, d, width), 2
         count, head_of = 8 * fsdp, lambda r: jnp.where(r % 8 < HEADS, r // 8 * HEADS + r % 8, -1)
@@ -1278,15 +1338,11 @@
         context, ow, last = context[None], weights[3:], 0
         count, head_of = PAIR, lambda r: 2 * (r % HD) + r // HD
 
+    n1, r1, low, low_t, ow, given = beside(
+        [to_u, to_d], attended, (tokens, context, ow, last, slabs), key=4, out=5
+    )
     finish(to_u)
-
-    def attended_up(place, *args):
-        normal = attended(*args)
-        return [*normal, *up(place, normal[2], slabs, to_u.blocks)]
-
-    n1, r1, low, low_t, ow, given, active, slope, uw = beside(
-        [to_d], attended_up, (place, tokens, context, ow, last, slabs), key=5, out=6
-    )
+    active, slope, uw = beside([to_d], up, (place, low, slabs, to_u.blocks))
     active, slope = beside([to_d], up_rest, (place, low, slabs, uw, active, slope))
     finish(to_d)
     cuts = context.shape[0]
@@ -1304,6 +1360,7 @@
         (place, branch, slope, dw, uw, low_t, so_far, shared),
     )
     of_u = Scatter(keep_u, send_u)
+    of_d.joined = of_u.joined = by_head
     inner, inner_vectors, gow, grad_context, delta = beside(
         [of_d, of_u], functools.partial(inner_back, count, head_of), (grad_normed, n1, r1, given, context, ow),
         key=3, out=2
@@ -1313,35 +1370,39 @@
         delta = delta.reshape(fsdp, 8, t)
 
         def back(away, moves, kept, lse):
-            args = (place, bucket, lengths, x_t, kept, grad_context, lse, delta, gow, inner_vectors, down_vectors, gub)
+            args = (place, x_t, kept, grad_context, lse, delta, gow, inner_vectors, down_vectors, gub, q_ext, k_ext)
             return beside(moves, functools.partial(attend_back_one, away, fsdp, depth), args)
 
         send_3, keep_3, grads_3 = back(3, [of_d, of_u], kept_3, lse_3)
         swap_3 = Once([swap(send_3)])
         send_1, keep_1, grads_1 = back(1, [swap_3, of_u], kept_1, lse_1)
         corner = Once([(add(keep_3, swap_3.got[0]), ("dp", "fsdp"), along_bit(0))])
-        send_2, keep_2, grads_2 = back(2, [corner, of_u], kept_2, lse_2)
-        sums = Once([swap(send_1), swap(send_2)])
-        beside([sums])
+        both = [
+            (jnp.concatenate([u, v]), "dp", along_z(-s - 1)) for s, (u, v) in enumerate(zip(of_u.send, of_d.send))
+        ]
+        near, rest = Once(both[:1]), Once(both[1:])
+        swap_1 = Once([swap(send_1)])
+        send_2, keep_2, grads_2 = back(2, [corner, near, swap_1], kept_2, lse_2)
+        swap_2 = Once([swap(send_2)])
+        beside([swap_2])
         add_both = lambda *v: sum(u.astype(f32) for u in v)
         through = corner.got[0]
-        sum_1 = add_both(keep_1, sums.got[0]) + select_core(jnp.zeros_like(through), through).astype(f32)
-        sum_2 = add_both(keep_2, sums.got[1]) + select_core(through, jnp.zeros_like(through)).astype(f32)
+        sum_1 = add_both(keep_1, swap_1.got[0]) + select_core(jnp.zeros_like(through), through).astype(f32)
+        sum_2 = add_both(keep_2, swap_2.got[0]) + select_core(through, jnp.zeros_like(through)).astype(f32)
         sides = Once([in_plane(sum_1.astype(bf16), 1), in_plane(sum_2.astype(bf16), 2)])
-        send_0, keep_0, grads_0 = back(0, [sides, of_u], kept_0, lse_0)
+        send_0, keep_0, grads_0 = back(0, [sides, rest], kept_0, lse_0)
         sums = Once([swap(send_0)])
         beside([sums, of_u])
-        total = add_both(keep_0, sums.got[0], *sides.got)
-        z = lax.axis_index("dp") // 2
-        at = lambda s: lax.dynamic_index_in_dim(total, (z - s) % depth, 0, keepdims=False)
-        along = Once([(at(s).astype(bf16), "dp", along_z(-s)) for s in range(1, depth)])
+        mine, *away = make_total(place, [keep_0, sums.got[0], *sides.got])
+        along = Once([(v, "dp", along_z(-s - 1)) for s, v in enumerate(away)])
         input_grad, = beside(
             [along, of_u], make_input_grad, (place, inner, (grads_0, grads_1, grads_2, grads_3), weights)
         )
-        *made, gqb, gvb, gob, gg1, gb1, gdb, gg2, gb2, gub = unblock(at(0), along.got)
+        *made, gqb, gvb, gob, gg1, gb1, gdb, gg2, gb2, gub = unblock(mine, along.got)
         vectors = (gqb, gvb, gob, gg1, gb1, gdb, gg2, gb2)
-        finish(of_d)
-        finish(of_u)
+        got, input_grad = lax.optimization_barrier((near.got + rest.got, input_grad))
+        sum_u = add_both(of_u.keep, *(v[:tall] for v in got))
+        sum_d = add_both(of_d.keep, *(v[tall:] for v in got))
     else:
         gg1, gb1, gob = (inner_vectors[0, n:n + 1] for n in range(3))
         gdb, gg2, gb2 = (down_vectors[0, n:n + 1] for n in range(3))
@@ -1358,9 +1419,14 @@
         made = [made_a[:tall, m * narrow:(m + 1) * narrow] for m in range(4)]
         vectors = [made_a[tall + n, m * narrow:(m + 1) * narrow] for n in range(2) for m in range(4)]
         gub = made_a[tall + 2]
+    if not by_head:
+        sum_u, sum_d = of_u.total, of_d.total
+    columns = down_weight.shape[0]
+    made_u = sum_u
+    made_d = jnp.concatenate([sum_d[:, c:c + columns] for c in range(0, width, columns)])
     return (
         out, pooled, input_grad, made[0], vectors[0], made[1], made[2], vectors[1], made[3], vectors[2], vectors[3],
-        vectors[4], of_u.total, gub, of_d.total.T, vectors[5], vectors[6], vectors[7],
+        vectors[4], made_u, gub, made_d.T, vectors[5], vectors[6], vectors[7],
     )
 
 

time: 287 us -> 279 us (0.972)
  waiting for transfers between devices: 34.6 us -> 42.2 us
  starting transfers between devices: 50.4 us -> 43 us
  local copies, waits for them, and re-layouts: 11.2 us -> 7.32 us
  other arithmetic: 9.73 us -> 6.21 us
    ppermute x46 -> x42, waiting for transfers between devices: 34.6 us -> 42.2 us  [beside(): lax.ppermute(v, axis, perm)]
    ppermute x46 -> x42, starting transfers between devices: 50.4 us -> 43 us  [beside(): lax.ppermute(v, axis, perm)]
    unnamed x58 -> x50, local copies, waits for them, and re-layouts: 7.74 us -> 4.58 us
    pallas_call x20 -> x21, Pallas kernels: 174 us -> 173 us  [run_far(): return run(*args[:prefetch], *given)]
  transfers between devices with their start and end apart: 46 -> 43, of which waited for: 14 -> 14; matrix products, arithmetic and copies ran while one was open for 3% -> 1% of each run, Pallas kernels for 52% -> 52%
where the time goes in v1:
time: 279 us; the launch traced here: 274 us
  Pallas kernels  173 us (62%)
  starting transfers between devices  43 us (15%)
  waiting for transfers between devices  42.2 us (15%)
  local copies, waits for them, and re-layouts  7.32 us (3%)
  other arithmetic  6.21 us (2%)
    pallas_call x21, Pallas kernels, run_far(): return run(*args[:prefetch], *given)  173 us
    ppermute x42, starting transfers between devices, beside(): lax.ppermute(v, axis, perm)  43 us
    ppermute x42, waiting for transfers between devices, beside(): lax.ppermute(v, axis, perm)  42.2 us
  transfers between devices with their start and end apart: 43, of which 14 were waited for; matrix products, arithmetic and copies ran while one was open for 1% of the time, Pallas kernels for 52%

profile of v1, /device:TPU:0, one launch (start us, length us, event | category | flops | bytes accessed | tf_op | source)
XLA Modules:
  0.0 273.7 jit_solution(11627642440633611334)
XLA Ops:
  0.7 1.7 block.1
  2.4 3.0 %collective-permute-start = (bf16[96,768]{1,0:T(8,128)(2,1)}, bf16[96,768]{1,0:T(8,128)(2,1)S(1)}, u32[]{:S(2)}, u32[]{:S(2)}) collective-permute-start(bf16[96,768]{1,0:T(8,128)(2,1)} %get-tuple-element.219.refs_0_), channel_id=1, source_target_pairs={{0,8},{4,12},{8,16},{12,20},{16,24},{20,28},{24,0},{28,4},{1,9},{5... | collective-permute-start | bytes 442376 | tf_op jit(solution)/shard_map/ppermute | solution.py:224
  5.4 2.6 collective-permute-start.1
  8.0 1.3 collective-permute-start.2
  9.4 2.6 copy.51
  12.4 5.5 %collective-permute-done.1.refs_2_ = bf16[96,768]{1,0:T(8,128)(2,1)S(1)} collective-permute-done((bf16[96,768]{1,0:T(8,128)(2,1)}, bf16[96,768]{1,0:T(8,128)(2,1)S(1)}, u32[]{:S(2)}, u32[]{:S(2)}) %collective-permute-start.1) | collective-permute-done | bytes 147488 | tf_op jit(solution)/shard_map/ppermute | solution.py:224
  18.6 2.5 line_up_rows.1.own
  21.1 1.5 collective-permute-start.4
  22.6 1.5 collective-permute-start.5
  24.8 3.6 %collective-permute-start.6 = (bf16[96,768]{1,0:T(8,128)(2,1)S(1)}, bf16[96,768]{1,0:T(8,128)(2,1)S(1)}, u32[]{:S(2)}, u32[]{:S(2)}) collective-permute-start(bf16[96,768]{1,0:T(8,128)(2,1)S(1)} %copy-done.18), channel_id=1, source_target_pairs={{0,8},{4,12},{8,16},{12,20},{16,24},{20,28},{24,0},{28,4},{1,9},{5... | collective-permute-start | bytes 442376 | tf_op jit(solution)/shard_map/ppermute | solution.py:224
  28.5 1.7 collective-permute-start.7
  32.0 8.0 %attend.4 = (bf16[4,1024,192]{2,1,0:T(8,128)(2,1)}, bf16[4,4,2,96,768]{4,3,2,1,0:T(8,128)(2,1)}, bf16[4,16,768]{2,1,0:T(8,128)(2,1)}, bf16[1024,640]{1,0:T(8,128...) custom-call(s32[29]{0:T(128)S(1)} %concatenate.21.place, ...), custom_call_target="tpu_custom_call" | custom-call | flops 5000000000 | bytes 8000000 | tf_op jit(solution)/shard_map/attend/pallas_call | solution.py:79
  40.8 2.5 line_up.1
  44.4 1.1 collective-permute-start.12
  45.5 3.4 %collective-permute-start.13 = (bf16[192,384]{1,0:T(8,128)(2,1)S(1)}, bf16[192,384]{1,0:T(8,128)(2,1)S(1)}, u32[]{:S(2)}, u32[]{:S(2)}) collective-permute-start(bf16[192,384]{1,0:T(8,128)(2,1)S(1)} %bitcast.56), channel_id=1, source_target_pairs={{0,8},{4,12},{8,16},{12,20},{16,24},{20,28},{24,0},{28,4},{1,9},{5... | collective-permute-start | bytes 442376 | tf_op jit(solution)/shard_map/ppermute | solution.py:224
  48.9 1.3 collective-permute-start.14
  50.2 1.6 collective-permute-start.15
  51.8 7.4 %attend.5 = (bf16[4,1024,192]{2,1,0:T(8,128)(2,1)}, bf16[4,4,2,96,768]{4,3,2,1,0:T(8,128)(2,1)}, bf16[4,16,768]{2,1,0:T(8,128)(2,1)}, bf16[1024,640]{1,0:T(8,128)(2,1)}, f32[8,1024]{1,0:T(8,128)}) custom-call(s32[29]{0:T(128)S(1)} %concatenate.21.place, s32[1]{0:T(128)S(6)} %copy.66.bucket, ...), custom_call_target="tpu_custom_call", output_to_operand_aliasing={{0}: (8, {}), {1}: (9, {}), {2}: (10, {})} | custom-call | flops 5000000000 | bytes 8000000 | tf_op jit(solution)/shard_map/attend/pallas_call | solution.py:79
  61.0 7.4 %attend.6 = (bf16[4,1024,192]{2,1,0:T(8,128)(2,1)}, bf16[4,4,2,96,768]{4,3,2,1,0:T(8,128)(2,1)}, bf16[4,16,768]{2,1,0:T(8,128)(2,1)}, bf16[1024,640]{1,0:T(8,128)(2,1)}, f32[8,1024]{1,0:T(8,128)}) custom-call(s32[29]{0:T(128)S(1)} %concatenate.21.place, s32[1]{0:T(128)S(6)} %copy.66.bucket, ...), custom_call_target="tpu_custom_call", output_to_operand_aliasing={{0}: (8, {}), {1}: (9, {}), {2}: (10, {})} | custom-call | flops 5000000000 | bytes 8000000 | tf_op jit(solution)/shard_map/attend/pallas_call | solution.py:79
  68.4 7.4 %attend.7 = (bf16[4,1024,192]{2,1,0:T(8,128)(2,1)}, bf16[4,4,2,96,768]{4,3,2,1,0:T(8,128)(2,1)}, bf16[4,16,768]{2,1,0:T(8,128)(2,1)}, bf16[1024,640]{1,0:T(8,128)(2,1)}, f32[8,1024]{1,0:T(8,128)}) custom-call(s32[29]{0:T(128)S(1)} %concatenate.21.place, s32[1]{0:T(128)S(6)} %copy.66.bucket, ...), custom_call_target="tpu_custom_call", output_to_operand_aliasing={{0}: (8, {}), {1}: (9, {}), {2}: (10, {})} | custom-call | flops 5000000000 | bytes 8000000 | tf_op jit(solution)/shard_map/attend/pallas_call | solution.py:79
  77.3 5.7 %attended.1 = (f32[1024,768]{1,0:T(8,128)S(1)}, f32[1024,128]{1,0:T(8,128)S(1)}, bf16[1024,768]{1,0:T(8,128)(2,1)S(1)}, bf16[768,1024]{1,0:T(8,128)(2,1)S(1)}, b...) custom-call(bf16[1024,768]{1,0:T(8,128)(2,1)} %x.9, bf16[4,1024,192]{2,1,0:T(8,128)(2,1)} %get-tuple-element.264.context, ...), custom_call_target="tpu_custom_call" | custom-call | flops 3000000000 | bytes 10000000 | tf_op jit(solution)/shard_map/attended/pallas_call | solution.py:79
  83.1 3.6 %collective-permute-done.20 = bf16[1,4,192,384]{3,2,1,0:T(8,128)(2,1)S(1)} collective-permute-done((bf16[1,4,192,384]{3,2,1,0:T(8,128)(2,1)S(1)}, bf16[1,4,192,384]{3,2,1,0:T(8,128)(2,1)S(1)}, u32[]{:S(2)}, u32[]{:S(2)}) %collective-permute-start.20) | collective-permute-done | bytes 589856 | tf_op jit(solution)/shard_map/ppermute | solution.py:224
  87.8 9.2 %up.1 = (bf16[4,1024,768]{2,1,0:T(8,128)(2,1)}, bf16[4,1024,768]{2,1,0:T(8,128)(2,1)}, bf16[4,4,2,96,768]{4,3,2,1,0:T(8,128)(2,1)}) custom-call(s32[29]{0:T(128)S(1)} %concatenate.21.place, bf16[1024,768]{1,0:T(8,128)(2,1)S(1)} %get-tuple-element.277.low, bf16[4,16,768]{2,1,0:T(8,128)(2,1)} %get-tuple-element.270.slabs, ...), custom_call_target="tpu_custom_call" | custom-call | flops 6000000000 | bytes 20000000 | tf_op jit(solution)/shard_map/up/pallas_call | solution.py:79
  97.1 6.1 %collective-permute-done.21.d1 = bf16[2,4,192,384]{3,2,1,0:T(8,128)(2,1)S(1)} collective-permute-done((bf16[2,4,192,384]{3,2,1,0:T(8,128)(2,1)S(1)}, bf16[2,4,192,384]{3,2,1,0:T(8,128)(2,1)S(1)}, u32[]{:S(2)}, u32[]{:S(2)}) %collective-permute-start.21) | collective-permute-done | bytes 1179680 | tf_op jit(solution)/shard_map/ppermute | solution.py:224
  103.6 8.1 %up_rest.1 = (bf16[4,1024,768]{2,1,0:T(8,128)(2,1)}, bf16[4,1024,768]{2,1,0:T(8,128)(2,1)}) custom-call(s32[29]{0:T(128)S(1)} %concatenate.21.place, bf16[1024,768]{1,0:T(8,128)(2,1)S(1)} %get-tuple-element.277.low, bf16[4,16,768]{2,1,0:T(8,128)(2,1)} %get-tuple-element.270.slabs, ...), custom_call_target="tpu_custom_call", output_to_operand_aliasing={{0}: (4, {}), {1}: (5, {})} | custom-call | flops 6000000000 | bytes 16000000 | tf_op jit(solution)/shard_map/up_rest/pallas_call | solution.py:79
  111.8 21.9 %down.1 = (bf16[1024,768]{1,0:T(8,128)(2,1)}, f32[8,768]{1,0:T(8,128)}, f32[1024,768]{1,0:T(8,128)S(1)}, bf16[1024,768]{1,0:T(8,128)(2,1)S(1)}, f32[4,8,192]{2,1...) custom-call(s32[29]{0:T(128)S(1)} %concatenate.21.place, ...), custom_call_target="tpu_custom_call" | custom-call | flops 12000000000 | bytes 35000000 | tf_op jit(solution)/shard_map/down/pallas_call | solution.py:79
  133.7 13.7 %feed_back.2 = (bf16[4,4,96,768]{3,2,1,0:T(8,128)(2,1)}, bf16[4,4,96,768]{3,2,1,0:T(8,128)(2,1)}, f32[4,1,768]{2,1,0:T(1,128)}, f32[1024,768]{1,0:T(8,128)S(1)}) custom-call(s32[29]{0:T(128)S(1)} %concatenate.21.place, bf16[1024,768]{1,0:T(8,128)(2,1)S(1)} %get-tuple-element.300.branch, bf16[4,1024,768]{2,1,0:T(8,128)(2,1)} %get-tuple-element.301.slope, ...), custom_call_target="tpu_custom_call" | custom-call | flops 15000000512 | bytes 35000000 | tf_op jit(solution)/shard_map/feed_back/pallas_call | solution.py:79
  149.0 13.5 %feed_back.3 = (bf16[4,4,96,768]{3,2,1,0:T(8,128)(2,1)}, bf16[4,4,96,768]{3,2,1,0:T(8,128)(2,1)}, f32[4,1,768]{2,1,0:T(1,128)}, f32[1024,768]{1,0:T(8,128)S(1)}) custom-call(s32[29]{0:T(128)S(1)} %concatenate.21.place, bf16[1024,768]{1,0:T(8,128)(2,1)S(1)} %get-tuple-element.300.branch, ...), custom_call_target="tpu_custom_call", output_to_operand_aliasing={{0}: (7, {}), {1}: (8, {}), {2}: (9, {})} | custom-call | flops 15000000512 | bytes 35000000 | tf_op jit(solution)/shard_map/feed_back/pallas_call | solution.py:79
  162.5 1.8 collective-permute-done.25
  164.6 1.4 copy-done.22
  166.5 9.8 %inner_back.1 = (f32[1024,768]{1,0:T(8,128)}, f32[4,8,192]{2,1,0:T(8,128)}, bf16[4,768,192]{2,1,0:T(8,128)(2,1)}, bf16[4,1024,192]{2,1,0:T(8,128)(2,1)}, f32[32,1024]{1,0:T(8,128)}) custom-call(f32[1024,768]{1,0:T(8,128)S(1)} %get-tuple-element.314.grad_normed, f32[1024,768]{1,0:T(8,128)S(1)} %get-tuple-element.291.n1, ...), custom_call_target="tpu_custom_call" | custom-call | flops 4000000000 | bytes 10000000 | tf_op jit(solution)/shard_map/inner_back/pallas_call | solution.py:79
  178.1 9.3 %attend_back.4 = (bf16[4,112,768]{2,1,0:T(8,128)(2,1)}, bf16[4,112,768]{2,1,0:T(8,128)(2,1)}, bf16[1024,640]{1,0:T(8,128)(2,1)}) custom-call(s32[29]{0:T(128)S(1)} %concatenate.21.place, bf16[768,1024]{1,0:T(8,128)(2,1)} %bitcast.52, bf16[1024,640]{1,0:T(8,128)(2,1)} %get-tuple-element.328.kept, bf16[4,1024,192]{2,1,0:T(8,128)(2,1)} %get-tuple-element.329.grad_context, ...), custom_call_target="tpu_custom_call" | custom-call | flops 10000000000 | bytes 12000000 | tf_op jit(solution)/shard_map/attend_back/pallas_call | solution.py:79
  187.4 6.0 %collective-permute-done.28 = bf16[2,4,96,768]{3,2,1,0:T(8,128)(2,1)S(1)} collective-permute-done((bf16[2,4,96,768]{3,2,1,0:T(8,128)(2,1)S(1)}, bf16[2,4,96,768]{3,2,1,0:T(8,128)(2,1)S(1)}, u32[]{:S(2)}, u32[]{:S(2)}) %collective-permute-start.28) | collective-permute-done | bytes 1179680 | tf_op jit(solution)/shard_map/ppermute | solution.py:224
  193.7 1.6 collective-permute-start.30
  195.3 9.3 %attend_back.5 = (bf16[4,112,768]{2,1,0:T(8,128)(2,1)}, bf16[4,112,768]{2,1,0:T(8,128)(2,1)}, bf16[1024,640]{1,0:T(8,128)(2,1)}) custom-call(s32[29]{0:T(128)S(1)} %concatenate.21.place, bf16[768,1024]{1,0:T(8,128)(2,1)} %bitcast.53, bf16[1024,640]{1,0:T(8,128)(2,1)} %get-tuple-element.342.kept, bf16[4,1024,192]{2,1,0:T(8,128)(2,1)} %get-tuple-element.329.grad_context, ...), custom_call_target="tpu_custom_call" | custom-call | flops 10000000000 | bytes 12000000 | tf_op jit(solution)/shard_map/attend_back/pallas_call | solution.py:79
  205.0 4.5 %collective-permute-start.32 = (bf16[192,768]{1,0:T(8,128)(2,1)S(1)}, bf16[192,768]{1,0:T(8,128)(2,1)S(1)}, u32[]{:S(2)}, u32[]{:S(2)}) collective-permute-start(bf16[192,768]{1,0:T(8,128)(2,1)S(1)} %pad_maximum_fusion.2), channel_id=1, source_target_pairs={{0,24},{4,28},{8,0},{12,4},{16,8},{20,12},{24,16},{28,20},{1,25},{... | collective-permute-start | bytes 884744 | tf_op jit(solution)/shard_map/ppermute | solution.py:224
  210.4 9.6 %attend_back.6 = (bf16[4,112,768]{2,1,0:T(8,128)(2,1)}, bf16[4,112,768]{2,1,0:T(8,128)(2,1)}, bf16[1024,640]{1,0:T(8,128)(2,1)}) custom-call(s32[29]{0:T(128)S(1)} %concatenate.21.place, bf16[768,1024]{1,0:T(8,128)(2,1)} %bitcast.54, bf16[1024,640]{1,0:T(8,128)(2,1)} %get-tuple-element.352.kept, bf16[4,1024,192]{2,1,0:T(8,128)(2,1)} %get-tuple-element.329.grad_context, ...), custom_call_target="tpu_custom_call" | custom-call | flops 10000000000 | bytes 12000000 | tf_op jit(solution)/shard_map/attend_back/pallas_call | solution.py:79
  220.4 2.3 collective-permute-done.34
  222.7 1.7 add_convert_fusion.4
  226.0 1.1 collective-permute-start.36
  227.1 9.3 %attend_back.7 = (bf16[4,112,768]{2,1,0:T(8,128)(2,1)}, bf16[4,112,768]{2,1,0:T(8,128)(2,1)}, bf16[1024,640]{1,0:T(8,128)(2,1)}) custom-call(s32[29]{0:T(128)S(1)} %concatenate.21.place, bf16[768,1024]{1,0:T(8,128)(2,1)} %bitcast.55, bf16[1024,640]{1,0:T(8,128)(2,1)} %get-tuple-element.365.kept, bf16[4,1024,192]{2,1,0:T(8,128)(2,1)} %get-tuple-element.329.grad_context, ...), custom_call_target="tpu_custom_call" | custom-call | flops 10000000000 | bytes 12000000 | tf_op jit(solution)/shard_map/attend_back/pallas_call | solution.py:79
  236.4 9.2 %collective-permute-done.37 = bf16[192,768]{1,0:T(8,128)(2,1)S(1)} collective-permute-done((bf16[192,768]{1,0:T(8,128)(2,1)S(1)}, bf16[192,768]{1,0:T(8,128)(2,1)S(1)}, u32[]{:S(2)}, u32[]{:S(2)}) %collective-permute-start.37) | collective-permute-done | bytes 294944 | tf_op jit(solution)/shard_map/ppermute | solution.py:224
  245.8 2.3 collective-permute-done.39.refs_1_
  248.9 3.4 %total.1 = (f32[112,768]{1,0:T(8,128)}, bf16[112,768]{1,0:T(8,128)(2,1)}, bf16[112,768]{1,0:T(8,128)(2,1)}, bf16[112,768]{1,0:T(8,128)(2,1)}) custom-call(s32[29]{0:T(128)S(1)} %concatenate.21.place, bf16[4,112,768]{2,1,0:T(8,128)(2,1)} %get-tuple-element.374.refs_0_, bf16[4,112,768]{2,1,0:T(8,128)(2,1)} %copy-done.10, bf16[4,112,768]{2,1,0:T(8,128)(2,1)} %copy-done.7, ...), custom_call_target="tpu_custom_call" | custom-call | flops 1000000 | bytes 4000000 | tf_op jit(solution)/shard_map/total/pallas_call | solution.py:79
  253.8 1.4 collective-permute-start.42
  255.1 10.7 %input_grad.1 = f32[1024,768]{1,0:T(8,128)} custom-call(s32[29]{0:T(128)S(1)} %concatenate.21.place, f32[1024,768]{1,0:T(8,128)} %get-tuple-element.382.inner, bf16[1024,640]{1,0:T(8,128)(2,1)} %get-tuple-element.383.refs_0_, bf16[1024,640]{1,0:T(8,128)(2,1)} %get-tuple-element.384.refs_1_, bf16[1024,640]{1,0:T(8,128)(2,1)} %get-tuple-element.385.refs_2_, ...), custom_call_target="tpu_custom_call" | custom-call | flops 5000000000 | bytes 15000000 | tf_op jit(solution)/shard_map/input_grad/pallas_call | solution.py:79
  265.9 3.5 %collective-permute-done.41.refs_1_ = bf16[112,768]{1,0:T(8,128)(2,1)S(1)} collective-permute-done((bf16[112,768]{1,0:T(8,128)(2,1)}, bf16[112,768]{1,0:T(8,128)(2,1)S(1)}, u32[]{:S(2)}, u32[]{:S(2)}) %collective-permute-start.41) | collective-permute-done | bytes 172064 | tf_op jit(solution)/shard_map/ppermute | solution.py:224
  271.1 2.1 unblock.1
  (132 shorter events, 21.5 us)
Async XLA Ops:
  2.4 10.0 %collective-permute-start = (bf16[96,768]{1,0:T(8,128)(2,1)}, bf16[96,768]{1,0:T(8,128)(2,1)S(1)}, u32[]{:S(2)}, u32[]{:S(2)}) collective-permute-start(bf16[96,768]{1,0:T(8,128)(2,1)} %get-tuple-element.219.refs_0_), channel_id=1, source_target_pairs={{0,8},{4,12},{8,16},{12,20},{16,24},{20,28},{24,0},{28,4},{1,9},{5... | collective-permute-start | bytes 442376 | tf_op jit(solution)/shard_map/ppermute | solution.py:224
  5.4 12.5 %collective-permute-start.1 = (bf16[96,768]{1,0:T(8,128)(2,1)}, bf16[96,768]{1,0:T(8,128)(2,1)S(1)}, u32[]{:S(2)}, u32[]{:S(2)}) collective-permute-start(bf16[96,768]{1,0:T(8,128)(2,1)} %get-tuple-element.219.refs_0_), channel_id=1, source_target_pairs={{0,16},{4,20},{8,24},{12,28},{16,0},{20,4},{24,8},{28,12},{1,17},{... | collective-permute-start | bytes 442376 | tf_op jit(solution)/shard_map/ppermute | solution.py:224
  8.0 9.9 %collective-permute-start.2 = (bf16[96,768]{1,0:T(8,128)(2,1)}, bf16[96,768]{1,0:T(8,128)(2,1)S(1)}, u32[]{:S(2)}, u32[]{:S(2)}) collective-permute-start(bf16[96,768]{1,0:T(8,128)(2,1)} %get-tuple-element.219.refs_0_), channel_id=1, source_target_pairs={{0,24},{4,28},{8,0},{12,4},{16,8},{20,12},{24,16},{28,20},{1,25},{... | collective-permute-start | bytes 442376 | tf_op jit(solution)/shard_map/ppermute | solution.py:224
  9.4 15.4 %copy-start.18 = (bf16[96,768]{1,0:T(8,128)(2,1)S(1)}, bf16[96,768]{1,0:T(8,128)(2,1)}, u32[]{:S(2)}) copy-start(bf16[96,768]{1,0:T(8,128)(2,1)} %refs_0_.3) | copy-start | bytes 442372
  9.4 21.5 %copy-start.1 = (s32[1,8]{1,0:T(1,128)S(1)}, s32[1,8]{1,0:T(1,128)}, u32[]{:S(2)}) copy-start(s32[1,8]{1,0:T(1,128)} %param.21) | copy-start | bytes 100
  21.1 9.0 %collective-permute-start.3 = (bf16[400,768]{1,0:T(8,128)(2,1)}, bf16[400,768]{1,0:T(8,128)(2,1)S(1)}, u32[]{:S(2)}, u32[]{:S(2)}) collective-permute-start(bf16[400,768]{1,0:T(8,128)(2,1)} %line_up_rows.1.own), channel_id=1, source_target_pairs={{0,4},{4,0},{8,12},{12,8},{16,20},{20,16},{24,28},{28,24},{1,5},{5... | collective-permute-start | bytes 1843208 | tf_op jit(solution)/shard_map/ppermute | solution.py:224
  21.1 19.0 %collective-permute-start.4 = (bf16[400,768]{1,0:T(8,128)(2,1)}, bf16[400,768]{1,0:T(8,128)(2,1)S(1)}, u32[]{:S(2)}, u32[]{:S(2)}) collective-permute-start(bf16[400,768]{1,0:T(8,128)(2,1)} %line_up_rows.1.own), channel_id=1, source_target_pairs={{0,1},{1,0},{2,3},{3,2},{4,5},{5,4},{6,7},{7,6},{8,9},{9,8},{10,11... | collective-permute-start | bytes 1843208 | tf_op jit(solution)/shard_map/ppermute | solution.py:224
  22.6 17.5 %collective-permute-start.5 = (bf16[400,768]{1,0:T(8,128)(2,1)}, bf16[400,768]{1,0:T(8,128)(2,1)S(1)}, u32[]{:S(2)}, u32[]{:S(2)}) collective-permute-start(bf16[400,768]{1,0:T(8,128)(2,1)} %line_up_rows.1.own), channel_id=1, source_target_pairs={{0,2},{1,3},{2,0},{3,1},{4,6},{5,7},{6,4},{7,5},{8,10},{9,11},{10,... | collective-permute-start | bytes 1843208 | tf_op jit(solution)/shard_map/ppermute | solution.py:224
  24.8 15.2 %collective-permute-start.6 = (bf16[96,768]{1,0:T(8,128)(2,1)S(1)}, bf16[96,768]{1,0:T(8,128)(2,1)S(1)}, u32[]{:S(2)}, u32[]{:S(2)}) collective-permute-start(bf16[96,768]{1,0:T(8,128)(2,1)S(1)} %copy-done.18), channel_id=1, source_target_pairs={{0,8},{4,12},{8,16},{12,20},{16,24},{20,28},{24,0},{28,4},{1,9},{5... | collective-permute-start | bytes 442376 | tf_op jit(solution)/shard_map/ppermute | solution.py:224
  28.5 11.6 %collective-permute-start.7 = (bf16[96,768]{1,0:T(8,128)(2,1)S(1)}, bf16[96,768]{1,0:T(8,128)(2,1)S(1)}, u32[]{:S(2)}, u32[]{:S(2)}) collective-permute-start(bf16[96,768]{1,0:T(8,128)(2,1)S(1)} %copy-done.18), channel_id=1, source_target_pairs={{0,16},{4,20},{8,24},{12,28},{16,0},{20,4},{24,8},{28,12},{1,17},{... | collective-permute-start | bytes 442376 | tf_op jit(solution)/shard_map/ppermute | solution.py:224
  30.1 10.0 %collective-permute-start.8 = (bf16[96,768]{1,0:T(8,128)(2,1)S(1)}, bf16[96,768]{1,0:T(8,128)(2,1)S(1)}, u32[]{:S(2)}, u32[]{:S(2)}) collective-permute-start(bf16[96,768]{1,0:T(8,128)(2,1)S(1)} %copy-done.18), channel_id=1, source_target_pairs={{0,24},{4,28},{8,0},{12,4},{16,8},{20,12},{24,16},{28,20},{1,25},{... | collective-permute-start | bytes 442376 | tf_op jit(solution)/shard_map/ppermute | solution.py:224
  40.1 8.8 %collective-permute-start.9 = (bf16[400,768]{1,0:T(8,128)(2,1)S(1)}, bf16[400,768]{1,0:T(8,128)(2,1)S(1)}, u32[]{:S(2)}, u32[]{:S(2)}) collective-permute-start(bf16[400,768]{1,0:T(8,128)(2,1)S(1)} %collective-permute-done.4.own), channel_id=1, source_target_pairs={{0,4},{4,0},{8,12},{12,8},{16,20},{20,16},{24,28},{28,24},{1,5},{5... | collective-permute-start | bytes 1843208 | tf_op jit(solution)/shard_map/ppermute | solution.py:224
  40.2 10.0 %collective-permute-start.10 = (bf16[400,768]{1,0:T(8,128)(2,1)S(1)}, bf16[400,768]{1,0:T(8,128)(2,1)S(1)}, u32[]{:S(2)}, u32[]{:S(2)}) collective-permute-start(bf16[400,768]{1,0:T(8,128)(2,1)S(1)} %collective-permute-done.5.own), channel_id=1, source_target_pairs={{0,4},{4,0},{8,12},{12,8},{16,20},{20,16},{24,28},{28,24},{1,5},{5... | collective-permute-start | bytes 1843208 | tf_op jit(solution)/shard_map/ppermute | solution.py:224
  43.4 16.5 %collective-permute-start.11 = (bf16[400,768]{1,0:T(8,128)(2,1)S(1)}, bf16[400,768]{1,0:T(8,128)(2,1)S(1)}, u32[]{:S(2)}, u32[]{:S(2)}) collective-permute-start(bf16[400,768]{1,0:T(8,128)(2,1)S(1)} %broadcast_select_fusion), channel_id=1, source_target_pairs={{0,1},{1,0},{2,3},{3,2},{4,6},{5,7},{6,4},{7,5},{8,9},{9,8},{10,11... | collective-permute-start | bytes 1843208 | tf_op jit(solution)/shard_map/ppermute | solution.py:224
  44.4 15.5 %collective-permute-start.12 = (bf16[1,4,96,768]{3,2,1,0:T(8,128)(2,1)S(1)}, bf16[1,4,96,768]{3,2,1,0:T(8,128)(2,1)S(1)}, u32[]{:S(2)}, u32[]{:S(2)}) collective-permute-start(bf16[1,4,96,768]{3,2,1,0:T(8,128)(2,1)S(1)} %bitcast.50), channel_id=1, source_target_pairs={{0,1},{1,0},{2,3},{3,2},{4,6},{5,7},{6,4},{7,5},{8,9},{9,8},{10,11... | collective-permute-start | bytes 1769480 | tf_op jit(solution)/shard_map/ppermute | solution.py:224
  45.5 13.7 %collective-permute-start.13 = (bf16[192,384]{1,0:T(8,128)(2,1)S(1)}, bf16[192,384]{1,0:T(8,128)(2,1)S(1)}, u32[]{:S(2)}, u32[]{:S(2)}) collective-permute-start(bf16[192,384]{1,0:T(8,128)(2,1)S(1)} %bitcast.56), channel_id=1, source_target_pairs={{0,8},{4,12},{8,16},{12,20},{16,24},{20,28},{24,0},{28,4},{1,9},{5... | collective-permute-start | bytes 442376 | tf_op jit(solution)/shard_map/ppermute | solution.py:224
  48.9 10.6 %collective-permute-start.14 = (bf16[192,384]{1,0:T(8,128)(2,1)S(1)}, bf16[192,384]{1,0:T(8,128)(2,1)S(1)}, u32[]{:S(2)}, u32[]{:S(2)}) collective-permute-start(bf16[192,384]{1,0:T(8,128)(2,1)S(1)} %bitcast.57), channel_id=1, source_target_pairs={{0,16},{4,20},{8,24},{12,28},{16,0},{20,4},{24,8},{28,12},{1,17},{... | collective-permute-start | bytes 442376 | tf_op jit(solution)/shard_map/ppermute | solution.py:224
  50.2 9.3 %collective-permute-start.15 = (bf16[192,384]{1,0:T(8,128)(2,1)S(1)}, bf16[192,384]{1,0:T(8,128)(2,1)S(1)}, u32[]{:S(2)}, u32[]{:S(2)}) collective-permute-start(bf16[192,384]{1,0:T(8,128)(2,1)S(1)} %bitcast.58), channel_id=1, source_target_pairs={{0,24},{4,28},{8,0},{12,4},{16,8},{20,12},{24,16},{28,20},{1,25},{... | collective-permute-start | bytes 442376 | tf_op jit(solution)/shard_map/ppermute | solution.py:224
  60.1 16.3 %collective-permute-start.17 = (bf16[2,4,96,768]{3,2,1,0:T(8,128)(2,1)S(1)}, bf16[2,4,96,768]{3,2,1,0:T(8,128)(2,1)S(1)}, u32[]{:S(2)}, u32[]{:S(2)}) collective-permute-start(bf16[2,4,96,768]{3,2,1,0:T(8,128)(2,1)S(1)} %pad_maximum_fusion.u0), channel_id=1, source_target_pairs={{0,2},{1,3},{2,0},{3,1},{4,5},{5,4},{6,7},{7,6},{8,10},{9,11},{10,... | collective-permute-start | bytes 3538952 | tf_op jit(solution)/shard_map/ppermute | solution.py:224
  60.9 7.5 %collective-permute-start.16 = (bf16[400,768]{1,0:T(8,128)(2,1)S(1)}, bf16[400,768]{1,0:T(8,128)(2,1)S(1)}, u32[]{:S(2)}, u32[]{:S(2)}) collective-permute-start(bf16[400,768]{1,0:T(8,128)(2,1)S(1)} %collective-permute-done.11.own), channel_id=1, source_target_pairs={{0,4},{4,0},{8,12},{12,8},{16,20},{20,16},{24,28},{28,24},{1,5},{5... | collective-permute-start | bytes 1843208 | tf_op jit(solution)/shard_map/ppermute | solution.py:1316
  76.3 10.4 %collective-permute-start.18 = (bf16[2,4,96,768]{3,2,1,0:T(8,128)(2,1)S(1)}, bf16[2,4,96,768]{3,2,1,0:T(8,128)(2,1)S(1)}, u32[]{:S(2)}, u32[]{:S(2)}) collective-permute-start(bf16[2,4,96,768]{3,2,1,0:T(8,128)(2,1)S(1)} %pad_maximum_fusion.u0), channel_id=1, source_target_pairs={{0,4},{4,0},{8,12},{12,8},{16,20},{20,16},{24,28},{28,24},{1,5},{5... | collective-permute-start | bytes 3538952 | tf_op jit(solution)/shard_map/ppermute | solution.py:224
  76.4 10.3 %collective-permute-start.19 = (bf16[2,4,96,768]{3,2,1,0:T(8,128)(2,1)S(1)}, bf16[2,4,96,768]{3,2,1,0:T(8,128)(2,1)S(1)}, u32[]{:S(2)}, u32[]{:S(2)}) collective-permute-start(bf16[2,4,96,768]{3,2,1,0:T(8,128)(2,1)S(1)} %collective-permute-done.17.u1), channel_id=1, source_target_pairs={{0,4},{4,0},{8,12},{12,8},{16,20},{20,16},{24,28},{28,24},{1,5},{5... | collective-permute-start | bytes 3538952 | tf_op jit(solution)/shard_map/ppermute | solution.py:224
  76.8 9.9 %collective-permute-start.20 = (bf16[1,4,192,384]{3,2,1,0:T(8,128)(2,1)S(1)}, bf16[1,4,192,384]{3,2,1,0:T(8,128)(2,1)S(1)}, u32[]{:S(2)}, u32[]{:S(2)}) collective-permute-start(bf16[1,4,192,384]{3,2,1,0:T(8,128)(2,1)S(1)} %maximum_bitcast_fusion), channel_id=1, source_target_pairs={{0,1},{1,0},{2,3},{3,2},{4,6},{5,7},{6,4},{7,5},{8,9},{9,8},{10,11... | collective-permute-start | bytes 1769480 | tf_op jit(solution)/shard_map/ppermute | solution.py:224
  86.9 16.3 %collective-permute-start.21 = (bf16[2,4,192,384]{3,2,1,0:T(8,128)(2,1)S(1)}, bf16[2,4,192,384]{3,2,1,0:T(8,128)(2,1)S(1)}, u32[]{:S(2)}, u32[]{:S(2)}) collective-permute-start(bf16[2,4,192,384]{3,2,1,0:T(8,128)(2,1)S(1)} %pad_maximum_fusion.1.d0), channel_id=1, source_target_pairs={{0,2},{1,3},{2,0},{3,1},{4,5},{5,4},{6,7},{7,6},{8,10},{9,11},{10,... | collective-permute-start | bytes 3538952 | tf_op jit(solution)/shard_map/ppermute | solution.py:224
  103.1 8.6 %collective-permute-start.22 = (bf16[2,4,192,384]{3,2,1,0:T(8,128)(2,1)S(1)}, bf16[2,4,192,384]{3,2,1,0:T(8,128)(2,1)S(1)}, u32[]{:S(2)}, u32[]{:S(2)}) collective-permute-start(bf16[2,4,192,384]{3,2,1,0:T(8,128)(2,1)S(1)} %pad_maximum_fusion.1.d0), channel_id=1, source_target_pairs={{0,4},{4,0},{8,12},{12,8},{16,20},{20,16},{24,28},{28,24},{1,5},{5... | collective-permute-start | bytes 3538952 | tf_op jit(solution)/shard_map/ppermute | solution.py:224
  103.1 8.6 %collective-permute-start.23 = (bf16[2,4,192,384]{3,2,1,0:T(8,128)(2,1)S(1)}, bf16[2,4,192,384]{3,2,1,0:T(8,128)(2,1)S(1)}, u32[]{:S(2)}, u32[]{:S(2)}) collective-permute-start(bf16[2,4,192,384]{3,2,1,0:T(8,128)(2,1)S(1)} %collective-permute-done.21.d1), channel_id=1, source_target_pairs={{0,4},{4,0},{8,12},{12,8},{16,20},{20,16},{24,28},{28,24},{1,5},{5... | collective-permute-start | bytes 3538952 | tf_op jit(solution)/shard_map/ppermute | solution.py:224
  133.6 13.8 %collective-permute-start.24 = (bf16[4,4,96,768]{3,2,1,0:T(8,128)(2,1)}, bf16[4,4,96,768]{3,2,1,0:T(8,128)(2,1)S(1)}, u32[]{:S(2)}, u32[]{:S(2)}) collective-permute-start(bf16[4,4,96,768]{3,2,1,0:T(8,128)(2,1)} %get-tuple-element.306), channel_id=1, source_target_pairs={{0,4},{4,0},{8,12},{12,8},{16,20},{20,16},{24,28},{28,24},{1,5},{5... | collective-permute-start | bytes 7077896 | tf_op jit(solution)/shard_map/ppermute | solution.py:224
  133.7 13.7 %copy-start.3 = (bf16[4,4,96,768]{3,2,1,0:T(8,128)(2,1)S(1)}, bf16[4,4,96,768]{3,2,1,0:T(8,128)(2,1)}, u32[]{:S(2)}) copy-start(bf16[4,4,96,768]{3,2,1,0:T(8,128)(2,1)} %get-tuple-element.297) | copy-start | bytes 7077892
  148.1 16.3 %collective-permute-start.25 = (bf16[2,4,96,768]{3,2,1,0:T(8,128)(2,1)S(1)}, bf16[2,4,96,768]{3,2,1,0:T(8,128)(2,1)S(1)}, u32[]{:S(2)}, u32[]{:S(2)}) collective-permute-start(bf16[2,4,96,768]{3,2,1,0:T(8,128)(2,1)S(1)} %get-tuple-element.317), channel_id=1, source_target_pairs={{0,2},{1,3},{2,0},{3,1},{4,5},{5,4},{6,7},{7,6},{8,10},{9,11},{10,... | collective-permute-start | bytes 3538952 | tf_op jit(solution)/shard_map/ppermute | solution.py:224
  166.0 10.3 %collective-permute-start.27 = (bf16[4,4,96,768]{3,2,1,0:T(8,128)(2,1)S(1)}, bf16[4,4,96,768]{3,2,1,0:T(8,128)(2,1)S(1)}, u32[]{:S(2)}, u32[]{:S(2)}) collective-permute-start(bf16[4,4,96,768]{3,2,1,0:T(8,128)(2,1)S(1)} %copy-done.22), channel_id=1, source_target_pairs={{0,4},{4,0},{8,12},{12,8},{16,20},{20,16},{24,28},{28,24},{1,5},{5... | collective-permute-start | bytes 7077896 | tf_op jit(solution)/shard_map/ppermute | solution.py:224
  166.0 10.3 %collective-permute-start.26 = (bf16[1,4,96,768]{3,2,1,0:T(8,128)(2,1)S(1)}, bf16[1,4,96,768]{3,2,1,0:T(8,128)(2,1)S(1)}, u32[]{:S(2)}, u32[]{:S(2)}) collective-permute-start(bf16[1,4,96,768]{3,2,1,0:T(8,128)(2,1)S(1)} %get-tuple-element.323), channel_id=1, source_target_pairs={{0,1},{1,0},{2,3},{3,2},{4,6},{5,7},{6,4},{7,5},{8,9},{9,8},{10,11... | collective-permute-start | bytes 1769480 | tf_op jit(solution)/shard_map/ppermute | solution.py:224
  166.5 9.9 %copy-start.4 = (bf16[4,4,96,768]{3,2,1,0:T(8,128)(2,1)S(1)}, bf16[4,4,96,768]{3,2,1,0:T(8,128)(2,1)}, u32[]{:S(2)}) copy-start(bf16[4,4,96,768]{3,2,1,0:T(8,128)(2,1)} %get-tuple-element.313) | copy-start | bytes 7077892
  177.1 16.3 %collective-permute-start.28 = (bf16[2,4,96,768]{3,2,1,0:T(8,128)(2,1)S(1)}, bf16[2,4,96,768]{3,2,1,0:T(8,128)(2,1)S(1)}, u32[]{:S(2)}, u32[]{:S(2)}) collective-permute-start(bf16[2,4,96,768]{3,2,1,0:T(8,128)(2,1)S(1)} %get-tuple-element.338), channel_id=1, source_target_pairs={{0,2},{1,3},{2,0},{3,1},{4,5},{5,4},{6,7},{7,6},{8,10},{9,11},{10,... | collective-permute-start | bytes 3538952 | tf_op jit(solution)/shard_map/ppermute | solution.py:224
  193.7 10.9 %collective-permute-start.30 = (bf16[1,4,96,768]{3,2,1,0:T(8,128)(2,1)S(1)}, bf16[1,4,96,768]{3,2,1,0:T(8,128)(2,1)S(1)}, u32[]{:S(2)}, u32[]{:S(2)}) collective-permute-start(bf16[1,4,96,768]{3,2,1,0:T(8,128)(2,1)S(1)} %get-tuple-element.346), channel_id=1, source_target_pairs={{0,1},{1,0},{2,3},{3,2},{4,6},{5,7},{6,4},{7,5},{8,9},{9,8},{10,11... | collective-permute-start | bytes 1769480 | tf_op jit(solution)/shard_map/ppermute | solution.py:224
  195.3 9.3 %collective-permute-start.29 = (bf16[4,112,768]{2,1,0:T(8,128)(2,1)S(1)}, bf16[4,112,768]{2,1,0:T(8,128)(2,1)S(1)}, u32[]{:S(2)}, u32[]{:S(2)}) collective-permute-start(bf16[4,112,768]{2,1,0:T(8,128)(2,1)S(1)} %copy-done.24), channel_id=1, source_target_pairs={{0,4},{4,0},{8,12},{12,8},{16,20},{20,16},{24,28},{28,24},{1,5},{5... | collective-permute-start | bytes 2064392 | tf_op jit(solution)/shard_map/ppermute | solution.py:224
  195.3 9.3 %copy-start.9 = (bf16[4,112,768]{2,1,0:T(8,128)(2,1)S(1)}, bf16[4,112,768]{2,1,0:T(8,128)(2,1)}, u32[]{:S(2)}) copy-start(bf16[4,112,768]{2,1,0:T(8,128)(2,1)} %get-tuple-element.336) | copy-start | bytes 2064388
  205.0 15.1 %collective-permute-start.32 = (bf16[192,768]{1,0:T(8,128)(2,1)S(1)}, bf16[192,768]{1,0:T(8,128)(2,1)S(1)}, u32[]{:S(2)}, u32[]{:S(2)}) collective-permute-start(bf16[192,768]{1,0:T(8,128)(2,1)S(1)} %pad_maximum_fusion.2), channel_id=1, source_target_pairs={{0,24},{4,28},{8,0},{12,4},{16,8},{20,12},{24,16},{28,20},{1,25},{... | collective-permute-start | bytes 884744 | tf_op jit(solution)/shard_map/ppermute | solution.py:224
  209.4 10.9 %collective-permute-start.31 = (bf16[4,112,768]{2,1,0:T(8,128)(2,1)S(1)}, bf16[4,112,768]{2,1,0:T(8,128)(2,1)S(1)}, u32[]{:S(2)}, u32[]{:S(2)}) collective-permute-start(bf16[4,112,768]{2,1,0:T(8,128)(2,1)S(1)} %add_convert_fusion.6), channel_id=1, source_target_pairs={{0,1},{1,0},{2,3},{3,2},{4,6},{5,7},{6,4},{7,5},{8,9},{9,8},{10,11... | collective-permute-start | bytes 2064392 | tf_op jit(solution)/shard_map/ppermute | solution.py:224
  210.1 10.2 %collective-permute-start.33 = (bf16[4,112,768]{2,1,0:T(8,128)(2,1)S(1)}, bf16[4,112,768]{2,1,0:T(8,128)(2,1)S(1)}, u32[]{:S(2)}, u32[]{:S(2)}) collective-permute-start(bf16[4,112,768]{2,1,0:T(8,128)(2,1)S(1)} %copy-done.23), channel_id=1, source_target_pairs={{0,4},{4,0},{8,12},{12,8},{16,20},{20,16},{24,28},{28,24},{1,5},{5... | collective-permute-start | bytes 2064392 | tf_op jit(solution)/shard_map/ppermute | solution.py:224
  220.4 2.4 collective-permute-start.34
  224.4 21.2 %collective-permute-start.37 = (bf16[192,768]{1,0:T(8,128)(2,1)S(1)}, bf16[192,768]{1,0:T(8,128)(2,1)S(1)}, u32[]{:S(2)}, u32[]{:S(2)}) collective-permute-start(bf16[192,768]{1,0:T(8,128)(2,1)S(1)} %pad_maximum_fusion.3), channel_id=1, source_target_pairs={{0,16},{4,20},{8,24},{12,28},{16,0},{20,4},{24,8},{28,12},{1,17},{... | collective-permute-start | bytes 884744 | tf_op jit(solution)/shard_map/ppermute | solution.py:224
  225.0 20.7 %collective-permute-start.38 = (bf16[192,768]{1,0:T(8,128)(2,1)S(1)}, bf16[192,768]{1,0:T(8,128)(2,1)S(1)}, u32[]{:S(2)}, u32[]{:S(2)}) collective-permute-start(bf16[192,768]{1,0:T(8,128)(2,1)S(1)} %pad_maximum_fusion.4), channel_id=1, source_target_pairs={{0,8},{4,12},{8,16},{12,20},{16,24},{20,28},{24,0},{28,4},{1,9},{5... | collective-permute-start | bytes 884744 | tf_op jit(solution)/shard_map/ppermute | solution.py:224
  225.3 20.3 %collective-permute-start.35 = (bf16[4,112,768]{2,1,0:T(8,128)(2,1)S(1)}, bf16[4,112,768]{2,1,0:T(8,128)(2,1)S(1)}, u32[]{:S(2)}, u32[]{:S(2)}) collective-permute-start(bf16[4,112,768]{2,1,0:T(8,128)(2,1)S(1)} %get-tuple-element.368), channel_id=1, source_target_pairs={{0,1},{1,0},{2,3},{3,2},{4,5},{5,4},{6,7},{7,6},{8,9},{9,8},{10,11... | collective-permute-start | bytes 2064392 | tf_op jit(solution)/shard_map/ppermute | solution.py:224
  226.0 19.6 %collective-permute-start.36 = (bf16[4,112,768]{2,1,0:T(8,128)(2,1)S(1)}, bf16[4,112,768]{2,1,0:T(8,128)(2,1)S(1)}, u32[]{:S(2)}, u32[]{:S(2)}) collective-permute-start(bf16[4,112,768]{2,1,0:T(8,128)(2,1)S(1)} %get-tuple-element.369), channel_id=1, source_target_pairs={{0,2},{1,3},{2,0},{3,1},{4,6},{5,7},{6,4},{7,5},{8,10},{9,11},{10,... | collective-permute-start | bytes 2064392 | tf_op jit(solution)/shard_map/ppermute | solution.py:224
  245.7 2.4 collective-permute-start.39
  252.3 13.6 %collective-permute-start.40 = (bf16[112,768]{1,0:T(8,128)(2,1)}, bf16[112,768]{1,0:T(8,128)(2,1)S(1)}, u32[]{:S(2)}, u32[]{:S(2)}) collective-permute-start(bf16[112,768]{1,0:T(8,128)(2,1)} %get-tuple-element.387), channel_id=1, source_target_pairs={{0,24},{4,28},{8,0},{12,4},{16,8},{20,12},{24,16},{28,20},{1,25},{... | collective-permute-start | bytes 516104 | tf_op jit(solution)/shard_map/ppermute | solution.py:224
  253.1 16.3 %collective-permute-start.41 = (bf16[112,768]{1,0:T(8,128)(2,1)}, bf16[112,768]{1,0:T(8,128)(2,1)S(1)}, u32[]{:S(2)}, u32[]{:S(2)}) collective-permute-start(bf16[112,768]{1,0:T(8,128)(2,1)} %get-tuple-element.388), channel_id=1, source_target_pairs={{0,16},{4,20},{8,24},{12,28},{16,0},{20,4},{24,8},{28,12},{1,17},{... | collective-permute-start | bytes 516104 | tf_op jit(solution)/shard_map/ppermute | solution.py:224
  253.8 15.7 %collective-permute-start.42 = (bf16[112,768]{1,0:T(8,128)(2,1)}, bf16[112,768]{1,0:T(8,128)(2,1)S(1)}, u32[]{:S(2)}, u32[]{:S(2)}) collective-permute-start(bf16[112,768]{1,0:T(8,128)(2,1)} %get-tuple-element.389), channel_id=1, source_target_pairs={{0,8},{4,12},{8,16},{12,20},{16,24},{20,28},{24,0},{28,4},{1,9},{5... | collective-permute-start | bytes 516104 | tf_op jit(solution)/shard_map/ppermute | solution.py:224
  (20 other events, 44.2 us)

commit v2 on v1

--- a/solution.py
+++ b/solution.py
@@ -140,18 +140,20 @@
 
     def stage(self):
         bits = axis_facts()[3]
+        if self.round < bits - 1:
+            return [(self.held, ("dp", "fsdp"), along_bit(self.round))]
         if self.round < bits:
-            return [(self.held, ("dp", "fsdp"), along_bit(self.round))]
-        return [(v, "dp", across_cores()) for v in self.own]
+            return [(self.held, ("dp", "fsdp"), along_bit(self.round)), (self.held, "dp", across_cores())]
+        return [(self.own[1], "dp", across_cores())]
 
     def take(self, got):
         bits = axis_facts()[3]
         if self.round < bits - 1:
             self.held = jnp.concatenate([self.held] + got)
         elif self.round < bits:
-            self.own = [self.held] + got
+            self.own, self.other = [self.held, got[0]], got[1]
         else:
-            self.blocks = self.own + got
+            self.blocks = self.own + [self.other] + got
         self.round += 1
 
     def done(self):
@@ -497,10 +499,16 @@
 
 def total_kernel(place, *refs):
     parts, first, others = refs[:4], refs[4], refs[5:]
-    depth = parts[0].shape[0]
+    depth = 1 + len(others)
+    tall = (parts[0].shape[0] - 16) // depth
+
+    def summed(rows):
+        return sum((part[rows, :].astype(f32) for part in parts[1:]), parts[0][rows, :].astype(f32))
+
+    below = summed(pl.ds(depth * tall, 16))
     for s in range(depth):
         z = row_of(place, 0, s, depth) // 2
-        total = sum((part[z].astype(f32) for part in parts[1:]), parts[0][z].astype(f32))
+        total = jnp.concatenate([summed(pl.ds(pl.multiple_of(z * tall, 16), tall)), below])
         if s:
             others[s - 1][...] = total.astype(bf16)
         else:
@@ -508,8 +516,9 @@
 
 
 def make_total(place, parts):
-    depth, height, width = parts[0].shape
-    out = (height, width)
+    depth = axis_facts()[2]
+    height, width = parts[0].shape
+    out = ((height - 16) // depth + 16, width)
     return call(
         total_kernel, "total", (1,), [whole(parts[0].shape)] * 4, [whole(out)] * depth,
         [sds(out, f32)] + [sds(out, bf16)] * (depth - 1), prefetch=1, cost=guess(1e6, 4e6), limit=SMALL,
@@ -692,12 +701,12 @@
 
 
 def attend_back_one_kernel(
-    away, place, x_t_far, kept, grad_context, lse, delta, gow_far, inner, outer, gub, queries_ext, keys_ext,
+    away, depth, place, x_t_far, kept, grad_context, lse, delta, gow_far, inner, outer, gub, queries_ext, keys_ext,
     send, keep, grads_out,
     grads, found, sums, x_t, gow, sems,
 ):
-    depth, height, width = send.shape
-    tall = height - 16
+    height, width = send.shape
+    tall = (height - 16) // depth
     step, steps = pl.program_id(0), pl.num_programs(0)
     fsdp = w_out_fsdp(place, depth)
     core, j = core_of(place, depth, fsdp), neighbour_of(place, away, depth, fsdp)
@@ -770,8 +779,8 @@
         for n, target in ((1, send), (0, keep)):
             for z in range(depth):
                 i = 2 * z + lax.rem(core + n, 2)
-                target[z, :tall, :] = found[pl.ds(pl.multiple_of(i * tall, 16), tall), :]
-                target[z, tall:, :] = below
+                target[z * tall:(z + 1) * tall, :] = found[pl.ds(pl.multiple_of(i * tall, 16), tall), :]
+            target[depth * tall:, :] = below
 
 
 def attend_back_one(
@@ -782,10 +791,10 @@
     j = lambda place: neighbour_of(place, away, depth, fsdp)
     any_space = pl.BlockSpec(memory_space=pl.ANY)
     small = lambda *shape: pl.BlockSpec((1, *shape), lambda s, place, *_: (j(place), 0, 0))
-    sent = (depth, tall + 16, width)
+    sent = (depth * tall + 16, width)
     rows = pl.BlockSpec((PLEN, USED), lambda s, *_: (s, 0))
     return call(
-        functools.partial(attend_back_one_kernel, away), "attend_back", (t // PLEN,),
+        functools.partial(attend_back_one_kernel, away, depth), "attend_back", (t // PLEN,),
         [any_space, rows, pl.BlockSpec((1, PLEN, narrow), lambda s, place, *_: (j(place), s, 0)),
          pl.BlockSpec((8, PLEN), lambda s, *_: (0, s)),
          pl.BlockSpec((1, 8, PLEN), lambda s, place, *_: (j(place), 0, s)), any_space,
@@ -980,41 +989,19 @@
     up_tiles(low[rows, :], uw, slabs, act_out, slope_out)
 
 
-def up_rest_kernel(place, low, slabs, uw, act_in, slope_in, act_out, slope_out):
-    rows = pl.ds(pl.multiple_of(pl.program_id(0) * ROWS, ROWS), ROWS)
-    up_tiles(low[rows, :], uw, slabs, act_out, slope_out)
-
-
 def up(place, low, slabs, blocks):
     t, d = low.shape
     half, depth, tall, wide = blocks[0].shape
     f = 2 * half
-    high = pl.BlockSpec((half, ROWS, wide), lambda r, *_: (0, r, 0))
+    high = pl.BlockSpec((f, ROWS, wide), lambda r, *_: (0, r, 0))
     return call(
         up_kernel, "up", (t // ROWS,),
-        [held(), whole((half, 16, wide))] + [pl.BlockSpec(memory_space=pl.ANY)] * 4,
+        [held(), whole((f, 16, wide))] + [pl.BlockSpec(memory_space=pl.ANY)] * 4,
         [high, high, whole((f, depth, 2, tall, wide))],
         [sds((f, t, wide), bf16), sds((f, t, wide), bf16), sds((f, depth, 2, tall, wide), bf16)],
         [pltpu.SemaphoreType.DMA((2 * f,))],
-        prefetch=1, cost=guess(6e9, 20e6), limit=SMALL, free=pl.ANY,
+        prefetch=1, cost=guess(12e9, 30e6), limit=SMALL, free=pl.ANY,
     )(place, low, slabs, *blocks)
-
-
-def up_rest(place, low, slabs, uw, act, slope):
-    t, d = low.shape
-    f, depth, _, tall, wide = uw.shape
-    half = f // 2
-    high = pl.BlockSpec((half, ROWS, wide), lambda r, *_: (1, r, 0))
-    any_space = pl.BlockSpec(memory_space=pl.ANY)
-    return call(
-        up_rest_kernel, "up_rest", (t // ROWS,),
-        [held(), pl.BlockSpec((half, 16, wide), lambda r, *_: (1, 0, 0)),
-         pl.BlockSpec((half, depth, 2, tall, wide), lambda r, *_: (1, 0, 0, 0, 0)),
-         any_space, any_space],
-        [high, high],
-        [sds((f, t, wide), bf16), sds((f, t, wide), bf16)],
-        prefetch=1, cost=guess(6e9, 16e6), limit=SMALL, aliases={4: 0, 5: 1},
-    )(place, low, slabs, uw, act, slope)
 
 
 def down_kernel(
@@ -1343,7 +1330,6 @@
     )
     finish(to_u)
     active, slope, uw = beside([to_d], up, (place, low, slabs, to_u.blocks))
-    active, slope = beside([to_d], up_rest, (place, low, slabs, uw, active, slope))
     finish(to_d)
     cuts = context.shape[0]
     out, pooled, mixed, branch, down_vectors, send_d, keep_d, dw = down(
@@ -1360,7 +1346,7 @@
         (place, branch, slope, dw, uw, low_t, so_far, shared),
     )
     of_u = Scatter(keep_u, send_u)
-    of_d.joined = of_u.joined = by_head
+    of_u.joined = by_head
     inner, inner_vectors, gow, grad_context, delta = beside(
         [of_d, of_u], functools.partial(inner_back, count, head_of), (grad_normed, n1, r1, given, context, ow),
         key=3, out=2
@@ -1373,14 +1359,12 @@
             args = (place, x_t, kept, grad_context, lse, delta, gow, inner_vectors, down_vectors, gub, q_ext, k_ext)
             return beside(moves, functools.partial(attend_back_one, away, fsdp, depth), args)
 
-        send_3, keep_3, grads_3 = back(3, [of_d, of_u], kept_3, lse_3)
+        send_3, keep_3, grads_3 = back(3, [of_u, of_d], kept_3, lse_3)
         swap_3 = Once([swap(send_3)])
         send_1, keep_1, grads_1 = back(1, [swap_3, of_u], kept_1, lse_1)
         corner = Once([(add(keep_3, swap_3.got[0]), ("dp", "fsdp"), along_bit(0))])
-        both = [
-            (jnp.concatenate([u, v]), "dp", along_z(-s - 1)) for s, (u, v) in enumerate(zip(of_u.send, of_d.send))
-        ]
-        near, rest = Once(both[:1]), Once(both[1:])
+        both = [(u, "dp", along_z(-s - 1)) for s, u in enumerate(of_u.send)]
+        near, rest = Once(both[::2]), Once(both[1::2])
         swap_1 = Once([swap(send_1)])
         send_2, keep_2, grads_2 = back(2, [corner, near, swap_1], kept_2, lse_2)
         swap_2 = Once([swap(send_2)])
@@ -1401,8 +1385,7 @@
         *made, gqb, gvb, gob, gg1, gb1, gdb, gg2, gb2, gub = unblock(mine, along.got)
         vectors = (gqb, gvb, gob, gg1, gb1, gdb, gg2, gb2)
         got, input_grad = lax.optimization_barrier((near.got + rest.got, input_grad))
-        sum_u = add_both(of_u.keep, *(v[:tall] for v in got))
-        sum_d = add_both(of_d.keep, *(v[tall:] for v in got))
+        sum_u, sum_d = add_both(of_u.keep, *got), of_d.total
     else:
         gg1, gb1, gob = (inner_vectors[0, n:n + 1] for n in range(3))
         gdb, gg2, gb2 = (down_vectors[0, n:n + 1] for n in range(3))

time: 279 us -> 271 us (0.971)
  waiting for transfers between devices: 42.2 us -> 33.2 us
  starting transfers between devices: 43 us -> 48.9 us
  Pallas kernels: 173 us -> 169 us
    ppermute x42 -> x45, waiting for transfers between devices: 42.2 us -> 33.2 us  [beside(): lax.ppermute(v, axis, perm)]
    ppermute x42 -> x45, starting transfers between devices: 43 us -> 48.4 us  [beside(): lax.ppermute(v, axis, perm)]
    pallas_call x21 -> x20, Pallas kernels: 173 us -> 169 us  [run_far(): return run(*args[:prefetch], *given)]
  transfers between devices with their start and end apart: 43 -> 46, of which waited for: 14 -> 14; matrix products, arithmetic and copies ran while one was open for 1% -> 1% of each run, Pallas kernels for 52% -> 51%
where the time goes in v2:
time: 271 us; the launch traced here: 266 us
  Pallas kernels  169 us (62%)
  starting transfers between devices  48.9 us (18%)
  waiting for transfers between devices  33.2 us (12%)
  local copies, waits for them, and re-layouts  7.24 us (3%)
  other arithmetic  6.05 us (2%)
    pallas_call x20, Pallas kernels, run_far(): return run(*args[:prefetch], *given)  169 us
    ppermute x45, starting transfers between devices, beside(): lax.ppermute(v, axis, perm)  48.4 us
    ppermute x45, waiting for transfers between devices, beside(): lax.ppermute(v, axis, perm)  33.2 us
  transfers between devices with their start and end apart: 46, of which 14 were waited for; matrix products, arithmetic and copies ran while one was open for 1% of the time, Pallas kernels for 51%

profile of v2, /device:TPU:0, one launch (start us, length us, event | category | flops | bytes accessed | tf_op | source)
XLA Modules:
  0.0 266.3 jit_solution(4461993510563253785)
XLA Ops:
  0.7 1.7 block.1
  2.4 3.0 %collective-permute-start = (bf16[96,768]{1,0:T(8,128)(2,1)}, bf16[96,768]{1,0:T(8,128)(2,1)S(1)}, u32[]{:S(2)}, u32[]{:S(2)}) collective-permute-start(bf16[96,768]{1,0:T(8,128)(2,1)} %get-tuple-element.219.refs_0_), channel_id=1, source_target_pairs={{0,8},{4,12},{8,16},{12,20},{16,24},{20,28},{24,0},{28,4},{1,9},{5... | collective-permute-start | bytes 442376 | tf_op jit(solution)/shard_map/ppermute | solution.py:226
  5.4 2.6 collective-permute-start.1
  8.0 1.3 collective-permute-start.2
  9.4 2.6 copy.49
  12.4 5.5 %collective-permute-done.1.refs_2_ = bf16[96,768]{1,0:T(8,128)(2,1)S(1)} collective-permute-done((bf16[96,768]{1,0:T(8,128)(2,1)}, bf16[96,768]{1,0:T(8,128)(2,1)S(1)}, u32[]{:S(2)}, u32[]{:S(2)}) %collective-permute-start.1) | collective-permute-done | bytes 147488 | tf_op jit(solution)/shard_map/ppermute | solution.py:226
  18.6 2.5 line_up_rows.1.own
  21.1 1.5 collective-permute-start.4
  22.6 1.5 collective-permute-start.5
  24.8 3.6 %collective-permute-start.6 = (bf16[96,768]{1,0:T(8,128)(2,1)S(1)}, bf16[96,768]{1,0:T(8,128)(2,1)S(1)}, u32[]{:S(2)}, u32[]{:S(2)}) collective-permute-start(bf16[96,768]{1,0:T(8,128)(2,1)S(1)} %copy-done.18), channel_id=1, source_target_pairs={{0,8},{4,12},{8,16},{12,20},{16,24},{20,28},{24,0},{28,4},{1,9},{5... | collective-permute-start | bytes 442376 | tf_op jit(solution)/shard_map/ppermute | solution.py:226
  28.5 1.7 collective-permute-start.7
  32.0 8.0 %attend.4 = (bf16[4,1024,192]{2,1,0:T(8,128)(2,1)}, bf16[4,4,2,96,768]{4,3,2,1,0:T(8,128)(2,1)}, bf16[4,16,768]{2,1,0:T(8,128)(2,1)}, bf16[1024,640]{1,0:T(8,128...) custom-call(s32[29]{0:T(128)S(1)} %concatenate.12.place, ...), custom_call_target="tpu_custom_call" | custom-call | flops 5000000000 | bytes 8000000 | tf_op jit(solution)/shard_map/attend/pallas_call | solution.py:79
  40.8 2.5 line_up.1
  45.5 3.4 %collective-permute-start.13 = (bf16[192,384]{1,0:T(8,128)(2,1)S(1)}, bf16[192,384]{1,0:T(8,128)(2,1)S(1)}, u32[]{:S(2)}, u32[]{:S(2)}) collective-permute-start(bf16[192,384]{1,0:T(8,128)(2,1)S(1)} %bitcast.56), channel_id=1, source_target_pairs={{0,8},{4,12},{8,16},{12,20},{16,24},{20,28},{24,0},{28,4},{1,9},{5... | collective-permute-start | bytes 442376 | tf_op jit(solution)/shard_map/ppermute | solution.py:226
  50.2 1.4 collective-permute-start.15
  51.6 7.4 %attend.5 = (bf16[4,1024,192]{2,1,0:T(8,128)(2,1)}, bf16[4,4,2,96,768]{4,3,2,1,0:T(8,128)(2,1)}, bf16[4,16,768]{2,1,0:T(8,128)(2,1)}, bf16[1024,640]{1,0:T(8,128)(2,1)}, f32[8,1024]{1,0:T(8,128)}) custom-call(s32[29]{0:T(128)S(1)} %concatenate.12.place, s32[1]{0:T(128)S(6)} %copy.62.bucket, ...), custom_call_target="tpu_custom_call", output_to_operand_aliasing={{0}: (8, {}), {1}: (9, {}), {2}: (10, {})} | custom-call | flops 5000000000 | bytes 8000000 | tf_op jit(solution)/shard_map/attend/pallas_call | solution.py:79
  61.5 7.4 %attend.6 = (bf16[4,1024,192]{2,1,0:T(8,128)(2,1)}, bf16[4,4,2,96,768]{4,3,2,1,0:T(8,128)(2,1)}, bf16[4,16,768]{2,1,0:T(8,128)(2,1)}, bf16[1024,640]{1,0:T(8,128)(2,1)}, f32[8,1024]{1,0:T(8,128)}) custom-call(s32[29]{0:T(128)S(1)} %concatenate.12.place, s32[1]{0:T(128)S(6)} %copy.62.bucket, ...), custom_call_target="tpu_custom_call", output_to_operand_aliasing={{0}: (8, {}), {1}: (9, {}), {2}: (10, {})} | custom-call | flops 5000000000 | bytes 8000000 | tf_op jit(solution)/shard_map/attend/pallas_call | solution.py:79
  68.9 7.4 %attend.7 = (bf16[4,1024,192]{2,1,0:T(8,128)(2,1)}, bf16[4,4,2,96,768]{4,3,2,1,0:T(8,128)(2,1)}, bf16[4,16,768]{2,1,0:T(8,128)(2,1)}, bf16[1024,640]{1,0:T(8,128)(2,1)}, f32[8,1024]{1,0:T(8,128)}) custom-call(s32[29]{0:T(128)S(1)} %concatenate.12.place, s32[1]{0:T(128)S(6)} %copy.62.bucket, ...), custom_call_target="tpu_custom_call", output_to_operand_aliasing={{0}: (8, {}), {1}: (9, {}), {2}: (10, {})} | custom-call | flops 5000000000 | bytes 8000000 | tf_op jit(solution)/shard_map/attend/pallas_call | solution.py:79
  77.0 5.7 %attended.1 = (f32[1024,768]{1,0:T(8,128)S(1)}, f32[1024,128]{1,0:T(8,128)S(1)}, bf16[1024,768]{1,0:T(8,128)(2,1)S(1)}, bf16[768,1024]{1,0:T(8,128)(2,1)S(1)}, b...) custom-call(bf16[1024,768]{1,0:T(8,128)(2,1)} %x.9, bf16[4,1024,192]{2,1,0:T(8,128)(2,1)} %get-tuple-element.264.context, ...), custom_call_target="tpu_custom_call" | custom-call | flops 3000000000 | bytes 10000000 | tf_op jit(solution)/shard_map/attended/pallas_call | solution.py:79
  82.8 3.6 %collective-permute-done.20 = bf16[1,4,192,384]{3,2,1,0:T(8,128)(2,1)S(1)} collective-permute-done((bf16[1,4,192,384]{3,2,1,0:T(8,128)(2,1)S(1)}, bf16[1,4,192,384]{3,2,1,0:T(8,128)(2,1)S(1)}, u32[]{:S(2)}, u32[]{:S(2)}) %collective-permute-start.20) | collective-permute-done | bytes 589856 | tf_op jit(solution)/shard_map/ppermute | solution.py:226
  87.8 13.6 %up.1 = (bf16[4,1024,768]{2,1,0:T(8,128)(2,1)}, bf16[4,1024,768]{2,1,0:T(8,128)(2,1)}, bf16[4,4,2,96,768]{4,3,2,1,0:T(8,128)(2,1)}) custom-call(s32[29]{0:T(128)S(1)} %concatenate.12.place, bf16[1024,768]{1,0:T(8,128)(2,1)S(1)} %get-tuple-element.277.low, bf16[4,16,768]{2,1,0:T(8,128)(2,1)} %get-tuple-element.271.slabs, ...), custom_call_target="tpu_custom_call" | custom-call | flops 12000000000 | bytes 30000000 | tf_op jit(solution)/shard_map/up/pallas_call | solution.py:79
  101.4 1.4 collective-permute-done.21.d1
  102.8 2.8 %collective-permute-done.23.d3 = bf16[2,4,192,384]{3,2,1,0:T(8,128)(2,1)S(1)} collective-permute-done((bf16[2,4,192,384]{3,2,1,0:T(8,128)(2,1)S(1)}, bf16[2,4,192,384]{3,2,1,0:T(8,128)(2,1)S(1)}, u32[]{:S(2)}, u32[]{:S(2)}) %collective-permute-start.23) | collective-permute-done | bytes 1179680 | tf_op jit(solution)/shard_map/ppermute | solution.py:226
  105.6 22.2 %down.1 = (bf16[1024,768]{1,0:T(8,128)(2,1)}, f32[8,768]{1,0:T(8,128)}, f32[1024,768]{1,0:T(8,128)S(1)}, bf16[1024,768]{1,0:T(8,128)(2,1)S(1)}, f32[4,8,192]{2,1...) custom-call(s32[29]{0:T(128)S(1)} %concatenate.12.place, ...), custom_call_target="tpu_custom_call" | custom-call | flops 12000000000 | bytes 35000000 | tf_op jit(solution)/shard_map/down/pallas_call | solution.py:79
  128.0 13.7 %feed_back.2 = (bf16[4,4,96,768]{3,2,1,0:T(8,128)(2,1)}, bf16[4,4,96,768]{3,2,1,0:T(8,128)(2,1)}, f32[4,1,768]{2,1,0:T(1,128)}, f32[1024,768]{1,0:T(8,128)S(1)}) custom-call(s32[29]{0:T(128)S(1)} %concatenate.12.place, bf16[1024,768]{1,0:T(8,128)(2,1)S(1)} %get-tuple-element.293.branch, bf16[4,1024,768]{2,1,0:T(8,128)(2,1)} %get-tuple-element.294.slope, ...), custom_call_target="tpu_custom_call" | custom-call | flops 15000000512 | bytes 35000000 | tf_op jit(solution)/shard_map/feed_back/pallas_call | solution.py:79
  143.6 13.5 %feed_back.3 = (bf16[4,4,96,768]{3,2,1,0:T(8,128)(2,1)}, bf16[4,4,96,768]{3,2,1,0:T(8,128)(2,1)}, f32[4,1,768]{2,1,0:T(1,128)}, f32[1024,768]{1,0:T(8,128)S(1)}) custom-call(s32[29]{0:T(128)S(1)} %concatenate.12.place, bf16[1024,768]{1,0:T(8,128)(2,1)S(1)} %get-tuple-element.293.branch, ...), custom_call_target="tpu_custom_call", output_to_operand_aliasing={{0}: (7, {}), {1}: (8, {}), {2}: (9, {})} | custom-call | flops 15000000512 | bytes 35000000 | tf_op jit(solution)/shard_map/feed_back/pallas_call | solution.py:79
  157.1 1.5 collective-permute-done.25
  158.9 1.4 copy-done.22
  160.8 9.8 %inner_back.1 = (f32[1024,768]{1,0:T(8,128)}, f32[4,8,192]{2,1,0:T(8,128)}, bf16[4,768,192]{2,1,0:T(8,128)(2,1)}, bf16[4,1024,192]{2,1,0:T(8,128)(2,1)}, f32[32,1024]{1,0:T(8,128)}) custom-call(f32[1024,768]{1,0:T(8,128)S(1)} %get-tuple-element.308.grad_normed, f32[1024,768]{1,0:T(8,128)S(1)} %get-tuple-element.284.n1, ...), custom_call_target="tpu_custom_call" | custom-call | flops 4000000000 | bytes 10000000 | tf_op jit(solution)/shard_map/inner_back/pallas_call | solution.py:79
  172.7 4.3 %collective-permute-start.29 = (bf16[96,768]{1,0:T(8,128)(2,1)S(1)}, bf16[96,768]{1,0:T(8,128)(2,1)S(1)}, u32[]{:S(2)}, u32[]{:S(2)}) collective-permute-start(bf16[96,768]{1,0:T(8,128)(2,1)S(1)} %get-tuple-element.334), channel_id=1, source_target_pairs={{0,24},{4,28},{8,0},{12,4},{16,8},{20,12},{24,16},{28,20},{1,25},{... | collective-permute-start | bytes 442376 | tf_op jit(solution)/shard_map/ppermute | solution.py:226
  177.7 9.2 %attend_back.4 = (bf16[400,768]{1,0:T(8,128)(2,1)}, bf16[400,768]{1,0:T(8,128)(2,1)}, bf16[1024,640]{1,0:T(8,128)(2,1)}) custom-call(s32[29]{0:T(128)S(1)} %concatenate.12.place, bf16[768,1024]{1,0:T(8,128)(2,1)} %bitcast.52, bf16[1024,640]{1,0:T(8,128)(2,1)} %get-tuple-element.323.kept, bf16[4,1024,192]{2,1,0:T(8,128)(2,1)} %get-tuple-element.324.grad_context, ...), custom_call_target="tpu_custom_call" | custom-call | flops 10000000000 | bytes 12000000 | tf_op jit(solution)/shard_map/attend_back/pallas_call | solution.py:79
  187.0 3.9 %collective-permute-done.30 = bf16[96,768]{1,0:T(8,128)(2,1)S(1)} collective-permute-done((bf16[96,768]{1,0:T(8,128)(2,1)S(1)}, bf16[96,768]{1,0:T(8,128)(2,1)S(1)}, u32[]{:S(2)}, u32[]{:S(2)}) %collective-permute-start.30) | collective-permute-done | bytes 147488 | tf_op jit(solution)/shard_map/ppermute | solution.py:226
  191.2 1.5 collective-permute-start.33
  192.7 9.3 %attend_back.5 = (bf16[400,768]{1,0:T(8,128)(2,1)}, bf16[400,768]{1,0:T(8,128)(2,1)}, bf16[1024,640]{1,0:T(8,128)(2,1)}) custom-call(s32[29]{0:T(128)S(1)} %concatenate.12.place, bf16[768,1024]{1,0:T(8,128)(2,1)} %bitcast.53, bf16[1024,640]{1,0:T(8,128)(2,1)} %get-tuple-element.340.kept, bf16[4,1024,192]{2,1,0:T(8,128)(2,1)} %get-tuple-element.324.grad_context, ...), custom_call_target="tpu_custom_call" | custom-call | flops 10000000000 | bytes 12000000 | tf_op jit(solution)/shard_map/attend_back/pallas_call | solution.py:79
  202.3 1.8 collective-permute-start.35
  205.0 9.5 %attend_back.6 = (bf16[400,768]{1,0:T(8,128)(2,1)}, bf16[400,768]{1,0:T(8,128)(2,1)}, bf16[1024,640]{1,0:T(8,128)(2,1)}) custom-call(s32[29]{0:T(128)S(1)} %concatenate.12.place, bf16[768,1024]{1,0:T(8,128)(2,1)} %bitcast.54, bf16[1024,640]{1,0:T(8,128)(2,1)} %get-tuple-element.349.kept, bf16[4,1024,192]{2,1,0:T(8,128)(2,1)} %get-tuple-element.324.grad_context, ...), custom_call_target="tpu_custom_call" | custom-call | flops 10000000000 | bytes 12000000 | tf_op jit(solution)/shard_map/attend_back/pallas_call | solution.py:79
  215.1 1.9 collective-permute-done.38
  217.0 1.6 add_convert_fusion.4
  218.6 1.7 collective-permute-start.41
  222.8 9.2 %attend_back.7 = (bf16[400,768]{1,0:T(8,128)(2,1)}, bf16[400,768]{1,0:T(8,128)(2,1)}, bf16[1024,640]{1,0:T(8,128)(2,1)}) custom-call(s32[29]{0:T(128)S(1)} %concatenate.12.place, bf16[768,1024]{1,0:T(8,128)(2,1)} %bitcast.55, bf16[1024,640]{1,0:T(8,128)(2,1)} %get-tuple-element.364.kept, bf16[4,1024,192]{2,1,0:T(8,128)(2,1)} %get-tuple-element.324.grad_context, ...), custom_call_target="tpu_custom_call" | custom-call | flops 10000000000 | bytes 12000000 | tf_op jit(solution)/shard_map/attend_back/pallas_call | solution.py:79
  232.0 4.0 %collective-permute-done.39.refs_2_ = bf16[400,768]{1,0:T(8,128)(2,1)S(1)} collective-permute-done((bf16[400,768]{1,0:T(8,128)(2,1)S(1)}, bf16[400,768]{1,0:T(8,128)(2,1)S(1)}, u32[]{:S(2)}, u32[]{:S(2)}) %collective-permute-start.39) | collective-permute-done | bytes 614432 | tf_op jit(solution)/shard_map/ppermute | solution.py:226
  238.0 1.3 collective-permute-done.42.refs_1_
  240.2 3.2 %total.1 = (f32[112,768]{1,0:T(8,128)}, bf16[112,768]{1,0:T(8,128)(2,1)}, bf16[112,768]{1,0:T(8,128)(2,1)}, bf16[112,768]{1,0:T(8,128)(2,1)}) custom-call(s32[29]{0:T(128)S(1)} %concatenate.12.place, bf16[400,768]{1,0:T(8,128)(2,1)} %get-tuple-element.371.refs_0_, bf16[400,768]{1,0:T(8,128)(2,1)} %copy-done.10, bf16[400,768]{1,0:T(8,128)(2,1)} %copy-done.8, ...), custom_call_target="tpu_custom_call" | custom-call | flops 1000000 | bytes 4000000 | tf_op jit(solution)/shard_map/total/pallas_call | solution.py:79
  243.4 2.4 collective-permute-start.43
  245.8 1.7 collective-permute-start.44
  247.4 10.7 %input_grad.1 = f32[1024,768]{1,0:T(8,128)} custom-call(s32[29]{0:T(128)S(1)} %concatenate.12.place, f32[1024,768]{1,0:T(8,128)} %get-tuple-element.379.inner, bf16[1024,640]{1,0:T(8,128)(2,1)} %get-tuple-element.380.refs_0_, bf16[1024,640]{1,0:T(8,128)(2,1)} %get-tuple-element.381.refs_1_, bf16[1024,640]{1,0:T(8,128)(2,1)} %get-tuple-element.382.refs_2_, ...), custom_call_target="tpu_custom_call" | custom-call | flops 5000000000 | bytes 15000000 | tf_op jit(solution)/shard_map/input_grad/pallas_call | solution.py:79
  258.2 4.9 %collective-permute-done.44.refs_1_ = bf16[112,768]{1,0:T(8,128)(2,1)S(1)} collective-permute-done((bf16[112,768]{1,0:T(8,128)(2,1)}, bf16[112,768]{1,0:T(8,128)(2,1)S(1)}, u32[]{:S(2)}, u32[]{:S(2)}) %collective-permute-start.44) | collective-permute-done | bytes 172064 | tf_op jit(solution)/shard_map/ppermute | solution.py:226
  263.9 2.1 unblock.1
  (135 shorter events, 25.5 us)
Async XLA Ops:
  2.4 10.0 %collective-permute-start = (bf16[96,768]{1,0:T(8,128)(2,1)}, bf16[96,768]{1,0:T(8,128)(2,1)S(1)}, u32[]{:S(2)}, u32[]{:S(2)}) collective-permute-start(bf16[96,768]{1,0:T(8,128)(2,1)} %get-tuple-element.219.refs_0_), channel_id=1, source_target_pairs={{0,8},{4,12},{8,16},{12,20},{16,24},{20,28},{24,0},{28,4},{1,9},{5... | collective-permute-start | bytes 442376 | tf_op jit(solution)/shard_map/ppermute | solution.py:226
  5.4 12.5 %collective-permute-start.1 = (bf16[96,768]{1,0:T(8,128)(2,1)}, bf16[96,768]{1,0:T(8,128)(2,1)S(1)}, u32[]{:S(2)}, u32[]{:S(2)}) collective-permute-start(bf16[96,768]{1,0:T(8,128)(2,1)} %get-tuple-element.219.refs_0_), channel_id=1, source_target_pairs={{0,16},{4,20},{8,24},{12,28},{16,0},{20,4},{24,8},{28,12},{1,17},{... | collective-permute-start | bytes 442376 | tf_op jit(solution)/shard_map/ppermute | solution.py:226
  8.0 9.9 %collective-permute-start.2 = (bf16[96,768]{1,0:T(8,128)(2,1)}, bf16[96,768]{1,0:T(8,128)(2,1)S(1)}, u32[]{:S(2)}, u32[]{:S(2)}) collective-permute-start(bf16[96,768]{1,0:T(8,128)(2,1)} %get-tuple-element.219.refs_0_), channel_id=1, source_target_pairs={{0,24},{4,28},{8,0},{12,4},{16,8},{20,12},{24,16},{28,20},{1,25},{... | collective-permute-start | bytes 442376 | tf_op jit(solution)/shard_map/ppermute | solution.py:226
  12.0 18.9 %copy-start.1 = (s32[1,8]{1,0:T(1,128)S(1)}, s32[1,8]{1,0:T(1,128)}, u32[]{:S(2)}) copy-start(s32[1,8]{1,0:T(1,128)} %param.21) | copy-start | bytes 100
  21.1 9.0 %collective-permute-start.3 = (bf16[400,768]{1,0:T(8,128)(2,1)}, bf16[400,768]{1,0:T(8,128)(2,1)S(1)}, u32[]{:S(2)}, u32[]{:S(2)}) collective-permute-start(bf16[400,768]{1,0:T(8,128)(2,1)} %line_up_rows.1.own), channel_id=1, source_target_pairs={{0,4},{4,0},{8,12},{12,8},{16,20},{20,16},{24,28},{28,24},{1,5},{5... | collective-permute-start | bytes 1843208 | tf_op jit(solution)/shard_map/ppermute | solution.py:226
  21.1 19.0 %collective-permute-start.4 = (bf16[400,768]{1,0:T(8,128)(2,1)}, bf16[400,768]{1,0:T(8,128)(2,1)S(1)}, u32[]{:S(2)}, u32[]{:S(2)}) collective-permute-start(bf16[400,768]{1,0:T(8,128)(2,1)} %line_up_rows.1.own), channel_id=1, source_target_pairs={{0,1},{1,0},{2,3},{3,2},{4,5},{5,4},{6,7},{7,6},{8,9},{9,8},{10,11... | collective-permute-start | bytes 1843208 | tf_op jit(solution)/shard_map/ppermute | solution.py:226
  22.6 17.5 %collective-permute-start.5 = (bf16[400,768]{1,0:T(8,128)(2,1)}, bf16[400,768]{1,0:T(8,128)(2,1)S(1)}, u32[]{:S(2)}, u32[]{:S(2)}) collective-permute-start(bf16[400,768]{1,0:T(8,128)(2,1)} %line_up_rows.1.own), channel_id=1, source_target_pairs={{0,2},{1,3},{2,0},{3,1},{4,6},{5,7},{6,4},{7,5},{8,10},{9,11},{10,... | collective-permute-start | bytes 1843208 | tf_op jit(solution)/shard_map/ppermute | solution.py:226
  24.8 15.2 %collective-permute-start.6 = (bf16[96,768]{1,0:T(8,128)(2,1)S(1)}, bf16[96,768]{1,0:T(8,128)(2,1)S(1)}, u32[]{:S(2)}, u32[]{:S(2)}) collective-permute-start(bf16[96,768]{1,0:T(8,128)(2,1)S(1)} %copy-done.18), channel_id=1, source_target_pairs={{0,8},{4,12},{8,16},{12,20},{16,24},{20,28},{24,0},{28,4},{1,9},{5... | collective-permute-start | bytes 442376 | tf_op jit(solution)/shard_map/ppermute | solution.py:226
  28.5 11.6 %collective-permute-start.7 = (bf16[96,768]{1,0:T(8,128)(2,1)S(1)}, bf16[96,768]{1,0:T(8,128)(2,1)S(1)}, u32[]{:S(2)}, u32[]{:S(2)}) collective-permute-start(bf16[96,768]{1,0:T(8,128)(2,1)S(1)} %copy-done.18), channel_id=1, source_target_pairs={{0,16},{4,20},{8,24},{12,28},{16,0},{20,4},{24,8},{28,12},{1,17},{... | collective-permute-start | bytes 442376 | tf_op jit(solution)/shard_map/ppermute | solution.py:226
  30.1 9.9 %collective-permute-start.8 = (bf16[96,768]{1,0:T(8,128)(2,1)S(1)}, bf16[96,768]{1,0:T(8,128)(2,1)S(1)}, u32[]{:S(2)}, u32[]{:S(2)}) collective-permute-start(bf16[96,768]{1,0:T(8,128)(2,1)S(1)} %copy-done.18), channel_id=1, source_target_pairs={{0,24},{4,28},{8,0},{12,4},{16,8},{20,12},{24,16},{28,20},{1,25},{... | collective-permute-start | bytes 442376 | tf_op jit(solution)/shard_map/ppermute | solution.py:226
  40.1 8.8 %collective-permute-start.9 = (bf16[400,768]{1,0:T(8,128)(2,1)S(1)}, bf16[400,768]{1,0:T(8,128)(2,1)S(1)}, u32[]{:S(2)}, u32[]{:S(2)}) collective-permute-start(bf16[400,768]{1,0:T(8,128)(2,1)S(1)} %collective-permute-done.4.own), channel_id=1, source_target_pairs={{0,4},{4,0},{8,12},{12,8},{16,20},{20,16},{24,28},{28,24},{1,5},{5... | collective-permute-start | bytes 1843208 | tf_op jit(solution)/shard_map/ppermute | solution.py:226
  40.2 10.0 %collective-permute-start.10 = (bf16[400,768]{1,0:T(8,128)(2,1)S(1)}, bf16[400,768]{1,0:T(8,128)(2,1)S(1)}, u32[]{:S(2)}, u32[]{:S(2)}) collective-permute-start(bf16[400,768]{1,0:T(8,128)(2,1)S(1)} %collective-permute-done.5.own), channel_id=1, source_target_pairs={{0,4},{4,0},{8,12},{12,8},{16,20},{20,16},{24,28},{28,24},{1,5},{5... | collective-permute-start | bytes 1843208 | tf_op jit(solution)/shard_map/ppermute | solution.py:226
  43.4 16.5 %collective-permute-start.11 = (bf16[400,768]{1,0:T(8,128)(2,1)S(1)}, bf16[400,768]{1,0:T(8,128)(2,1)S(1)}, u32[]{:S(2)}, u32[]{:S(2)}) collective-permute-start(bf16[400,768]{1,0:T(8,128)(2,1)S(1)} %broadcast_select_fusion), channel_id=1, source_target_pairs={{0,1},{1,0},{2,3},{3,2},{4,6},{5,7},{6,4},{7,5},{8,9},{9,8},{10,11... | collective-permute-start | bytes 1843208 | tf_op jit(solution)/shard_map/ppermute | solution.py:226
  44.4 15.5 %collective-permute-start.12 = (bf16[1,4,96,768]{3,2,1,0:T(8,128)(2,1)S(1)}, bf16[1,4,96,768]{3,2,1,0:T(8,128)(2,1)S(1)}, u32[]{:S(2)}, u32[]{:S(2)}) collective-permute-start(bf16[1,4,96,768]{3,2,1,0:T(8,128)(2,1)S(1)} %bitcast.50), channel_id=1, source_target_pairs={{0,1},{1,0},{2,3},{3,2},{4,6},{5,7},{6,4},{7,5},{8,9},{9,8},{10,11... | collective-permute-start | bytes 1769480 | tf_op jit(solution)/shard_map/ppermute | solution.py:226
  45.5 13.5 %collective-permute-start.13 = (bf16[192,384]{1,0:T(8,128)(2,1)S(1)}, bf16[192,384]{1,0:T(8,128)(2,1)S(1)}, u32[]{:S(2)}, u32[]{:S(2)}) collective-permute-start(bf16[192,384]{1,0:T(8,128)(2,1)S(1)} %bitcast.56), channel_id=1, source_target_pairs={{0,8},{4,12},{8,16},{12,20},{16,24},{20,28},{24,0},{28,4},{1,9},{5... | collective-permute-start | bytes 442376 | tf_op jit(solution)/shard_map/ppermute | solution.py:226
  48.9 10.6 %collective-permute-start.14 = (bf16[192,384]{1,0:T(8,128)(2,1)S(1)}, bf16[192,384]{1,0:T(8,128)(2,1)S(1)}, u32[]{:S(2)}, u32[]{:S(2)}) collective-permute-start(bf16[192,384]{1,0:T(8,128)(2,1)S(1)} %bitcast.57), channel_id=1, source_target_pairs={{0,16},{4,20},{8,24},{12,28},{16,0},{20,4},{24,8},{28,12},{1,17},{... | collective-permute-start | bytes 442376 | tf_op jit(solution)/shard_map/ppermute | solution.py:226
  50.2 9.3 %collective-permute-start.15 = (bf16[192,384]{1,0:T(8,128)(2,1)S(1)}, bf16[192,384]{1,0:T(8,128)(2,1)S(1)}, u32[]{:S(2)}, u32[]{:S(2)}) collective-permute-start(bf16[192,384]{1,0:T(8,128)(2,1)S(1)} %bitcast.58), channel_id=1, source_target_pairs={{0,24},{4,28},{8,0},{12,4},{16,8},{20,12},{24,16},{28,20},{1,25},{... | collective-permute-start | bytes 442376 | tf_op jit(solution)/shard_map/ppermute | solution.py:226
  60.0 16.3 %collective-permute-start.17 = (bf16[2,4,96,768]{3,2,1,0:T(8,128)(2,1)S(1)}, bf16[2,4,96,768]{3,2,1,0:T(8,128)(2,1)S(1)}, u32[]{:S(2)}, u32[]{:S(2)}) collective-permute-start(bf16[2,4,96,768]{3,2,1,0:T(8,128)(2,1)S(1)} %pad_maximum_fusion.u0), channel_id=1, source_target_pairs={{0,2},{1,3},{2,0},{3,1},{4,5},{5,4},{6,7},{7,6},{8,10},{9,11},{10,... | collective-permute-start | bytes 3538952 | tf_op jit(solution)/shard_map/ppermute | solution.py:226
  60.9 15.4 %collective-permute-start.18 = (bf16[2,4,96,768]{3,2,1,0:T(8,128)(2,1)S(1)}, bf16[2,4,96,768]{3,2,1,0:T(8,128)(2,1)S(1)}, u32[]{:S(2)}, u32[]{:S(2)}) collective-permute-start(bf16[2,4,96,768]{3,2,1,0:T(8,128)(2,1)S(1)} %pad_maximum_fusion.u0), channel_id=1, source_target_pairs={{0,4},{4,0},{8,12},{12,8},{16,20},{20,16},{24,28},{28,24},{1,5},{5... | collective-permute-start | bytes 3538952 | tf_op jit(solution)/shard_map/ppermute | solution.py:226
  60.9 8.0 %collective-permute-start.16 = (bf16[400,768]{1,0:T(8,128)(2,1)S(1)}, bf16[400,768]{1,0:T(8,128)(2,1)S(1)}, u32[]{:S(2)}, u32[]{:S(2)}) collective-permute-start(bf16[400,768]{1,0:T(8,128)(2,1)S(1)} %collective-permute-done.11.own), channel_id=1, source_target_pairs={{0,4},{4,0},{8,12},{12,8},{16,20},{20,16},{24,28},{28,24},{1,5},{5... | collective-permute-start | bytes 1843208 | tf_op jit(solution)/shard_map/ppermute | solution.py:1303
  76.3 10.0 %collective-permute-start.19 = (bf16[2,4,96,768]{3,2,1,0:T(8,128)(2,1)S(1)}, bf16[2,4,96,768]{3,2,1,0:T(8,128)(2,1)S(1)}, u32[]{:S(2)}, u32[]{:S(2)}) collective-permute-start(bf16[2,4,96,768]{3,2,1,0:T(8,128)(2,1)S(1)} %collective-permute-done.17.u1), channel_id=1, source_target_pairs={{0,4},{4,0},{8,12},{12,8},{16,20},{20,16},{24,28},{28,24},{1,5},{5... | collective-permute-start | bytes 3538952 | tf_op jit(solution)/shard_map/ppermute | solution.py:226
  76.4 9.9 %collective-permute-start.20 = (bf16[1,4,192,384]{3,2,1,0:T(8,128)(2,1)S(1)}, bf16[1,4,192,384]{3,2,1,0:T(8,128)(2,1)S(1)}, u32[]{:S(2)}, u32[]{:S(2)}) collective-permute-start(bf16[1,4,192,384]{3,2,1,0:T(8,128)(2,1)S(1)} %maximum_bitcast_fusion), channel_id=1, source_target_pairs={{0,1},{1,0},{2,3},{3,2},{4,6},{5,7},{6,4},{7,5},{8,9},{9,8},{10,11... | collective-permute-start | bytes 1769480 | tf_op jit(solution)/shard_map/ppermute | solution.py:226
  86.5 16.3 %collective-permute-start.21 = (bf16[2,4,192,384]{3,2,1,0:T(8,128)(2,1)S(1)}, bf16[2,4,192,384]{3,2,1,0:T(8,128)(2,1)S(1)}, u32[]{:S(2)}, u32[]{:S(2)}) collective-permute-start(bf16[2,4,192,384]{3,2,1,0:T(8,128)(2,1)S(1)} %pad_maximum_fusion.1.d0), channel_id=1, source_target_pairs={{0,2},{1,3},{2,0},{3,1},{4,5},{5,4},{6,7},{7,6},{8,10},{9,11},{10,... | collective-permute-start | bytes 3538952 | tf_op jit(solution)/shard_map/ppermute | solution.py:226
  87.8 15.0 %collective-permute-start.22 = (bf16[2,4,192,384]{3,2,1,0:T(8,128)(2,1)S(1)}, bf16[2,4,192,384]{3,2,1,0:T(8,128)(2,1)S(1)}, u32[]{:S(2)}, u32[]{:S(2)}) collective-permute-start(bf16[2,4,192,384]{3,2,1,0:T(8,128)(2,1)S(1)} %pad_maximum_fusion.1.d0), channel_id=1, source_target_pairs={{0,4},{4,0},{8,12},{12,8},{16,20},{20,16},{24,28},{28,24},{1,5},{5... | collective-permute-start | bytes 3538952 | tf_op jit(solution)/shard_map/ppermute | solution.py:226
  102.8 2.8 %collective-permute-start.23 = (bf16[2,4,192,384]{3,2,1,0:T(8,128)(2,1)S(1)}, bf16[2,4,192,384]{3,2,1,0:T(8,128)(2,1)S(1)}, u32[]{:S(2)}, u32[]{:S(2)}) collective-permute-start(bf16[2,4,192,384]{3,2,1,0:T(8,128)(2,1)S(1)} %collective-permute-done.21.d1), channel_id=1, source_target_pairs={{0,4},{4,0},{8,12},{12,8},{16,20},{20,16},{24,28},{28,24},{1,5},{5... | collective-permute-start | bytes 3538952 | tf_op jit(solution)/shard_map/ppermute | solution.py:226
  127.8 13.9 %collective-permute-start.24 = (bf16[4,4,96,768]{3,2,1,0:T(8,128)(2,1)}, bf16[4,4,96,768]{3,2,1,0:T(8,128)(2,1)S(1)}, u32[]{:S(2)}, u32[]{:S(2)}) collective-permute-start(bf16[4,4,96,768]{3,2,1,0:T(8,128)(2,1)} %get-tuple-element.300), channel_id=1, source_target_pairs={{0,4},{4,0},{8,12},{12,8},{16,20},{20,16},{24,28},{28,24},{1,5},{5... | collective-permute-start | bytes 7077896 | tf_op jit(solution)/shard_map/ppermute | solution.py:226
  128.0 13.7 %copy-start.3 = (bf16[4,4,96,768]{3,2,1,0:T(8,128)(2,1)S(1)}, bf16[4,4,96,768]{3,2,1,0:T(8,128)(2,1)}, u32[]{:S(2)}) copy-start(bf16[4,4,96,768]{3,2,1,0:T(8,128)(2,1)} %get-tuple-element.290) | copy-start | bytes 7077892
  142.4 16.3 %collective-permute-start.25 = (bf16[2,4,96,768]{3,2,1,0:T(8,128)(2,1)S(1)}, bf16[2,4,96,768]{3,2,1,0:T(8,128)(2,1)S(1)}, u32[]{:S(2)}, u32[]{:S(2)}) collective-permute-start(bf16[2,4,96,768]{3,2,1,0:T(8,128)(2,1)S(1)} %get-tuple-element.311), channel_id=1, source_target_pairs={{0,2},{1,3},{2,0},{3,1},{4,5},{5,4},{6,7},{7,6},{8,10},{9,11},{10,... | collective-permute-start | bytes 3538952 | tf_op jit(solution)/shard_map/ppermute | solution.py:226
  160.3 10.3 %collective-permute-start.27 = (bf16[4,4,96,768]{3,2,1,0:T(8,128)(2,1)S(1)}, bf16[4,4,96,768]{3,2,1,0:T(8,128)(2,1)S(1)}, u32[]{:S(2)}, u32[]{:S(2)}) collective-permute-start(bf16[4,4,96,768]{3,2,1,0:T(8,128)(2,1)S(1)} %copy-done.22), channel_id=1, source_target_pairs={{0,4},{4,0},{8,12},{12,8},{16,20},{20,16},{24,28},{28,24},{1,5},{5... | collective-permute-start | bytes 7077896 | tf_op jit(solution)/shard_map/ppermute | solution.py:226
  160.3 10.3 %collective-permute-start.26 = (bf16[1,4,96,768]{3,2,1,0:T(8,128)(2,1)S(1)}, bf16[1,4,96,768]{3,2,1,0:T(8,128)(2,1)S(1)}, u32[]{:S(2)}, u32[]{:S(2)}) collective-permute-start(bf16[1,4,96,768]{3,2,1,0:T(8,128)(2,1)S(1)} %get-tuple-element.317), channel_id=1, source_target_pairs={{0,1},{1,0},{2,3},{3,2},{4,6},{5,7},{6,4},{7,5},{8,9},{9,8},{10,11... | collective-permute-start | bytes 1769480 | tf_op jit(solution)/shard_map/ppermute | solution.py:226
  171.4 19.4 %collective-permute-start.28 = (bf16[2,4,96,768]{3,2,1,0:T(8,128)(2,1)S(1)}, bf16[2,4,96,768]{3,2,1,0:T(8,128)(2,1)S(1)}, u32[]{:S(2)}, u32[]{:S(2)}) collective-permute-start(bf16[2,4,96,768]{3,2,1,0:T(8,128)(2,1)S(1)} %get-tuple-element.333), channel_id=1, source_target_pairs={{0,2},{1,3},{2,0},{3,1},{4,5},{5,4},{6,7},{7,6},{8,10},{9,11},{10,... | collective-permute-start | bytes 3538952 | tf_op jit(solution)/shard_map/ppermute | solution.py:226
  172.7 14.3 %collective-permute-start.29 = (bf16[96,768]{1,0:T(8,128)(2,1)S(1)}, bf16[96,768]{1,0:T(8,128)(2,1)S(1)}, u32[]{:S(2)}, u32[]{:S(2)}) collective-permute-start(bf16[96,768]{1,0:T(8,128)(2,1)S(1)} %get-tuple-element.334), channel_id=1, source_target_pairs={{0,24},{4,28},{8,0},{12,4},{16,8},{20,12},{24,16},{28,20},{1,25},{... | collective-permute-start | bytes 442376 | tf_op jit(solution)/shard_map/ppermute | solution.py:226
  177.0 13.8 %collective-permute-start.30 = (bf16[96,768]{1,0:T(8,128)(2,1)S(1)}, bf16[96,768]{1,0:T(8,128)(2,1)S(1)}, u32[]{:S(2)}, u32[]{:S(2)}) collective-permute-start(bf16[96,768]{1,0:T(8,128)(2,1)S(1)} %get-tuple-element.335), channel_id=1, source_target_pairs={{0,16},{4,20},{8,24},{12,28},{16,0},{20,4},{24,8},{28,12},{1,17},{... | collective-permute-start | bytes 442376 | tf_op jit(solution)/shard_map/ppermute | solution.py:226
  177.7 13.2 %collective-permute-start.31 = (bf16[96,768]{1,0:T(8,128)(2,1)S(1)}, bf16[96,768]{1,0:T(8,128)(2,1)S(1)}, u32[]{:S(2)}, u32[]{:S(2)}) collective-permute-start(bf16[96,768]{1,0:T(8,128)(2,1)S(1)} %get-tuple-element.336), channel_id=1, source_target_pairs={{0,8},{4,12},{8,16},{12,20},{16,24},{20,28},{24,0},{28,4},{1,9},{5... | collective-permute-start | bytes 442376 | tf_op jit(solution)/shard_map/ppermute | solution.py:226
  191.2 10.8 %collective-permute-start.33 = (bf16[1,4,96,768]{3,2,1,0:T(8,128)(2,1)S(1)}, bf16[1,4,96,768]{3,2,1,0:T(8,128)(2,1)S(1)}, u32[]{:S(2)}, u32[]{:S(2)}) collective-permute-start(bf16[1,4,96,768]{3,2,1,0:T(8,128)(2,1)S(1)} %get-tuple-element.344), channel_id=1, source_target_pairs={{0,1},{1,0},{2,3},{3,2},{4,6},{5,7},{6,4},{7,5},{8,9},{9,8},{10,11... | collective-permute-start | bytes 1769480 | tf_op jit(solution)/shard_map/ppermute | solution.py:226
  192.7 9.3 %collective-permute-start.32 = (bf16[400,768]{1,0:T(8,128)(2,1)S(1)}, bf16[400,768]{1,0:T(8,128)(2,1)S(1)}, u32[]{:S(2)}, u32[]{:S(2)}) collective-permute-start(bf16[400,768]{1,0:T(8,128)(2,1)S(1)} %copy-done.24), channel_id=1, source_target_pairs={{0,4},{4,0},{8,12},{12,8},{16,20},{20,16},{24,28},{28,24},{1,5},{5... | collective-permute-start | bytes 1843208 | tf_op jit(solution)/shard_map/ppermute | solution.py:226
  202.3 12.3 %collective-permute-start.35 = (bf16[96,768]{1,0:T(8,128)(2,1)S(1)}, bf16[96,768]{1,0:T(8,128)(2,1)S(1)}, u32[]{:S(2)}, u32[]{:S(2)}) collective-permute-start(bf16[96,768]{1,0:T(8,128)(2,1)S(1)} %get-tuple-element.353), channel_id=1, source_target_pairs={{0,24},{4,28},{8,0},{12,4},{16,8},{20,12},{24,16},{28,20},{1,25},{... | collective-permute-start | bytes 442376 | tf_op jit(solution)/shard_map/ppermute | solution.py:226
  204.0 10.5 %collective-permute-start.36 = (bf16[96,768]{1,0:T(8,128)(2,1)S(1)}, bf16[96,768]{1,0:T(8,128)(2,1)S(1)}, u32[]{:S(2)}, u32[]{:S(2)}) collective-permute-start(bf16[96,768]{1,0:T(8,128)(2,1)S(1)} %get-tuple-element.354), channel_id=1, source_target_pairs={{0,8},{4,12},{8,16},{12,20},{16,24},{20,28},{24,0},{28,4},{1,9},{5... | collective-permute-start | bytes 442376 | tf_op jit(solution)/shard_map/ppermute | solution.py:226
  204.3 10.2 %collective-permute-start.34 = (bf16[400,768]{1,0:T(8,128)(2,1)S(1)}, bf16[400,768]{1,0:T(8,128)(2,1)S(1)}, u32[]{:S(2)}, u32[]{:S(2)}) collective-permute-start(bf16[400,768]{1,0:T(8,128)(2,1)S(1)} %add_convert_fusion.6), channel_id=1, source_target_pairs={{0,1},{1,0},{2,3},{3,2},{4,6},{5,7},{6,4},{7,5},{8,9},{9,8},{10,11... | collective-permute-start | bytes 1843208 | tf_op jit(solution)/shard_map/ppermute | solution.py:226
  205.0 9.6 %collective-permute-start.37 = (bf16[400,768]{1,0:T(8,128)(2,1)S(1)}, bf16[400,768]{1,0:T(8,128)(2,1)S(1)}, u32[]{:S(2)}, u32[]{:S(2)}) collective-permute-start(bf16[400,768]{1,0:T(8,128)(2,1)S(1)} %copy-done.23), channel_id=1, source_target_pairs={{0,4},{4,0},{8,12},{12,8},{16,20},{20,16},{24,28},{28,24},{1,5},{5... | collective-permute-start | bytes 1843208 | tf_op jit(solution)/shard_map/ppermute | solution.py:226
  214.6 2.4 collective-permute-start.38
  218.6 13.4 %collective-permute-start.41 = (bf16[96,768]{1,0:T(8,128)(2,1)S(1)}, bf16[96,768]{1,0:T(8,128)(2,1)S(1)}, u32[]{:S(2)}, u32[]{:S(2)}) collective-permute-start(bf16[96,768]{1,0:T(8,128)(2,1)S(1)} %get-tuple-element.369), channel_id=1, source_target_pairs={{0,16},{4,20},{8,24},{12,28},{16,0},{20,4},{24,8},{28,12},{1,17},{... | collective-permute-start | bytes 442376 | tf_op jit(solution)/shard_map/ppermute | solution.py:226
  220.3 15.7 %collective-permute-start.39 = (bf16[400,768]{1,0:T(8,128)(2,1)S(1)}, bf16[400,768]{1,0:T(8,128)(2,1)S(1)}, u32[]{:S(2)}, u32[]{:S(2)}) collective-permute-start(bf16[400,768]{1,0:T(8,128)(2,1)S(1)} %get-tuple-element.367), channel_id=1, source_target_pairs={{0,1},{1,0},{2,3},{3,2},{4,5},{5,4},{6,7},{7,6},{8,9},{9,8},{10,11... | collective-permute-start | bytes 1843208 | tf_op jit(solution)/shard_map/ppermute | solution.py:226
  221.5 15.6 %collective-permute-start.40 = (bf16[400,768]{1,0:T(8,128)(2,1)S(1)}, bf16[400,768]{1,0:T(8,128)(2,1)S(1)}, u32[]{:S(2)}, u32[]{:S(2)}) collective-permute-start(bf16[400,768]{1,0:T(8,128)(2,1)S(1)} %get-tuple-element.368), channel_id=1, source_target_pairs={{0,2},{1,3},{2,0},{3,1},{4,6},{5,7},{6,4},{7,5},{8,10},{9,11},{10,... | collective-permute-start | bytes 1843208 | tf_op jit(solution)/shard_map/ppermute | solution.py:226
  237.1 2.2 collective-permute-start.42
  243.4 14.8 %collective-permute-start.43 = (bf16[112,768]{1,0:T(8,128)(2,1)}, bf16[112,768]{1,0:T(8,128)(2,1)S(1)}, u32[]{:S(2)}, u32[]{:S(2)}) collective-permute-start(bf16[112,768]{1,0:T(8,128)(2,1)} %get-tuple-element.384), channel_id=1, source_target_pairs={{0,24},{4,28},{8,0},{12,4},{16,8},{20,12},{24,16},{28,20},{1,25},{... | collective-permute-start | bytes 516104 | tf_op jit(solution)/shard_map/ppermute | solution.py:226
  245.8 17.3 %collective-permute-start.44 = (bf16[112,768]{1,0:T(8,128)(2,1)}, bf16[112,768]{1,0:T(8,128)(2,1)S(1)}, u32[]{:S(2)}, u32[]{:S(2)}) collective-permute-start(bf16[112,768]{1,0:T(8,128)(2,1)} %get-tuple-element.385), channel_id=1, source_target_pairs={{0,16},{4,20},{8,24},{12,28},{16,0},{20,4},{24,8},{28,12},{1,17},{... | collective-permute-start | bytes 516104 | tf_op jit(solution)/shard_map/ppermute | solution.py:226
  247.4 15.7 %collective-permute-start.45 = (bf16[112,768]{1,0:T(8,128)(2,1)}, bf16[112,768]{1,0:T(8,128)(2,1)S(1)}, u32[]{:S(2)}, u32[]{:S(2)}) collective-permute-start(bf16[112,768]{1,0:T(8,128)(2,1)} %get-tuple-element.386), channel_id=1, source_target_pairs={{0,8},{4,12},{8,16},{12,20},{16,24},{20,28},{24,0},{28,4},{1,9},{5... | collective-permute-start | bytes 516104 | tf_op jit(solution)/shard_map/ppermute | solution.py:226
  (23 other events, 87.1 us)

commit v3 on v2

--- a/solution.py
+++ b/solution.py
@@ -46,12 +46,12 @@
 
 def call(
     kernel, name, grid, in_specs, out_specs, out_shape, scratch=(), prefetch=0, cost=None, limit=LIMIT, aliases={},
-    least=BIG, free=pltpu.VMEM,
+    least=BIG, free=pltpu.VMEM, most=BIG,
 ):
     several = isinstance(out_shape, list)
     shapes = [
         pltpu.HBM(v.shape, v.dtype)
-        if isinstance(v, jax.ShapeDtypeStruct) and v.size * v.dtype.itemsize >= BIG else v
+        if isinstance(v, jax.ShapeDtypeStruct) and v.size * v.dtype.itemsize >= most else v
         for v in (out_shape if several else [out_shape])
     ]
     run = pl.pallas_call(
@@ -493,7 +493,7 @@
     shapes = [(tall, 4 * narrow), (16, 4 * narrow)]
     return call(
         block_kernel, "block", (1,), [whole(q.shape)] * 4 + [whole(u.shape) for u in vectors],
-        [whole(v) for v in shapes], [sds(v, bf16) for v in shapes], cost=guess(1e6, 1e6), limit=SMALL, least=0,
+        [whole(v) for v in shapes], [sds(v, bf16) for v in shapes], cost=guess(1e6, 1e6), limit=SMALL, least=0, most=1 << 40,
     )(q, k, v, o, *vectors)
 
 
@@ -520,8 +520,8 @@
     height, width = parts[0].shape
     out = ((height - 16) // depth + 16, width)
     return call(
-        total_kernel, "total", (1,), [whole(parts[0].shape)] * 4, [whole(out)] * depth,
-        [sds(out, f32)] + [sds(out, bf16)] * (depth - 1), prefetch=1, cost=guess(1e6, 4e6), limit=SMALL,
+        total_kernel, "total", (1,), [held()] * 4, [whole(out)] * depth,
+        [sds(out, f32)] + [sds(out, bf16)] * (depth - 1), prefetch=1, cost=guess(1e6, 4e6), limit=SMALL, most=1 << 40,
     )(place, *parts)
 
 
@@ -552,7 +552,7 @@
     tall, narrow = height - 16, width // 4
     shapes = [(tall, narrow)] * 4 + [(narrow,)] * 8 + [(width,)]
     return call(
-        unblock_kernel, "unblock", (1,), [whole(total.shape)] * (1 + len(got)), [whole(v) for v in shapes],
+        unblock_kernel, "unblock", (1,), [held()] * (1 + len(got)), [whole(v) for v in shapes],
         [sds(v, f32) for v in shapes], cost=guess(1e6, 1e6), limit=SMALL,
     )(total, *got)
 
@@ -568,8 +568,8 @@
     shape = parts[0].shape
     out = (len(parts), *shape)
     return call(
-        line_up_kernel, "line_up", (1,), [whole(shape)] * len(parts), whole(out), sds(out, parts[0].dtype),
-        prefetch=1, cost=guess(1e6, 1e6), limit=SMALL,
+        line_up_kernel, "line_up", (1,), [held()] * len(parts), whole(out), sds(out, parts[0].dtype),
+        prefetch=1, cost=guess(1e6, 1e6), limit=SMALL, most=1 << 40,
     )(place, *parts)
 
 
@@ -586,8 +586,8 @@
     tall, width = parts[0].shape
     out = (len(parts) * tall + 16, width)
     return call(
-        line_up_rows_kernel, "line_up_rows", (1,), [whole((tall, width))] * len(parts) + [whole(slab.shape)],
-        whole(out), sds(out, bf16), prefetch=1, cost=guess(1e6, 1e6), limit=SMALL,
+        line_up_rows_kernel, "line_up_rows", (1,), [held()] * (len(parts) + 1),
+        whole(out), sds(out, bf16), prefetch=1, cost=guess(1e6, 1e6), limit=SMALL, most=1 << 40,
     )(place, *parts, slab)
 
 
@@ -803,7 +803,7 @@
         [sds(sent, bf16)] * 2 + [sds((t, USED), bf16)],
         [pltpu.VMEM((t, USED), bf16), pltpu.VMEM((d, width), bf16), pltpu.VMEM((8, USED), f32), pltpu.VMEM((d, t), bf16),
          pltpu.VMEM((d, narrow), bf16), pltpu.SemaphoreType.DMA((2,))],
-        prefetch=1, cost=guess(10e9, 12e6), limit=SMALL,
+        prefetch=1, cost=guess(10e9, 12e6), limit=SMALL, most=1 << 40,
     )(place, x_t, kept, grad_context, lse, delta, gow, inner, outer, gub, q_ext, k_ext)
 
 

time: 271 us -> 258 us (0.952)
  Pallas kernels: 169 us -> 156 us
  waiting for transfers between devices: 33.2 us -> 36.6 us
  local copies, waits for them, and re-layouts: 7.24 us -> 4.49 us
    pallas_call x20, Pallas kernels: 169 us -> 156 us  [run_far(): return run(*args[:prefetch], *given)]
    ppermute x45, waiting for transfers between devices: 33.2 us -> 36.6 us  [beside(): lax.ppermute(v, axis, perm)]
    unnamed x50 -> x22, local copies, waits for them, and re-layouts: 4.53 us -> 1.74 us
  transfers between devices with their start and end apart: 46 -> 46, of which waited for: 14 -> 18; matrix products, arithmetic and copies ran while one was open for 1% -> 1% of each run, Pallas kernels for 51% -> 52%
where the time goes in v3:
time: 258 us; the launch traced here: 253 us
  Pallas kernels  156 us (60%)
  starting transfers between devices  49.1 us (19%)
  waiting for transfers between devices  36.6 us (14%)
  other arithmetic  5 us (2%)
  local copies, waits for them, and re-layouts  4.49 us (2%)
    pallas_call x20, Pallas kernels, run_far(): return run(*args[:prefetch], *given)  156 us
    ppermute x45, starting transfers between devices, beside(): lax.ppermute(v, axis, perm)  48.6 us
    ppermute x45, waiting for transfers between devices, beside(): lax.ppermute(v, axis, perm)  36.6 us
  transfers between devices with their start and end apart: 46, of which 18 were waited for; matrix products, arithmetic and copies ran while one was open for 1% of the time, Pallas kernels for 52%

profile of v3, /device:TPU:0, one launch (start us, length us, event | category | flops | bytes accessed | tf_op | source)
XLA Modules:
  0.0 253.2 jit_solution(459501807195180269)
XLA Ops:
  1.7 3.1 %collective-permute-start = (bf16[96,768]{1,0:T(8,128)(2,1)S(1)}, bf16[96,768]{1,0:T(8,128)(2,1)S(1)}, u32[]{:S(2)}, u32[]{:S(2)}) collective-permute-start(bf16[96,768]{1,0:T(8,128)(2,1)S(1)} %get-tuple-element.219.refs_0_), channel_id=1, source_target_pairs={{0,8},{4,12},{8,16},{12,20},{16,24},{20,28},{24,0},{28,4},{1,9},{5... | collective-permute-start | bytes 442376 | tf_op jit(solution)/shard_map/ppermute | solution.py:226
  4.8 2.6 %collective-permute-start.1 = (bf16[96,768]{1,0:T(8,128)(2,1)S(1)}, bf16[96,768]{1,0:T(8,128)(2,1)S(1)}, u32[]{:S(2)}, u32[]{:S(2)}) collective-permute-start(bf16[96,768]{1,0:T(8,128)(2,1)S(1)} %get-tuple-element.219.refs_0_), channel_id=1, source_target_pairs={{0,16},{4,20},{8,24},{12,28},{16,0},{20,4},{24,8},{28,12},{1,17},{... | collective-permute-start | bytes 442376 | tf_op jit(solution)/shard_map/ppermute | solution.py:226
  7.4 1.3 collective-permute-start.2
  8.8 2.6 %copy.49 = bf16[1024,768]{0,1:T(8,128)(2,1)} copy(bf16[1024,768]{1,0:T(8,128)(2,1)} %x.9) | data formatting | bytes 3145728 | tf_op jit(solution)/shard_map/optimization_barrier | solution.py:221
  11.6 5.5 %collective-permute-done.1.refs_2_ = bf16[96,768]{1,0:T(8,128)(2,1)S(1)} collective-permute-done((bf16[96,768]{1,0:T(8,128)(2,1)S(1)}, bf16[96,768]{1,0:T(8,128)(2,1)S(1)}, u32[]{:S(2)}, u32[]{:S(2)}) %collective-permute-start.1) | collective-permute-done | bytes 147488 | tf_op jit(solution)/shard_map/ppermute | solution.py:226
  17.8 1.6 collective-permute-start.4
  19.3 1.5 collective-permute-start.5
  21.5 3.7 %collective-permute-start.6 = (bf16[96,768]{1,0:T(8,128)(2,1)S(1)}, bf16[96,768]{1,0:T(8,128)(2,1)S(1)}, u32[]{:S(2)}, u32[]{:S(2)}) collective-permute-start(bf16[96,768]{1,0:T(8,128)(2,1)S(1)} %copy-done), channel_id=1, source_target_pairs={{0,8},{4,12},{8,16},{12,20},{16,24},{20,28},{24,0},{28,4},{1,9},{5... | collective-permute-start | bytes 442376 | tf_op jit(solution)/shard_map/ppermute | solution.py:226
  25.2 1.6 collective-permute-start.7
  27.6 8.0 %attend.4 = (bf16[4,1024,192]{2,1,0:T(8,128)(2,1)}, bf16[4,4,2,96,768]{4,3,2,1,0:T(8,128)(2,1)}, bf16[4,16,768]{2,1,0:T(8,128)(2,1)}, bf16[1024,640]{1,0:T(8,128...) custom-call(s32[29]{0:T(128)S(1)} %concatenate.12.place, ...), custom_call_target="tpu_custom_call" | custom-call | flops 5000000000 | bytes 8000000 | tf_op jit(solution)/shard_map/attend/pallas_call | solution.py:79
  38.4 1.5 collective-permute-start.12
  39.9 3.6 %collective-permute-start.13 = (bf16[192,384]{1,0:T(8,128)(2,1)S(1)}, bf16[192,384]{1,0:T(8,128)(2,1)S(1)}, u32[]{:S(2)}, u32[]{:S(2)}) collective-permute-start(bf16[192,384]{1,0:T(8,128)(2,1)S(1)} %bitcast.56), channel_id=1, source_target_pairs={{0,8},{4,12},{8,16},{12,20},{16,24},{20,28},{24,0},{28,4},{1,9},{5... | collective-permute-start | bytes 442376 | tf_op jit(solution)/shard_map/ppermute | solution.py:226
  43.5 1.3 collective-permute-start.14
  44.9 1.4 collective-permute-start.15
  46.3 7.4 %attend.5 = (bf16[4,1024,192]{2,1,0:T(8,128)(2,1)}, bf16[4,4,2,96,768]{4,3,2,1,0:T(8,128)(2,1)}, bf16[4,16,768]{2,1,0:T(8,128)(2,1)}, bf16[1024,640]{1,0:T(8,128)(2,1)}, f32[8,1024]{1,0:T(8,128)}) custom-call(s32[29]{0:T(128)S(1)} %concatenate.12.place, s32[1]{0:T(128)S(6)} %copy.62.bucket, ...), custom_call_target="tpu_custom_call", output_to_operand_aliasing={{0}: (8, {}), {1}: (9, {}), {2}: (10, {})} | custom-call | flops 5000000000 | bytes 8000000 | tf_op jit(solution)/shard_map/attend/pallas_call | solution.py:79
  55.7 7.4 %attend.6 = (bf16[4,1024,192]{2,1,0:T(8,128)(2,1)}, bf16[4,4,2,96,768]{4,3,2,1,0:T(8,128)(2,1)}, bf16[4,16,768]{2,1,0:T(8,128)(2,1)}, bf16[1024,640]{1,0:T(8,128)(2,1)}, f32[8,1024]{1,0:T(8,128)}) custom-call(s32[29]{0:T(128)S(1)} %concatenate.12.place, s32[1]{0:T(128)S(6)} %copy.62.bucket, ...), custom_call_target="tpu_custom_call", output_to_operand_aliasing={{0}: (8, {}), {1}: (9, {}), {2}: (10, {})} | custom-call | flops 5000000000 | bytes 8000000 | tf_op jit(solution)/shard_map/attend/pallas_call | solution.py:79
  63.1 7.4 %attend.7 = (bf16[4,1024,192]{2,1,0:T(8,128)(2,1)}, bf16[4,4,2,96,768]{4,3,2,1,0:T(8,128)(2,1)}, bf16[4,16,768]{2,1,0:T(8,128)(2,1)}, bf16[1024,640]{1,0:T(8,128)(2,1)}, f32[8,1024]{1,0:T(8,128)}) custom-call(s32[29]{0:T(128)S(1)} %concatenate.12.place, s32[1]{0:T(128)S(6)} %copy.62.bucket, ...), custom_call_target="tpu_custom_call", output_to_operand_aliasing={{0}: (8, {}), {1}: (9, {}), {2}: (10, {})} | custom-call | flops 5000000000 | bytes 8000000 | tf_op jit(solution)/shard_map/attend/pallas_call | solution.py:79
  71.7 5.7 %attended.1 = (f32[1024,768]{1,0:T(8,128)S(1)}, f32[1024,128]{1,0:T(8,128)S(1)}, bf16[1024,768]{1,0:T(8,128)(2,1)S(1)}, bf16[768,1024]{1,0:T(8,128)(2,1)S(1)}, b...) custom-call(bf16[1024,768]{1,0:T(8,128)(2,1)} %x.9, bf16[4,1024,192]{2,1,0:T(8,128)(2,1)} %get-tuple-element.264.context, ...), custom_call_target="tpu_custom_call" | custom-call | flops 3000000000 | bytes 10000000 | tf_op jit(solution)/shard_map/attended/pallas_call | solution.py:79
  77.4 3.2 %collective-permute-done.20 = bf16[1,4,192,384]{3,2,1,0:T(8,128)(2,1)S(1)} collective-permute-done((bf16[1,4,192,384]{3,2,1,0:T(8,128)(2,1)S(1)}, bf16[1,4,192,384]{3,2,1,0:T(8,128)(2,1)S(1)}, u32[]{:S(2)}, u32[]{:S(2)}) %collective-permute-start.20) | collective-permute-done | bytes 589856 | tf_op jit(solution)/shard_map/ppermute | solution.py:226
  80.8 1.5 collective-permute-start.21
  82.3 13.6 %up.1 = (bf16[4,1024,768]{2,1,0:T(8,128)(2,1)}, bf16[4,1024,768]{2,1,0:T(8,128)(2,1)}, bf16[4,4,2,96,768]{4,3,2,1,0:T(8,128)(2,1)}) custom-call(s32[29]{0:T(128)S(1)} %concatenate.12.place, bf16[1024,768]{1,0:T(8,128)(2,1)S(1)} %get-tuple-element.277.low, bf16[4,16,768]{2,1,0:T(8,128)(2,1)} %get-tuple-element.271.slabs, ...), custom_call_target="tpu_custom_call" | custom-call | flops 12000000000 | bytes 30000000 | tf_op jit(solution)/shard_map/up/pallas_call | solution.py:79
  97.1 2.8 %collective-permute-done.23.d3 = bf16[2,4,192,384]{3,2,1,0:T(8,128)(2,1)S(1)} collective-permute-done((bf16[2,4,192,384]{3,2,1,0:T(8,128)(2,1)S(1)}, bf16[2,4,192,384]{3,2,1,0:T(8,128)(2,1)S(1)}, u32[]{:S(2)}, u32[]{:S(2)}) %collective-permute-start.23) | collective-permute-done | bytes 1179680 | tf_op jit(solution)/shard_map/ppermute | solution.py:226
  99.9 22.2 %down.1 = (bf16[1024,768]{1,0:T(8,128)(2,1)}, f32[8,768]{1,0:T(8,128)}, f32[1024,768]{1,0:T(8,128)S(1)}, bf16[1024,768]{1,0:T(8,128)(2,1)S(1)}, f32[4,8,192]{2,1...) custom-call(s32[29]{0:T(128)S(1)} %concatenate.12.place, ...), custom_call_target="tpu_custom_call" | custom-call | flops 12000000000 | bytes 35000000 | tf_op jit(solution)/shard_map/down/pallas_call | solution.py:79
  122.3 13.8 %feed_back.2 = (bf16[4,4,96,768]{3,2,1,0:T(8,128)(2,1)}, bf16[4,4,96,768]{3,2,1,0:T(8,128)(2,1)}, f32[4,1,768]{2,1,0:T(1,128)}, f32[1024,768]{1,0:T(8,128)S(1)}) custom-call(s32[29]{0:T(128)S(1)} %concatenate.12.place, bf16[1024,768]{1,0:T(8,128)(2,1)S(1)} %get-tuple-element.293.branch, bf16[4,1024,768]{2,1,0:T(8,128)(2,1)} %get-tuple-element.294.slope, ...), custom_call_target="tpu_custom_call" | custom-call | flops 15000000512 | bytes 35000000 | tf_op jit(solution)/shard_map/feed_back/pallas_call | solution.py:79
  136.8 1.4 collective-permute-start.25
  138.1 13.6 %feed_back.3 = (bf16[4,4,96,768]{3,2,1,0:T(8,128)(2,1)}, bf16[4,4,96,768]{3,2,1,0:T(8,128)(2,1)}, f32[4,1,768]{2,1,0:T(1,128)}, f32[1024,768]{1,0:T(8,128)S(1)}) custom-call(s32[29]{0:T(128)S(1)} %concatenate.12.place, bf16[1024,768]{1,0:T(8,128)(2,1)S(1)} %get-tuple-element.293.branch, ...), custom_call_target="tpu_custom_call", output_to_operand_aliasing={{0}: (7, {}), {1}: (8, {}), {2}: (9, {})} | custom-call | flops 15000000512 | bytes 35000000 | tf_op jit(solution)/shard_map/feed_back/pallas_call | solution.py:79
  151.7 1.3 collective-permute-done.25
  153.3 1.4 copy-done.10
  155.5 9.8 %inner_back.1 = (f32[1024,768]{1,0:T(8,128)}, f32[4,8,192]{2,1,0:T(8,128)}, bf16[4,768,192]{2,1,0:T(8,128)(2,1)}, bf16[4,1024,192]{2,1,0:T(8,128)(2,1)}, f32[32,1024]{1,0:T(8,128)}) custom-call(f32[1024,768]{1,0:T(8,128)S(1)} %get-tuple-element.308.grad_normed, f32[1024,768]{1,0:T(8,128)S(1)} %get-tuple-element.284.n1, ...), custom_call_target="tpu_custom_call" | custom-call | flops 4000000000 | bytes 10000000 | tf_op jit(solution)/shard_map/inner_back/pallas_call | solution.py:79
  166.2 1.2 collective-permute-start.28
  167.4 4.6 %collective-permute-start.29 = (bf16[96,768]{1,0:T(8,128)(2,1)S(1)}, bf16[96,768]{1,0:T(8,128)(2,1)S(1)}, u32[]{:S(2)}, u32[]{:S(2)}) collective-permute-start(bf16[96,768]{1,0:T(8,128)(2,1)S(1)} %get-tuple-element.334), channel_id=1, source_target_pairs={{0,24},{4,28},{8,0},{12,4},{16,8},{20,12},{24,16},{28,20},{1,25},{... | collective-permute-start | bytes 442376 | tf_op jit(solution)/shard_map/ppermute | solution.py:226
  172.5 8.0 %attend_back.4 = (bf16[400,768]{1,0:T(8,128)(2,1)S(1)}, bf16[400,768]{1,0:T(8,128)(2,1)S(1)}, bf16[1024,640]{1,0:T(8,128)(2,1)S(1)}) custom-call(s32[29]{0:T(128)S(1)} %concatenate.12.place, bf16[768,1024]{1,0:T(8,128)(2,1)} %bitcast.52, bf16[1024,640]{1,0:T(8,128)(2,1)} %get-tuple-element.323.kept, bf16[4,1024,192]{2,1,0:T(8,128)(2,1)} %get-tuple-element.324.grad_context, ...), custom_call_target="tpu_custom_call" | custom-call | flops 10000000000 | bytes 12000000 | tf_op jit(solution)/shard_map/attend_back/pallas_call | solution.py:79
  180.5 5.1 %collective-permute-done.30 = bf16[96,768]{1,0:T(8,128)(2,1)S(1)} collective-permute-done((bf16[96,768]{1,0:T(8,128)(2,1)S(1)}, bf16[96,768]{1,0:T(8,128)(2,1)S(1)}, u32[]{:S(2)}, u32[]{:S(2)}) %collective-permute-start.30) | collective-permute-done | bytes 147488 | tf_op jit(solution)/shard_map/ppermute | solution.py:226
  185.9 1.5 collective-permute-start.33
  187.4 8.0 %attend_back.5 = (bf16[400,768]{1,0:T(8,128)(2,1)S(1)}, bf16[400,768]{1,0:T(8,128)(2,1)S(1)}, bf16[1024,640]{1,0:T(8,128)(2,1)S(1)}) custom-call(s32[29]{0:T(128)S(1)} %concatenate.12.place, bf16[768,1024]{1,0:T(8,128)(2,1)} %bitcast.53, bf16[1024,640]{1,0:T(8,128)(2,1)} %get-tuple-element.340.kept, bf16[4,1024,192]{2,1,0:T(8,128)(2,1)} %get-tuple-element.324.grad_context, ...), custom_call_target="tpu_custom_call" | custom-call | flops 10000000000 | bytes 12000000 | tf_op jit(solution)/shard_map/attend_back/pallas_call | solution.py:79
  196.5 1.2 collective-permute-start.35
  198.6 1.2 collective-permute-start.34
  199.7 8.2 %attend_back.6 = (bf16[400,768]{1,0:T(8,128)(2,1)S(1)}, bf16[400,768]{1,0:T(8,128)(2,1)S(1)}, bf16[1024,640]{1,0:T(8,128)(2,1)S(1)}) custom-call(s32[29]{0:T(128)S(1)} %concatenate.12.place, bf16[768,1024]{1,0:T(8,128)(2,1)} %bitcast.54, bf16[1024,640]{1,0:T(8,128)(2,1)} %get-tuple-element.349.kept, bf16[4,1024,192]{2,1,0:T(8,128)(2,1)} %get-tuple-element.324.grad_context, ...), custom_call_target="tpu_custom_call" | custom-call | flops 10000000000 | bytes 12000000 | tf_op jit(solution)/shard_map/attend_back/pallas_call | solution.py:79
  208.7 2.0 collective-permute-done.38
  211.3 1.6 collective-permute-start.41
  212.9 1.2 collective-permute-start.39
  214.8 8.0 %attend_back.7 = (bf16[400,768]{1,0:T(8,128)(2,1)S(1)}, bf16[400,768]{1,0:T(8,128)(2,1)S(1)}, bf16[1024,640]{1,0:T(8,128)(2,1)S(1)}) custom-call(s32[29]{0:T(128)S(1)} %concatenate.12.place, bf16[768,1024]{1,0:T(8,128)(2,1)} %bitcast.55, bf16[1024,640]{1,0:T(8,128)(2,1)} %get-tuple-element.364.kept, bf16[4,1024,192]{2,1,0:T(8,128)(2,1)} %get-tuple-element.324.grad_context, ...), custom_call_target="tpu_custom_call" | custom-call | flops 10000000000 | bytes 12000000 | tf_op jit(solution)/shard_map/attend_back/pallas_call | solution.py:79
  222.8 5.7 %collective-permute-done.39.refs_2_ = bf16[400,768]{1,0:T(8,128)(2,1)S(1)} collective-permute-done((bf16[400,768]{1,0:T(8,128)(2,1)S(1)}, bf16[400,768]{1,0:T(8,128)(2,1)S(1)}, u32[]{:S(2)}, u32[]{:S(2)}) %collective-permute-start.39) | collective-permute-done | bytes 614432 | tf_op jit(solution)/shard_map/ppermute | solution.py:226
  230.3 1.2 collective-permute-done.42.refs_1_
  232.3 1.9 collective-permute-start.43
  234.2 1.7 collective-permute-start.44
  235.8 10.7 %input_grad.1 = f32[1024,768]{1,0:T(8,128)} custom-call(s32[29]{0:T(128)S(1)} %concatenate.12.place, f32[1024,768]{1,0:T(8,128)} %get-tuple-element.379.inner, bf16[1024,640]{1,0:T(8,128)(2,1)} %copy-done.5, bf16[1024,640]{1,0:T(8,128)(2,1)} %copy-done.3, bf16[1024,640]{1,0:T(8,128)(2,1)} %copy-done.4, bf16[1024,640]{1,0:T(8,128)(2,1)} %copy-done.2, ...), custom_call_target="tpu_custom_call" | custom-call | flops 5000000000 | bytes 15000000 | tf_op jit(solution)/shard_map/input_grad/pallas_call | solution.py:79
  246.6 4.7 %collective-permute-done.44.refs_1_ = bf16[112,768]{1,0:T(8,128)(2,1)S(1)} collective-permute-done((bf16[112,768]{1,0:T(8,128)(2,1)S(1)}, bf16[112,768]{1,0:T(8,128)(2,1)S(1)}, u32[]{:S(2)}, u32[]{:S(2)}) %collective-permute-start.44) | collective-permute-done | bytes 172064 | tf_op jit(solution)/shard_map/ppermute | solution.py:226
  (107 shorter events, 21.6 us)
Async XLA Ops:
  1.7 9.9 %collective-permute-start = (bf16[96,768]{1,0:T(8,128)(2,1)S(1)}, bf16[96,768]{1,0:T(8,128)(2,1)S(1)}, u32[]{:S(2)}, u32[]{:S(2)}) collective-permute-start(bf16[96,768]{1,0:T(8,128)(2,1)S(1)} %get-tuple-element.219.refs_0_), channel_id=1, source_target_pairs={{0,8},{4,12},{8,16},{12,20},{16,24},{20,28},{24,0},{28,4},{1,9},{5... | collective-permute-start | bytes 442376 | tf_op jit(solution)/shard_map/ppermute | solution.py:226
  4.8 12.3 %collective-permute-start.1 = (bf16[96,768]{1,0:T(8,128)(2,1)S(1)}, bf16[96,768]{1,0:T(8,128)(2,1)S(1)}, u32[]{:S(2)}, u32[]{:S(2)}) collective-permute-start(bf16[96,768]{1,0:T(8,128)(2,1)S(1)} %get-tuple-element.219.refs_0_), channel_id=1, source_target_pairs={{0,16},{4,20},{8,24},{12,28},{16,0},{20,4},{24,8},{28,12},{1,17},{... | collective-permute-start | bytes 442376 | tf_op jit(solution)/shard_map/ppermute | solution.py:226
  7.4 9.7 %collective-permute-start.2 = (bf16[96,768]{1,0:T(8,128)(2,1)S(1)}, bf16[96,768]{1,0:T(8,128)(2,1)S(1)}, u32[]{:S(2)}, u32[]{:S(2)}) collective-permute-start(bf16[96,768]{1,0:T(8,128)(2,1)S(1)} %get-tuple-element.219.refs_0_), channel_id=1, source_target_pairs={{0,24},{4,28},{8,0},{12,4},{16,8},{20,12},{24,16},{28,20},{1,25},{... | collective-permute-start | bytes 442376 | tf_op jit(solution)/shard_map/ppermute | solution.py:226
  11.4 16.2 %copy-start.1 = (s32[1,8]{1,0:T(1,128)S(1)}, s32[1,8]{1,0:T(1,128)}, u32[]{:S(2)}) copy-start(s32[1,8]{1,0:T(1,128)} %param.21) | copy-start | bytes 100
  17.7 9.1 %collective-permute-start.3 = (bf16[400,768]{1,0:T(8,128)(2,1)S(1)}, bf16[400,768]{1,0:T(8,128)(2,1)S(1)}, u32[]{:S(2)}, u32[]{:S(2)}) collective-permute-start(bf16[400,768]{1,0:T(8,128)(2,1)S(1)} %line_up_rows.1.own), channel_id=1, source_target_pairs={{0,4},{4,0},{8,12},{12,8},{16,20},{20,16},{24,28},{28,24},{1,5},{5... | collective-permute-start | bytes 1843208 | tf_op jit(solution)/shard_map/ppermute | solution.py:226
  17.8 18.8 %collective-permute-start.4 = (bf16[400,768]{1,0:T(8,128)(2,1)S(1)}, bf16[400,768]{1,0:T(8,128)(2,1)S(1)}, u32[]{:S(2)}, u32[]{:S(2)}) collective-permute-start(bf16[400,768]{1,0:T(8,128)(2,1)S(1)} %line_up_rows.1.own), channel_id=1, source_target_pairs={{0,1},{1,0},{2,3},{3,2},{4,5},{5,4},{6,7},{7,6},{8,9},{9,8},{10,11... | collective-permute-start | bytes 1843208 | tf_op jit(solution)/shard_map/ppermute | solution.py:226
  19.3 17.2 %collective-permute-start.5 = (bf16[400,768]{1,0:T(8,128)(2,1)S(1)}, bf16[400,768]{1,0:T(8,128)(2,1)S(1)}, u32[]{:S(2)}, u32[]{:S(2)}) collective-permute-start(bf16[400,768]{1,0:T(8,128)(2,1)S(1)} %line_up_rows.1.own), channel_id=1, source_target_pairs={{0,2},{1,3},{2,0},{3,1},{4,6},{5,7},{6,4},{7,5},{8,10},{9,11},{10,... | collective-permute-start | bytes 1843208 | tf_op jit(solution)/shard_map/ppermute | solution.py:226
  21.5 14.2 %collective-permute-start.6 = (bf16[96,768]{1,0:T(8,128)(2,1)S(1)}, bf16[96,768]{1,0:T(8,128)(2,1)S(1)}, u32[]{:S(2)}, u32[]{:S(2)}) collective-permute-start(bf16[96,768]{1,0:T(8,128)(2,1)S(1)} %copy-done), channel_id=1, source_target_pairs={{0,8},{4,12},{8,16},{12,20},{16,24},{20,28},{24,0},{28,4},{1,9},{5... | collective-permute-start | bytes 442376 | tf_op jit(solution)/shard_map/ppermute | solution.py:226
  25.2 11.4 %collective-permute-start.7 = (bf16[96,768]{1,0:T(8,128)(2,1)S(1)}, bf16[96,768]{1,0:T(8,128)(2,1)S(1)}, u32[]{:S(2)}, u32[]{:S(2)}) collective-permute-start(bf16[96,768]{1,0:T(8,128)(2,1)S(1)} %copy-done), channel_id=1, source_target_pairs={{0,16},{4,20},{8,24},{12,28},{16,0},{20,4},{24,8},{28,12},{1,17},{... | collective-permute-start | bytes 442376 | tf_op jit(solution)/shard_map/ppermute | solution.py:226
  26.8 9.7 %collective-permute-start.8 = (bf16[96,768]{1,0:T(8,128)(2,1)S(1)}, bf16[96,768]{1,0:T(8,128)(2,1)S(1)}, u32[]{:S(2)}, u32[]{:S(2)}) collective-permute-start(bf16[96,768]{1,0:T(8,128)(2,1)S(1)} %copy-done), channel_id=1, source_target_pairs={{0,24},{4,28},{8,0},{12,4},{16,8},{20,12},{24,16},{28,20},{1,25},{... | collective-permute-start | bytes 442376 | tf_op jit(solution)/shard_map/ppermute | solution.py:226
  36.6 7.0 %collective-permute-start.9 = (bf16[400,768]{1,0:T(8,128)(2,1)S(1)}, bf16[400,768]{1,0:T(8,128)(2,1)S(1)}, u32[]{:S(2)}, u32[]{:S(2)}) collective-permute-start(bf16[400,768]{1,0:T(8,128)(2,1)S(1)} %collective-permute-done.4.own), channel_id=1, source_target_pairs={{0,4},{4,0},{8,12},{12,8},{16,20},{20,16},{24,28},{28,24},{1,5},{5... | collective-permute-start | bytes 1843208 | tf_op jit(solution)/shard_map/ppermute | solution.py:226
  36.7 8.2 %collective-permute-start.10 = (bf16[400,768]{1,0:T(8,128)(2,1)S(1)}, bf16[400,768]{1,0:T(8,128)(2,1)S(1)}, u32[]{:S(2)}, u32[]{:S(2)}) collective-permute-start(bf16[400,768]{1,0:T(8,128)(2,1)S(1)} %collective-permute-done.5.own), channel_id=1, source_target_pairs={{0,4},{4,0},{8,12},{12,8},{16,20},{20,16},{24,28},{28,24},{1,5},{5... | collective-permute-start | bytes 1843208 | tf_op jit(solution)/shard_map/ppermute | solution.py:226
  37.8 16.5 %collective-permute-start.11 = (bf16[400,768]{1,0:T(8,128)(2,1)S(1)}, bf16[400,768]{1,0:T(8,128)(2,1)S(1)}, u32[]{:S(2)}, u32[]{:S(2)}) collective-permute-start(bf16[400,768]{1,0:T(8,128)(2,1)S(1)} %broadcast_select_fusion), channel_id=1, source_target_pairs={{0,1},{1,0},{2,3},{3,2},{4,6},{5,7},{6,4},{7,5},{8,9},{9,8},{10,11... | collective-permute-start | bytes 1843208 | tf_op jit(solution)/shard_map/ppermute | solution.py:226
  38.4 15.9 %collective-permute-start.12 = (bf16[1,4,96,768]{3,2,1,0:T(8,128)(2,1)S(1)}, bf16[1,4,96,768]{3,2,1,0:T(8,128)(2,1)S(1)}, u32[]{:S(2)}, u32[]{:S(2)}) collective-permute-start(bf16[1,4,96,768]{3,2,1,0:T(8,128)(2,1)S(1)} %bitcast.45), channel_id=1, source_target_pairs={{0,1},{1,0},{2,3},{3,2},{4,6},{5,7},{6,4},{7,5},{8,9},{9,8},{10,11... | collective-permute-start | bytes 1769480 | tf_op jit(solution)/shard_map/ppermute | solution.py:226
  39.9 13.7 %collective-permute-start.13 = (bf16[192,384]{1,0:T(8,128)(2,1)S(1)}, bf16[192,384]{1,0:T(8,128)(2,1)S(1)}, u32[]{:S(2)}, u32[]{:S(2)}) collective-permute-start(bf16[192,384]{1,0:T(8,128)(2,1)S(1)} %bitcast.56), channel_id=1, source_target_pairs={{0,8},{4,12},{8,16},{12,20},{16,24},{20,28},{24,0},{28,4},{1,9},{5... | collective-permute-start | bytes 442376 | tf_op jit(solution)/shard_map/ppermute | solution.py:226
  43.5 10.7 %collective-permute-start.14 = (bf16[192,384]{1,0:T(8,128)(2,1)S(1)}, bf16[192,384]{1,0:T(8,128)(2,1)S(1)}, u32[]{:S(2)}, u32[]{:S(2)}) collective-permute-start(bf16[192,384]{1,0:T(8,128)(2,1)S(1)} %bitcast.57), channel_id=1, source_target_pairs={{0,16},{4,20},{8,24},{12,28},{16,0},{20,4},{24,8},{28,12},{1,17},{... | collective-permute-start | bytes 442376 | tf_op jit(solution)/shard_map/ppermute | solution.py:226
  44.9 9.4 %collective-permute-start.15 = (bf16[192,384]{1,0:T(8,128)(2,1)S(1)}, bf16[192,384]{1,0:T(8,128)(2,1)S(1)}, u32[]{:S(2)}, u32[]{:S(2)}) collective-permute-start(bf16[192,384]{1,0:T(8,128)(2,1)S(1)} %bitcast.58), channel_id=1, source_target_pairs={{0,24},{4,28},{8,0},{12,4},{16,8},{20,12},{24,16},{28,20},{1,25},{... | collective-permute-start | bytes 442376 | tf_op jit(solution)/shard_map/ppermute | solution.py:226
  54.5 16.3 %collective-permute-start.17 = (bf16[2,4,96,768]{3,2,1,0:T(8,128)(2,1)S(1)}, bf16[2,4,96,768]{3,2,1,0:T(8,128)(2,1)S(1)}, u32[]{:S(2)}, u32[]{:S(2)}) collective-permute-start(bf16[2,4,96,768]{3,2,1,0:T(8,128)(2,1)S(1)} %pad_maximum_fusion.u0), channel_id=1, source_target_pairs={{0,2},{1,3},{2,0},{3,1},{4,5},{5,4},{6,7},{7,6},{8,10},{9,11},{10,... | collective-permute-start | bytes 3538952 | tf_op jit(solution)/shard_map/ppermute | solution.py:226
  55.1 15.7 %collective-permute-start.18 = (bf16[2,4,96,768]{3,2,1,0:T(8,128)(2,1)S(1)}, bf16[2,4,96,768]{3,2,1,0:T(8,128)(2,1)S(1)}, u32[]{:S(2)}, u32[]{:S(2)}) collective-permute-start(bf16[2,4,96,768]{3,2,1,0:T(8,128)(2,1)S(1)} %pad_maximum_fusion.u0), channel_id=1, source_target_pairs={{0,4},{4,0},{8,12},{12,8},{16,20},{20,16},{24,28},{28,24},{1,5},{5... | collective-permute-start | bytes 3538952 | tf_op jit(solution)/shard_map/ppermute | solution.py:226
  55.1 8.1 %collective-permute-start.16 = (bf16[400,768]{1,0:T(8,128)(2,1)S(1)}, bf16[400,768]{1,0:T(8,128)(2,1)S(1)}, u32[]{:S(2)}, u32[]{:S(2)}) collective-permute-start(bf16[400,768]{1,0:T(8,128)(2,1)S(1)} %collective-permute-done.11.own), channel_id=1, source_target_pairs={{0,4},{4,0},{8,12},{12,8},{16,20},{20,16},{24,28},{28,24},{1,5},{5... | collective-permute-start | bytes 1843208 | tf_op jit(solution)/shard_map/ppermute | solution.py:1303
  70.8 9.9 %collective-permute-start.19 = (bf16[2,4,96,768]{3,2,1,0:T(8,128)(2,1)S(1)}, bf16[2,4,96,768]{3,2,1,0:T(8,128)(2,1)S(1)}, u32[]{:S(2)}, u32[]{:S(2)}) collective-permute-start(bf16[2,4,96,768]{3,2,1,0:T(8,128)(2,1)S(1)} %collective-permute-done.17.u1), channel_id=1, source_target_pairs={{0,4},{4,0},{8,12},{12,8},{16,20},{20,16},{24,28},{28,24},{1,5},{5... | collective-permute-start | bytes 3538952 | tf_op jit(solution)/shard_map/ppermute | solution.py:226
  70.8 9.9 %collective-permute-start.20 = (bf16[1,4,192,384]{3,2,1,0:T(8,128)(2,1)S(1)}, bf16[1,4,192,384]{3,2,1,0:T(8,128)(2,1)S(1)}, u32[]{:S(2)}, u32[]{:S(2)}) collective-permute-start(bf16[1,4,192,384]{3,2,1,0:T(8,128)(2,1)S(1)} %maximum_bitcast_fusion), channel_id=1, source_target_pairs={{0,1},{1,0},{2,3},{3,2},{4,6},{5,7},{6,4},{7,5},{8,9},{9,8},{10,11... | collective-permute-start | bytes 1769480 | tf_op jit(solution)/shard_map/ppermute | solution.py:226
  80.8 16.3 %collective-permute-start.21 = (bf16[2,4,192,384]{3,2,1,0:T(8,128)(2,1)S(1)}, bf16[2,4,192,384]{3,2,1,0:T(8,128)(2,1)S(1)}, u32[]{:S(2)}, u32[]{:S(2)}) collective-permute-start(bf16[2,4,192,384]{3,2,1,0:T(8,128)(2,1)S(1)} %pad_maximum_fusion.1.d0), channel_id=1, source_target_pairs={{0,2},{1,3},{2,0},{3,1},{4,5},{5,4},{6,7},{7,6},{8,10},{9,11},{10,... | collective-permute-start | bytes 3538952 | tf_op jit(solution)/shard_map/ppermute | solution.py:226
  82.3 14.8 %collective-permute-start.22 = (bf16[2,4,192,384]{3,2,1,0:T(8,128)(2,1)S(1)}, bf16[2,4,192,384]{3,2,1,0:T(8,128)(2,1)S(1)}, u32[]{:S(2)}, u32[]{:S(2)}) collective-permute-start(bf16[2,4,192,384]{3,2,1,0:T(8,128)(2,1)S(1)} %pad_maximum_fusion.1.d0), channel_id=1, source_target_pairs={{0,4},{4,0},{8,12},{12,8},{16,20},{20,16},{24,28},{28,24},{1,5},{5... | collective-permute-start | bytes 3538952 | tf_op jit(solution)/shard_map/ppermute | solution.py:226
  97.1 2.8 %collective-permute-start.23 = (bf16[2,4,192,384]{3,2,1,0:T(8,128)(2,1)S(1)}, bf16[2,4,192,384]{3,2,1,0:T(8,128)(2,1)S(1)}, u32[]{:S(2)}, u32[]{:S(2)}) collective-permute-start(bf16[2,4,192,384]{3,2,1,0:T(8,128)(2,1)S(1)} %collective-permute-done.21.d1), channel_id=1, source_target_pairs={{0,4},{4,0},{8,12},{12,8},{16,20},{20,16},{24,28},{28,24},{1,5},{5... | collective-permute-start | bytes 3538952 | tf_op jit(solution)/shard_map/ppermute | solution.py:226
  122.1 13.9 %collective-permute-start.24 = (bf16[4,4,96,768]{3,2,1,0:T(8,128)(2,1)}, bf16[4,4,96,768]{3,2,1,0:T(8,128)(2,1)S(1)}, u32[]{:S(2)}, u32[]{:S(2)}) collective-permute-start(bf16[4,4,96,768]{3,2,1,0:T(8,128)(2,1)} %get-tuple-element.300), channel_id=1, source_target_pairs={{0,4},{4,0},{8,12},{12,8},{16,20},{20,16},{24,28},{28,24},{1,5},{5... | collective-permute-start | bytes 7077896 | tf_op jit(solution)/shard_map/ppermute | solution.py:226
  122.3 13.8 %copy-start.7 = (bf16[4,4,96,768]{3,2,1,0:T(8,128)(2,1)S(1)}, bf16[4,4,96,768]{3,2,1,0:T(8,128)(2,1)}, u32[]{:S(2)}) copy-start(bf16[4,4,96,768]{3,2,1,0:T(8,128)(2,1)} %get-tuple-element.290) | copy-start | bytes 7077892
  136.8 16.3 %collective-permute-start.25 = (bf16[2,4,96,768]{3,2,1,0:T(8,128)(2,1)S(1)}, bf16[2,4,96,768]{3,2,1,0:T(8,128)(2,1)S(1)}, u32[]{:S(2)}, u32[]{:S(2)}) collective-permute-start(bf16[2,4,96,768]{3,2,1,0:T(8,128)(2,1)S(1)} %get-tuple-element.311), channel_id=1, source_target_pairs={{0,2},{1,3},{2,0},{3,1},{4,5},{5,4},{6,7},{7,6},{8,10},{9,11},{10,... | collective-permute-start | bytes 3538952 | tf_op jit(solution)/shard_map/ppermute | solution.py:226
  154.7 10.6 %collective-permute-start.27 = (bf16[4,4,96,768]{3,2,1,0:T(8,128)(2,1)S(1)}, bf16[4,4,96,768]{3,2,1,0:T(8,128)(2,1)S(1)}, u32[]{:S(2)}, u32[]{:S(2)}) collective-permute-start(bf16[4,4,96,768]{3,2,1,0:T(8,128)(2,1)S(1)} %copy-done.10), channel_id=1, source_target_pairs={{0,4},{4,0},{8,12},{12,8},{16,20},{20,16},{24,28},{28,24},{1,5},{5... | collective-permute-start | bytes 7077896 | tf_op jit(solution)/shard_map/ppermute | solution.py:226
  154.7 10.6 %collective-permute-start.26 = (bf16[1,4,96,768]{3,2,1,0:T(8,128)(2,1)S(1)}, bf16[1,4,96,768]{3,2,1,0:T(8,128)(2,1)S(1)}, u32[]{:S(2)}, u32[]{:S(2)}) collective-permute-start(bf16[1,4,96,768]{3,2,1,0:T(8,128)(2,1)S(1)} %get-tuple-element.317), channel_id=1, source_target_pairs={{0,1},{1,0},{2,3},{3,2},{4,6},{5,7},{6,4},{7,5},{8,9},{9,8},{10,11... | collective-permute-start | bytes 1769480 | tf_op jit(solution)/shard_map/ppermute | solution.py:226
  166.2 19.4 %collective-permute-start.28 = (bf16[2,4,96,768]{3,2,1,0:T(8,128)(2,1)S(1)}, bf16[2,4,96,768]{3,2,1,0:T(8,128)(2,1)S(1)}, u32[]{:S(2)}, u32[]{:S(2)}) collective-permute-start(bf16[2,4,96,768]{3,2,1,0:T(8,128)(2,1)S(1)} %get-tuple-element.333), channel_id=1, source_target_pairs={{0,2},{1,3},{2,0},{3,1},{4,5},{5,4},{6,7},{7,6},{8,10},{9,11},{10,... | collective-permute-start | bytes 3538952 | tf_op jit(solution)/shard_map/ppermute | solution.py:226
  167.4 13.2 %collective-permute-start.29 = (bf16[96,768]{1,0:T(8,128)(2,1)S(1)}, bf16[96,768]{1,0:T(8,128)(2,1)S(1)}, u32[]{:S(2)}, u32[]{:S(2)}) collective-permute-start(bf16[96,768]{1,0:T(8,128)(2,1)S(1)} %get-tuple-element.334), channel_id=1, source_target_pairs={{0,24},{4,28},{8,0},{12,4},{16,8},{20,12},{24,16},{28,20},{1,25},{... | collective-permute-start | bytes 442376 | tf_op jit(solution)/shard_map/ppermute | solution.py:226
  171.9 13.7 %collective-permute-start.30 = (bf16[96,768]{1,0:T(8,128)(2,1)S(1)}, bf16[96,768]{1,0:T(8,128)(2,1)S(1)}, u32[]{:S(2)}, u32[]{:S(2)}) collective-permute-start(bf16[96,768]{1,0:T(8,128)(2,1)S(1)} %get-tuple-element.335), channel_id=1, source_target_pairs={{0,16},{4,20},{8,24},{12,28},{16,0},{20,4},{24,8},{28,12},{1,17},{... | collective-permute-start | bytes 442376 | tf_op jit(solution)/shard_map/ppermute | solution.py:226
  172.4 13.2 %collective-permute-start.31 = (bf16[96,768]{1,0:T(8,128)(2,1)S(1)}, bf16[96,768]{1,0:T(8,128)(2,1)S(1)}, u32[]{:S(2)}, u32[]{:S(2)}) collective-permute-start(bf16[96,768]{1,0:T(8,128)(2,1)S(1)} %get-tuple-element.336), channel_id=1, source_target_pairs={{0,8},{4,12},{8,16},{12,20},{16,24},{20,28},{24,0},{28,4},{1,9},{5... | collective-permute-start | bytes 442376 | tf_op jit(solution)/shard_map/ppermute | solution.py:226
  185.9 9.9 %collective-permute-start.33 = (bf16[1,4,96,768]{3,2,1,0:T(8,128)(2,1)S(1)}, bf16[1,4,96,768]{3,2,1,0:T(8,128)(2,1)S(1)}, u32[]{:S(2)}, u32[]{:S(2)}) collective-permute-start(bf16[1,4,96,768]{3,2,1,0:T(8,128)(2,1)S(1)} %get-tuple-element.344), channel_id=1, source_target_pairs={{0,1},{1,0},{2,3},{3,2},{4,6},{5,7},{6,4},{7,5},{8,9},{9,8},{10,11... | collective-permute-start | bytes 1769480 | tf_op jit(solution)/shard_map/ppermute | solution.py:226
  187.4 8.5 %collective-permute-start.32 = (bf16[400,768]{1,0:T(8,128)(2,1)S(1)}, bf16[400,768]{1,0:T(8,128)(2,1)S(1)}, u32[]{:S(2)}, u32[]{:S(2)}) collective-permute-start(bf16[400,768]{1,0:T(8,128)(2,1)S(1)} %get-tuple-element.343), channel_id=1, source_target_pairs={{0,4},{4,0},{8,12},{12,8},{16,20},{20,16},{24,28},{28,24},{1,5},{5... | collective-permute-start | bytes 1843208 | tf_op jit(solution)/shard_map/ppermute | solution.py:226
  196.5 11.4 %collective-permute-start.35 = (bf16[96,768]{1,0:T(8,128)(2,1)S(1)}, bf16[96,768]{1,0:T(8,128)(2,1)S(1)}, u32[]{:S(2)}, u32[]{:S(2)}) collective-permute-start(bf16[96,768]{1,0:T(8,128)(2,1)S(1)} %get-tuple-element.353), channel_id=1, source_target_pairs={{0,24},{4,28},{8,0},{12,4},{16,8},{20,12},{24,16},{28,20},{1,25},{... | collective-permute-start | bytes 442376 | tf_op jit(solution)/shard_map/ppermute | solution.py:226
  197.7 10.2 %collective-permute-start.36 = (bf16[96,768]{1,0:T(8,128)(2,1)S(1)}, bf16[96,768]{1,0:T(8,128)(2,1)S(1)}, u32[]{:S(2)}, u32[]{:S(2)}) collective-permute-start(bf16[96,768]{1,0:T(8,128)(2,1)S(1)} %get-tuple-element.354), channel_id=1, source_target_pairs={{0,8},{4,12},{8,16},{12,20},{16,24},{20,28},{24,0},{28,4},{1,9},{5... | collective-permute-start | bytes 442376 | tf_op jit(solution)/shard_map/ppermute | solution.py:226
  198.6 10.1 %collective-permute-start.34 = (bf16[400,768]{1,0:T(8,128)(2,1)S(1)}, bf16[400,768]{1,0:T(8,128)(2,1)S(1)}, u32[]{:S(2)}, u32[]{:S(2)}) collective-permute-start(bf16[400,768]{1,0:T(8,128)(2,1)S(1)} %add_convert_fusion.6), channel_id=1, source_target_pairs={{0,1},{1,0},{2,3},{3,2},{4,6},{5,7},{6,4},{7,5},{8,9},{9,8},{10,11... | collective-permute-start | bytes 1843208 | tf_op jit(solution)/shard_map/ppermute | solution.py:226
  199.7 9.0 %collective-permute-start.37 = (bf16[400,768]{1,0:T(8,128)(2,1)S(1)}, bf16[400,768]{1,0:T(8,128)(2,1)S(1)}, u32[]{:S(2)}, u32[]{:S(2)}) collective-permute-start(bf16[400,768]{1,0:T(8,128)(2,1)S(1)} %get-tuple-element.355), channel_id=1, source_target_pairs={{0,4},{4,0},{8,12},{12,8},{16,20},{20,16},{24,28},{28,24},{1,5},{5... | collective-permute-start | bytes 1843208 | tf_op jit(solution)/shard_map/ppermute | solution.py:226
  208.7 2.0 collective-permute-start.38
  211.3 11.5 %collective-permute-start.41 = (bf16[96,768]{1,0:T(8,128)(2,1)S(1)}, bf16[96,768]{1,0:T(8,128)(2,1)S(1)}, u32[]{:S(2)}, u32[]{:S(2)}) collective-permute-start(bf16[96,768]{1,0:T(8,128)(2,1)S(1)} %get-tuple-element.369), channel_id=1, source_target_pairs={{0,16},{4,20},{8,24},{12,28},{16,0},{20,4},{24,8},{28,12},{1,17},{... | collective-permute-start | bytes 442376 | tf_op jit(solution)/shard_map/ppermute | solution.py:226
  212.9 15.6 %collective-permute-start.39 = (bf16[400,768]{1,0:T(8,128)(2,1)S(1)}, bf16[400,768]{1,0:T(8,128)(2,1)S(1)}, u32[]{:S(2)}, u32[]{:S(2)}) collective-permute-start(bf16[400,768]{1,0:T(8,128)(2,1)S(1)} %get-tuple-element.367), channel_id=1, source_target_pairs={{0,1},{1,0},{2,3},{3,2},{4,5},{5,4},{6,7},{7,6},{8,9},{9,8},{10,11... | collective-permute-start | bytes 1843208 | tf_op jit(solution)/shard_map/ppermute | solution.py:226
  214.1 15.3 %collective-permute-start.40 = (bf16[400,768]{1,0:T(8,128)(2,1)S(1)}, bf16[400,768]{1,0:T(8,128)(2,1)S(1)}, u32[]{:S(2)}, u32[]{:S(2)}) collective-permute-start(bf16[400,768]{1,0:T(8,128)(2,1)S(1)} %get-tuple-element.368), channel_id=1, source_target_pairs={{0,2},{1,3},{2,0},{3,1},{4,6},{5,7},{6,4},{7,5},{8,10},{9,11},{10,... | collective-permute-start | bytes 1843208 | tf_op jit(solution)/shard_map/ppermute | solution.py:226
  229.4 2.0 collective-permute-start.42
  232.3 14.3 %collective-permute-start.43 = (bf16[112,768]{1,0:T(8,128)(2,1)S(1)}, bf16[112,768]{1,0:T(8,128)(2,1)S(1)}, u32[]{:S(2)}, u32[]{:S(2)}) collective-permute-start(bf16[112,768]{1,0:T(8,128)(2,1)S(1)} %get-tuple-element.384), channel_id=1, source_target_pairs={{0,24},{4,28},{8,0},{12,4},{16,8},{20,12},{24,16},{28,20},{1,25},{... | collective-permute-start | bytes 516104 | tf_op jit(solution)/shard_map/ppermute | solution.py:226
  234.2 17.1 %collective-permute-start.44 = (bf16[112,768]{1,0:T(8,128)(2,1)S(1)}, bf16[112,768]{1,0:T(8,128)(2,1)S(1)}, u32[]{:S(2)}, u32[]{:S(2)}) collective-permute-start(bf16[112,768]{1,0:T(8,128)(2,1)S(1)} %get-tuple-element.385), channel_id=1, source_target_pairs={{0,16},{4,20},{8,24},{12,28},{16,0},{20,4},{24,8},{28,12},{1,17},{... | collective-permute-start | bytes 516104 | tf_op jit(solution)/shard_map/ppermute | solution.py:226
  235.8 15.5 %collective-permute-start.45 = (bf16[112,768]{1,0:T(8,128)(2,1)S(1)}, bf16[112,768]{1,0:T(8,128)(2,1)S(1)}, u32[]{:S(2)}, u32[]{:S(2)}) collective-permute-start(bf16[112,768]{1,0:T(8,128)(2,1)S(1)} %get-tuple-element.386), channel_id=1, source_target_pairs={{0,8},{4,12},{8,16},{12,20},{16,24},{20,28},{24,0},{28,4},{1,9},{5... | collective-permute-start | bytes 516104 | tf_op jit(solution)/shard_map/ppermute | solution.py:226
  (9 other events, 50.7 us)

commit v4 on v3

--- a/solution.py
+++ b/solution.py
@@ -634,7 +634,7 @@
 
     rows = pl.ds(pl.multiple_of(step * PLEN, PLEN), PLEN)
     weights = weights_here[:, :, :, :USED].reshape(2 * depth * tall, USED)
-    qkv = dot(x[...], weights) + bias
+    qkv = dot(x[rows, :], weights) + bias
     tiles = [qkv[:, n * PAIR:(n + 1) * PAIR].astype(bf16) for n in range(5)]
     tiles[0] = tiles[0] * jnp.array(scale, bf16)
     tiles[3] = jnp.where(low_half, tiles[3] * jnp.array(scale, bf16), tiles[3])
@@ -684,7 +684,7 @@
     any_space = pl.BlockSpec(memory_space=pl.ANY)
     return call(
         functools.partial(attend_one_kernel, away), "attend", (t // PLEN,),
-        [pl.BlockSpec((PLEN, d), lambda s, *_: (s, 0)), any_space, any_space] + [held()] * len(ext)
+        [held(), any_space, any_space] + [held()] * len(ext)
         + [any_space] * len(shared),
         [
             pl.BlockSpec((1, PLEN, narrow), lambda s, place, *_: (j(place), s, 0)), any_space,
@@ -1303,11 +1303,12 @@
             pair_c = lax.ppermute(own_c, "dp", across_cores())
             *part, kept_2, lse_2 = one(2)(place, *run, own_y, pair_y, ext, shared)
             *part, kept_3, lse_3 = one(3)(place, *run, own_c, pair_c, ext, part)
-            return [*part, kept_2, lse_2, kept_3, lse_3]
-
-        *shared, kept_2, lse_2, kept_3, lse_3 = beside([to_u], last_two, (place, own_c), out=5)
+            normal = attended(tokens, part[0], part[1].reshape(fsdp, d, width), 2, part[2])
+            return [*part, kept_2, lse_2, kept_3, lse_3, *normal]
+
+        results = beside([to_u, to_d], last_two, (place, own_c), out=12)
+        shared, (kept_2, lse_2, kept_3, lse_3), normal = results[:3], results[3:7], results[7:]
         context, weights, slabs = shared
-        ow, last = weights.reshape(fsdp, d, width), 2
         count, head_of = 8 * fsdp, lambda r: jnp.where(r % 8 < HEADS, r // 8 * HEADS + r % 8, -1)
     else:
         block = jnp.concatenate([
@@ -1325,11 +1326,20 @@
         context, ow, last = context[None], weights[3:], 0
         count, head_of = PAIR, lambda r: 2 * (r % HD) + r // HD
 
-    n1, r1, low, low_t, ow, given = beside(
-        [to_u, to_d], attended, (tokens, context, ow, last, slabs), key=4, out=5
-    )
-    finish(to_u)
-    active, slope, uw = beside([to_d], up, (place, low, slabs, to_u.blocks))
+    if by_head:
+        n1, r1, low, low_t, ow, given = normal
+
+        def up_now(place, low, slabs, sent):
+            got = lax.ppermute(sent, "dp", across_cores())
+            return up(place, low, slabs, [*to_u.own, to_u.other, got])
+
+        active, slope, uw = beside([to_d], up_now, (place, low, slabs, to_u.own[1]))
+    else:
+        n1, r1, low, low_t, ow, given = beside(
+            [to_u, to_d], attended, (tokens, context, ow, last, slabs), key=4, out=5
+        )
+        finish(to_u)
+        active, slope, uw = beside([to_d], up, (place, low, slabs, to_u.blocks))
     finish(to_d)
     cuts = context.shape[0]
     out, pooled, mixed, branch, down_vectors, send_d, keep_d, dw = down(

time: 258 us -> 254 us (0.984)
  Pallas kernels: 156 us -> 152 us
    pallas_call x20, Pallas kernels: 156 us -> 152 us  [run_far(): return run(*args[:prefetch], *given)]
    ppermute x45 -> x44, starting transfers between devices: 48.6 us -> 47.7 us  [beside(): lax.ppermute(v, axis, perm)]
    ppermute x45 -> x44, waiting for transfers between devices: 36.6 us -> 36.6 us  [beside(): lax.ppermute(v, axis, perm)]
  transfers between devices with their start and end apart: 46 -> 46, of which waited for: 18 -> 17; matrix products, arithmetic and copies ran while one was open for 1% -> 2% of each run, Pallas kernels for 52% -> 50%
where the time goes in v4:
time: 254 us; the launch traced here: 249 us
  Pallas kernels  152 us (60%)
  starting transfers between devices  47.8 us (19%)
  waiting for transfers between devices  38.4 us (15%)
  other arithmetic  5.07 us (2%)
  local copies, waits for them, and re-layouts  4.6 us (2%)
    pallas_call x20, Pallas kernels, run_far(): return run(*args[:prefetch], *given)  152 us
    ppermute x44, starting transfers between devices, beside(): lax.ppermute(v, axis, perm)  47.7 us
    ppermute x44, waiting for transfers between devices, beside(): lax.ppermute(v, axis, perm)  36.6 us
  transfers between devices with their start and end apart: 46, of which 17 were waited for; matrix products, arithmetic and copies ran while one was open for 2% of the time, Pallas kernels for 50%

profile of v4, /device:TPU:0, one launch (start us, length us, event | category | flops | bytes accessed | tf_op | source)
XLA Modules:
  0.0 249.5 jit_solution(13310798717276998175)
XLA Ops:
  1.7 3.1 %collective-permute-start = (bf16[96,768]{1,0:T(8,128)(2,1)S(1)}, bf16[96,768]{1,0:T(8,128)(2,1)S(1)}, u32[]{:S(2)}, u32[]{:S(2)}) collective-permute-start(bf16[96,768]{1,0:T(8,128)(2,1)S(1)} %get-tuple-element.215.refs_0_), channel_id=1, source_target_pairs={{0,8},{4,12},{8,16},{12,20},{16,24},{20,28},{24,0},{28,4},{1,9},{5... | collective-permute-start | bytes 442376 | tf_op jit(solution)/shard_map/ppermute | solution.py:226
  4.8 2.6 %collective-permute-start.1 = (bf16[96,768]{1,0:T(8,128)(2,1)S(1)}, bf16[96,768]{1,0:T(8,128)(2,1)S(1)}, u32[]{:S(2)}, u32[]{:S(2)}) collective-permute-start(bf16[96,768]{1,0:T(8,128)(2,1)S(1)} %get-tuple-element.215.refs_0_), channel_id=1, source_target_pairs={{0,16},{4,20},{8,24},{12,28},{16,0},{20,4},{24,8},{28,12},{1,17},{... | collective-permute-start | bytes 442376 | tf_op jit(solution)/shard_map/ppermute | solution.py:226
  7.4 1.3 collective-permute-start.2
  8.8 2.7 %copy.49 = bf16[1024,768]{0,1:T(8,128)(2,1)} copy(bf16[1024,768]{1,0:T(8,128)(2,1)} %x.9) | data formatting | bytes 3145728 | tf_op jit(solution)/shard_map/optimization_barrier | solution.py:221
  11.6 5.4 %collective-permute-done.1.refs_2_ = bf16[96,768]{1,0:T(8,128)(2,1)S(1)} collective-permute-done((bf16[96,768]{1,0:T(8,128)(2,1)S(1)}, bf16[96,768]{1,0:T(8,128)(2,1)S(1)}, u32[]{:S(2)}, u32[]{:S(2)}) %collective-permute-start.1) | collective-permute-done | bytes 147488 | tf_op jit(solution)/shard_map/ppermute | solution.py:226
  17.8 1.6 collective-permute-start.4
  19.3 1.5 collective-permute-start.5
  21.5 3.7 %collective-permute-start.6 = (bf16[96,768]{1,0:T(8,128)(2,1)S(1)}, bf16[96,768]{1,0:T(8,128)(2,1)S(1)}, u32[]{:S(2)}, u32[]{:S(2)}) collective-permute-start(bf16[96,768]{1,0:T(8,128)(2,1)S(1)} %copy-done.1), channel_id=1, source_target_pairs={{0,8},{4,12},{8,16},{12,20},{16,24},{20,28},{24,0},{28,4},{1,9},{5... | collective-permute-start | bytes 442376 | tf_op jit(solution)/shard_map/ppermute | solution.py:226
  25.2 1.6 collective-permute-start.7
  27.6 7.0 %attend.4 = (bf16[4,1024,192]{2,1,0:T(8,128)(2,1)}, bf16[4,4,2,96,768]{4,3,2,1,0:T(8,128)(2,1)}, bf16[4,16,768]{2,1,0:T(8,128)(2,1)}, bf16[1024,640]{1,0:T(8,128...) custom-call(s32[29]{0:T(128)S(1)} %concatenate.12.place, ...), custom_call_target="tpu_custom_call" | custom-call | flops 5000000000 | bytes 8000000 | tf_op jit(solution)/shard_map/attend/pallas_call | solution.py:79
  34.6 2.0 collective-permute-done.7.refs_2_
  38.4 1.5 collective-permute-start.12
  39.9 3.6 %collective-permute-start.13 = (bf16[192,384]{1,0:T(8,128)(2,1)S(1)}, bf16[192,384]{1,0:T(8,128)(2,1)S(1)}, u32[]{:S(2)}, u32[]{:S(2)}) collective-permute-start(bf16[192,384]{1,0:T(8,128)(2,1)S(1)} %bitcast.56), channel_id=1, source_target_pairs={{0,8},{4,12},{8,16},{12,20},{16,24},{20,28},{24,0},{28,4},{1,9},{5... | collective-permute-start | bytes 442376 | tf_op jit(solution)/shard_map/ppermute | solution.py:226
  43.5 1.3 collective-permute-start.14
  44.9 1.4 collective-permute-start.15
  46.3 6.3 %attend.5 = (bf16[4,1024,192]{2,1,0:T(8,128)(2,1)}, bf16[4,4,2,96,768]{4,3,2,1,0:T(8,128)(2,1)}, bf16[4,16,768]{2,1,0:T(8,128)(2,1)}, bf16[1024,640]{1,0:T(8,128)(2,1)}, f32[8,1024]{1,0:T(8,128)}) custom-call(s32[29]{0:T(128)S(1)} %concatenate.12.place, s32[1]{0:T(128)S(6)} %copy.62.bucket, ...), custom_call_target="tpu_custom_call", output_to_operand_aliasing={{0}: (8, {}), {1}: (9, {}), {2}: (10, {})} | custom-call | flops 5000000000 | bytes 8000000 | tf_op jit(solution)/shard_map/attend/pallas_call | solution.py:79
  52.6 1.7 collective-permute-done.14
  55.7 6.3 %attend.6 = (bf16[4,1024,192]{2,1,0:T(8,128)(2,1)}, bf16[4,4,2,96,768]{4,3,2,1,0:T(8,128)(2,1)}, bf16[4,16,768]{2,1,0:T(8,128)(2,1)}, bf16[1024,640]{1,0:T(8,128)(2,1)}, f32[8,1024]{1,0:T(8,128)}) custom-call(s32[29]{0:T(128)S(1)} %concatenate.12.place, s32[1]{0:T(128)S(6)} %copy.62.bucket, ...), custom_call_target="tpu_custom_call", output_to_operand_aliasing={{0}: (8, {}), {1}: (9, {}), {2}: (10, {})} | custom-call | flops 5000000000 | bytes 8000000 | tf_op jit(solution)/shard_map/attend/pallas_call | solution.py:79
  62.0 6.3 %attend.7 = (bf16[4,1024,192]{2,1,0:T(8,128)(2,1)}, bf16[4,4,2,96,768]{4,3,2,1,0:T(8,128)(2,1)}, bf16[4,16,768]{2,1,0:T(8,128)(2,1)}, bf16[1024,640]{1,0:T(8,128)(2,1)}, f32[8,1024]{1,0:T(8,128)}) custom-call(s32[29]{0:T(128)S(1)} %concatenate.12.place, s32[1]{0:T(128)S(6)} %copy.62.bucket, ...), custom_call_target="tpu_custom_call", output_to_operand_aliasing={{0}: (8, {}), {1}: (9, {}), {2}: (10, {})} | custom-call | flops 5000000000 | bytes 8000000 | tf_op jit(solution)/shard_map/attend/pallas_call | solution.py:79
  68.3 5.8 %attended.1 = (f32[1024,768]{1,0:T(8,128)S(1)}, f32[1024,128]{1,0:T(8,128)S(1)}, bf16[1024,768]{1,0:T(8,128)(2,1)S(1)}, bf16[768,1024]{1,0:T(8,128)(2,1)S(1)}, b...) custom-call(bf16[1024,768]{1,0:T(8,128)(2,1)} %x.9, bf16[4,1024,192]{2,1,0:T(8,128)(2,1)} %get-tuple-element.260.context, ...), custom_call_target="tpu_custom_call" | custom-call | flops 3000000000 | bytes 10000000 | tf_op jit(solution)/shard_map/attended/pallas_call | solution.py:79
  74.1 2.6 %collective-permute-done.17.u1 = bf16[2,4,96,768]{3,2,1,0:T(8,128)(2,1)S(1)} collective-permute-done((bf16[2,4,96,768]{3,2,1,0:T(8,128)(2,1)S(1)}, bf16[2,4,96,768]{3,2,1,0:T(8,128)(2,1)S(1)}, u32[]{:S(2)}, u32[]{:S(2)}) %collective-permute-start.17) | collective-permute-done | bytes 1179680 | tf_op jit(solution)/shard_map/ppermute | solution.py:226
  77.7 1.9 collective-permute-done.20.u3
  79.6 13.6 %up.1 = (bf16[4,1024,768]{2,1,0:T(8,128)(2,1)}, bf16[4,1024,768]{2,1,0:T(8,128)(2,1)}, bf16[4,4,2,96,768]{4,3,2,1,0:T(8,128)(2,1)}) custom-call(s32[29]{0:T(128)S(1)} %concatenate.12.place, bf16[1024,768]{1,0:T(8,128)(2,1)S(1)} %get-tuple-element.269.low, bf16[4,16,768]{2,1,0:T(8,128)(2,1)} %get-tuple-element.262.slabs, ...), custom_call_target="tpu_custom_call" | custom-call | flops 12000000000 | bytes 30000000 | tf_op jit(solution)/shard_map/up/pallas_call | solution.py:79
  93.4 2.7 %collective-permute-done.23.d3 = bf16[2,4,192,384]{3,2,1,0:T(8,128)(2,1)S(1)} collective-permute-done((bf16[2,4,192,384]{3,2,1,0:T(8,128)(2,1)S(1)}, bf16[2,4,192,384]{3,2,1,0:T(8,128)(2,1)S(1)}, u32[]{:S(2)}, u32[]{:S(2)}) %collective-permute-start.23) | collective-permute-done | bytes 1179680 | tf_op jit(solution)/shard_map/ppermute | solution.py:226
  96.1 22.2 %down.1 = (bf16[1024,768]{1,0:T(8,128)(2,1)}, f32[8,768]{1,0:T(8,128)}, f32[1024,768]{1,0:T(8,128)S(1)}, bf16[1024,768]{1,0:T(8,128)(2,1)S(1)}, f32[4,8,192]{2,1...) custom-call(s32[29]{0:T(128)S(1)} %concatenate.12.place, ...), custom_call_target="tpu_custom_call" | custom-call | flops 12000000000 | bytes 35000000 | tf_op jit(solution)/shard_map/down/pallas_call | solution.py:79
  118.5 13.8 %feed_back.2 = (bf16[4,4,96,768]{3,2,1,0:T(8,128)(2,1)}, bf16[4,4,96,768]{3,2,1,0:T(8,128)(2,1)}, f32[4,1,768]{2,1,0:T(1,128)}, f32[1024,768]{1,0:T(8,128)S(1)}) custom-call(s32[29]{0:T(128)S(1)} %concatenate.12.place, bf16[1024,768]{1,0:T(8,128)(2,1)S(1)} %get-tuple-element.285.branch, bf16[4,1024,768]{2,1,0:T(8,128)(2,1)} %get-tuple-element.286.slope, ...), custom_call_target="tpu_custom_call" | custom-call | flops 15000000512 | bytes 35000000 | tf_op jit(solution)/shard_map/feed_back/pallas_call | solution.py:79
  133.6 13.6 %feed_back.3 = (bf16[4,4,96,768]{3,2,1,0:T(8,128)(2,1)}, bf16[4,4,96,768]{3,2,1,0:T(8,128)(2,1)}, f32[4,1,768]{2,1,0:T(1,128)}, f32[1024,768]{1,0:T(8,128)S(1)}) custom-call(s32[29]{0:T(128)S(1)} %concatenate.12.place, bf16[1024,768]{1,0:T(8,128)(2,1)S(1)} %get-tuple-element.285.branch, ...), custom_call_target="tpu_custom_call", output_to_operand_aliasing={{0}: (7, {}), {1}: (8, {}), {2}: (9, {})} | custom-call | flops 15000000512 | bytes 35000000 | tf_op jit(solution)/shard_map/feed_back/pallas_call | solution.py:79
  147.1 2.1 collective-permute-done.25
  149.5 1.4 copy-done.11
  151.3 9.8 %inner_back.1 = (f32[1024,768]{1,0:T(8,128)}, f32[4,8,192]{2,1,0:T(8,128)}, bf16[4,768,192]{2,1,0:T(8,128)(2,1)}, bf16[4,1024,192]{2,1,0:T(8,128)(2,1)}, f32[32,1024]{1,0:T(8,128)}) custom-call(f32[1024,768]{1,0:T(8,128)S(1)} %get-tuple-element.300.grad_normed, f32[1024,768]{1,0:T(8,128)S(1)} %get-tuple-element.276.n1, ...), custom_call_target="tpu_custom_call" | custom-call | flops 4000000000 | bytes 10000000 | tf_op jit(solution)/shard_map/inner_back/pallas_call | solution.py:79
  162.8 4.6 %collective-permute-start.29 = (bf16[96,768]{1,0:T(8,128)(2,1)S(1)}, bf16[96,768]{1,0:T(8,128)(2,1)S(1)}, u32[]{:S(2)}, u32[]{:S(2)}) collective-permute-start(bf16[96,768]{1,0:T(8,128)(2,1)S(1)} %get-tuple-element.326), channel_id=1, source_target_pairs={{0,24},{4,28},{8,0},{12,4},{16,8},{20,12},{24,16},{28,20},{1,25},{... | collective-permute-start | bytes 442376 | tf_op jit(solution)/shard_map/ppermute | solution.py:226
  168.0 8.0 %attend_back.4 = (bf16[400,768]{1,0:T(8,128)(2,1)S(1)}, bf16[400,768]{1,0:T(8,128)(2,1)S(1)}, bf16[1024,640]{1,0:T(8,128)(2,1)S(1)}) custom-call(s32[29]{0:T(128)S(1)} %concatenate.12.place, bf16[768,1024]{1,0:T(8,128)(2,1)} %bitcast.52, bf16[1024,640]{1,0:T(8,128)(2,1)} %get-tuple-element.315.kept, bf16[4,1024,192]{2,1,0:T(8,128)(2,1)} %get-tuple-element.316.grad_context, ...), custom_call_target="tpu_custom_call" | custom-call | flops 10000000000 | bytes 12000000 | tf_op jit(solution)/shard_map/attend_back/pallas_call | solution.py:79
  176.1 5.0 %collective-permute-done.30 = bf16[96,768]{1,0:T(8,128)(2,1)S(1)} collective-permute-done((bf16[96,768]{1,0:T(8,128)(2,1)S(1)}, bf16[96,768]{1,0:T(8,128)(2,1)S(1)}, u32[]{:S(2)}, u32[]{:S(2)}) %collective-permute-start.30) | collective-permute-done | bytes 147488 | tf_op jit(solution)/shard_map/ppermute | solution.py:226
  181.4 1.5 collective-permute-start.33
  182.9 8.0 %attend_back.5 = (bf16[400,768]{1,0:T(8,128)(2,1)S(1)}, bf16[400,768]{1,0:T(8,128)(2,1)S(1)}, bf16[1024,640]{1,0:T(8,128)(2,1)S(1)}) custom-call(s32[29]{0:T(128)S(1)} %concatenate.12.place, bf16[768,1024]{1,0:T(8,128)(2,1)} %bitcast.53, bf16[1024,640]{1,0:T(8,128)(2,1)} %get-tuple-element.332.kept, bf16[4,1024,192]{2,1,0:T(8,128)(2,1)} %get-tuple-element.316.grad_context, ...), custom_call_target="tpu_custom_call" | custom-call | flops 10000000000 | bytes 12000000 | tf_op jit(solution)/shard_map/attend_back/pallas_call | solution.py:79
  192.0 2.0 collective-permute-start.35
  194.0 1.2 collective-permute-start.34
  195.2 8.2 %attend_back.6 = (bf16[400,768]{1,0:T(8,128)(2,1)S(1)}, bf16[400,768]{1,0:T(8,128)(2,1)S(1)}, bf16[1024,640]{1,0:T(8,128)(2,1)S(1)}) custom-call(s32[29]{0:T(128)S(1)} %concatenate.12.place, bf16[768,1024]{1,0:T(8,128)(2,1)} %bitcast.54, bf16[1024,640]{1,0:T(8,128)(2,1)} %get-tuple-element.341.kept, bf16[4,1024,192]{2,1,0:T(8,128)(2,1)} %get-tuple-element.316.grad_context, ...), custom_call_target="tpu_custom_call" | custom-call | flops 10000000000 | bytes 12000000 | tf_op jit(solution)/shard_map/attend_back/pallas_call | solution.py:79
  204.2 2.0 collective-permute-done.38
  206.8 1.7 collective-permute-start.41
  209.6 1.5 collective-permute-start.40
  211.1 8.0 %attend_back.7 = (bf16[400,768]{1,0:T(8,128)(2,1)S(1)}, bf16[400,768]{1,0:T(8,128)(2,1)S(1)}, bf16[1024,640]{1,0:T(8,128)(2,1)S(1)}) custom-call(s32[29]{0:T(128)S(1)} %concatenate.12.place, bf16[768,1024]{1,0:T(8,128)(2,1)} %bitcast.55, bf16[1024,640]{1,0:T(8,128)(2,1)} %get-tuple-element.356.kept, bf16[4,1024,192]{2,1,0:T(8,128)(2,1)} %get-tuple-element.316.grad_context, ...), custom_call_target="tpu_custom_call" | custom-call | flops 10000000000 | bytes 12000000 | tf_op jit(solution)/shard_map/attend_back/pallas_call | solution.py:79
  219.1 5.0 %collective-permute-done.39.refs_2_ = bf16[400,768]{1,0:T(8,128)(2,1)S(1)} collective-permute-done((bf16[400,768]{1,0:T(8,128)(2,1)S(1)}, bf16[400,768]{1,0:T(8,128)(2,1)S(1)}, u32[]{:S(2)}, u32[]{:S(2)}) %collective-permute-start.39) | collective-permute-done | bytes 614432 | tf_op jit(solution)/shard_map/ppermute | solution.py:226
  225.8 1.2 collective-permute-done.42.refs_1_
  227.8 2.6 %collective-permute-start.43 = (bf16[112,768]{1,0:T(8,128)(2,1)S(1)}, bf16[112,768]{1,0:T(8,128)(2,1)S(1)}, u32[]{:S(2)}, u32[]{:S(2)}) collective-permute-start(bf16[112,768]{1,0:T(8,128)(2,1)S(1)} %get-tuple-element.376), channel_id=1, source_target_pairs={{0,24},{4,28},{8,0},{12,4},{16,8},{20,12},{24,16},{28,20},{1,25},{... | collective-permute-start | bytes 516104 | tf_op jit(solution)/shard_map/ppermute | solution.py:226
  230.5 1.7 collective-permute-start.44
  232.1 10.7 %input_grad.1 = f32[1024,768]{1,0:T(8,128)} custom-call(s32[29]{0:T(128)S(1)} %concatenate.12.place, f32[1024,768]{1,0:T(8,128)} %get-tuple-element.371.inner, bf16[1024,640]{1,0:T(8,128)(2,1)} %copy-done.6, bf16[1024,640]{1,0:T(8,128)(2,1)} %copy-done.4, bf16[1024,640]{1,0:T(8,128)(2,1)} %copy-done.5, bf16[1024,640]{1,0:T(8,128)(2,1)} %copy-done.3, ...), custom_call_target="tpu_custom_call" | custom-call | flops 5000000000 | bytes 15000000 | tf_op jit(solution)/shard_map/input_grad/pallas_call | solution.py:79
  242.9 4.7 %collective-permute-done.44.refs_1_ = bf16[112,768]{1,0:T(8,128)(2,1)S(1)} collective-permute-done((bf16[112,768]{1,0:T(8,128)(2,1)S(1)}, bf16[112,768]{1,0:T(8,128)(2,1)S(1)}, u32[]{:S(2)}, u32[]{:S(2)}) %collective-permute-start.44) | collective-permute-done | bytes 172064 | tf_op jit(solution)/shard_map/ppermute | solution.py:226
  (109 shorter events, 19.6 us)
Async XLA Ops:
  1.7 9.9 %collective-permute-start = (bf16[96,768]{1,0:T(8,128)(2,1)S(1)}, bf16[96,768]{1,0:T(8,128)(2,1)S(1)}, u32[]{:S(2)}, u32[]{:S(2)}) collective-permute-start(bf16[96,768]{1,0:T(8,128)(2,1)S(1)} %get-tuple-element.215.refs_0_), channel_id=1, source_target_pairs={{0,8},{4,12},{8,16},{12,20},{16,24},{20,28},{24,0},{28,4},{1,9},{5... | collective-permute-start | bytes 442376 | tf_op jit(solution)/shard_map/ppermute | solution.py:226
  4.8 12.3 %collective-permute-start.1 = (bf16[96,768]{1,0:T(8,128)(2,1)S(1)}, bf16[96,768]{1,0:T(8,128)(2,1)S(1)}, u32[]{:S(2)}, u32[]{:S(2)}) collective-permute-start(bf16[96,768]{1,0:T(8,128)(2,1)S(1)} %get-tuple-element.215.refs_0_), channel_id=1, source_target_pairs={{0,16},{4,20},{8,24},{12,28},{16,0},{20,4},{24,8},{28,12},{1,17},{... | collective-permute-start | bytes 442376 | tf_op jit(solution)/shard_map/ppermute | solution.py:226
  7.4 9.7 %collective-permute-start.2 = (bf16[96,768]{1,0:T(8,128)(2,1)S(1)}, bf16[96,768]{1,0:T(8,128)(2,1)S(1)}, u32[]{:S(2)}, u32[]{:S(2)}) collective-permute-start(bf16[96,768]{1,0:T(8,128)(2,1)S(1)} %get-tuple-element.215.refs_0_), channel_id=1, source_target_pairs={{0,24},{4,28},{8,0},{12,4},{16,8},{20,12},{24,16},{28,20},{1,25},{... | collective-permute-start | bytes 442376 | tf_op jit(solution)/shard_map/ppermute | solution.py:226
  8.8 18.9 %copy-start = (bf16[1024,768]{1,0:T(8,128)(2,1)S(1)}, bf16[1024,768]{1,0:T(8,128)(2,1)}, u32[]{:S(2)}) copy-start(bf16[1024,768]{1,0:T(8,128)(2,1)} %x.9) | copy-start | bytes 4718596
  11.5 16.1 %copy-start.2 = (s32[1,8]{1,0:T(1,128)S(1)}, s32[1,8]{1,0:T(1,128)}, u32[]{:S(2)}) copy-start(s32[1,8]{1,0:T(1,128)} %param.21) | copy-start | bytes 100
  17.7 9.1 %collective-permute-start.3 = (bf16[400,768]{1,0:T(8,128)(2,1)S(1)}, bf16[400,768]{1,0:T(8,128)(2,1)S(1)}, u32[]{:S(2)}, u32[]{:S(2)}) collective-permute-start(bf16[400,768]{1,0:T(8,128)(2,1)S(1)} %line_up_rows.1.own), channel_id=1, source_target_pairs={{0,4},{4,0},{8,12},{12,8},{16,20},{20,16},{24,28},{28,24},{1,5},{5... | collective-permute-start | bytes 1843208 | tf_op jit(solution)/shard_map/ppermute | solution.py:226
  17.8 18.8 %collective-permute-start.4 = (bf16[400,768]{1,0:T(8,128)(2,1)S(1)}, bf16[400,768]{1,0:T(8,128)(2,1)S(1)}, u32[]{:S(2)}, u32[]{:S(2)}) collective-permute-start(bf16[400,768]{1,0:T(8,128)(2,1)S(1)} %line_up_rows.1.own), channel_id=1, source_target_pairs={{0,1},{1,0},{2,3},{3,2},{4,5},{5,4},{6,7},{7,6},{8,9},{9,8},{10,11... | collective-permute-start | bytes 1843208 | tf_op jit(solution)/shard_map/ppermute | solution.py:226
  19.3 17.2 %collective-permute-start.5 = (bf16[400,768]{1,0:T(8,128)(2,1)S(1)}, bf16[400,768]{1,0:T(8,128)(2,1)S(1)}, u32[]{:S(2)}, u32[]{:S(2)}) collective-permute-start(bf16[400,768]{1,0:T(8,128)(2,1)S(1)} %line_up_rows.1.own), channel_id=1, source_target_pairs={{0,2},{1,3},{2,0},{3,1},{4,6},{5,7},{6,4},{7,5},{8,10},{9,11},{10,... | collective-permute-start | bytes 1843208 | tf_op jit(solution)/shard_map/ppermute | solution.py:226
  21.5 13.1 %collective-permute-start.6 = (bf16[96,768]{1,0:T(8,128)(2,1)S(1)}, bf16[96,768]{1,0:T(8,128)(2,1)S(1)}, u32[]{:S(2)}, u32[]{:S(2)}) collective-permute-start(bf16[96,768]{1,0:T(8,128)(2,1)S(1)} %copy-done.1), channel_id=1, source_target_pairs={{0,8},{4,12},{8,16},{12,20},{16,24},{20,28},{24,0},{28,4},{1,9},{5... | collective-permute-start | bytes 442376 | tf_op jit(solution)/shard_map/ppermute | solution.py:226
  25.2 11.4 %collective-permute-start.7 = (bf16[96,768]{1,0:T(8,128)(2,1)S(1)}, bf16[96,768]{1,0:T(8,128)(2,1)S(1)}, u32[]{:S(2)}, u32[]{:S(2)}) collective-permute-start(bf16[96,768]{1,0:T(8,128)(2,1)S(1)} %copy-done.1), channel_id=1, source_target_pairs={{0,16},{4,20},{8,24},{12,28},{16,0},{20,4},{24,8},{28,12},{1,17},{... | collective-permute-start | bytes 442376 | tf_op jit(solution)/shard_map/ppermute | solution.py:226
  26.8 9.7 %collective-permute-start.8 = (bf16[96,768]{1,0:T(8,128)(2,1)S(1)}, bf16[96,768]{1,0:T(8,128)(2,1)S(1)}, u32[]{:S(2)}, u32[]{:S(2)}) collective-permute-start(bf16[96,768]{1,0:T(8,128)(2,1)S(1)} %copy-done.1), channel_id=1, source_target_pairs={{0,24},{4,28},{8,0},{12,4},{16,8},{20,12},{24,16},{28,20},{1,25},{... | collective-permute-start | bytes 442376 | tf_op jit(solution)/shard_map/ppermute | solution.py:226
  36.6 7.0 %collective-permute-start.9 = (bf16[400,768]{1,0:T(8,128)(2,1)S(1)}, bf16[400,768]{1,0:T(8,128)(2,1)S(1)}, u32[]{:S(2)}, u32[]{:S(2)}) collective-permute-start(bf16[400,768]{1,0:T(8,128)(2,1)S(1)} %collective-permute-done.4.own), channel_id=1, source_target_pairs={{0,4},{4,0},{8,12},{12,8},{16,20},{20,16},{24,28},{28,24},{1,5},{5... | collective-permute-start | bytes 1843208 | tf_op jit(solution)/shard_map/ppermute | solution.py:226
  36.7 8.2 %collective-permute-start.10 = (bf16[400,768]{1,0:T(8,128)(2,1)S(1)}, bf16[400,768]{1,0:T(8,128)(2,1)S(1)}, u32[]{:S(2)}, u32[]{:S(2)}) collective-permute-start(bf16[400,768]{1,0:T(8,128)(2,1)S(1)} %collective-permute-done.5.own), channel_id=1, source_target_pairs={{0,4},{4,0},{8,12},{12,8},{16,20},{20,16},{24,28},{28,24},{1,5},{5... | collective-permute-start | bytes 1843208 | tf_op jit(solution)/shard_map/ppermute | solution.py:226
  37.8 16.5 %collective-permute-start.11 = (bf16[400,768]{1,0:T(8,128)(2,1)S(1)}, bf16[400,768]{1,0:T(8,128)(2,1)S(1)}, u32[]{:S(2)}, u32[]{:S(2)}) collective-permute-start(bf16[400,768]{1,0:T(8,128)(2,1)S(1)} %broadcast_select_fusion), channel_id=1, source_target_pairs={{0,1},{1,0},{2,3},{3,2},{4,6},{5,7},{6,4},{7,5},{8,9},{9,8},{10,11... | collective-permute-start | bytes 1843208 | tf_op jit(solution)/shard_map/ppermute | solution.py:226
  38.4 15.9 %collective-permute-start.12 = (bf16[1,4,96,768]{3,2,1,0:T(8,128)(2,1)S(1)}, bf16[1,4,96,768]{3,2,1,0:T(8,128)(2,1)S(1)}, u32[]{:S(2)}, u32[]{:S(2)}) collective-permute-start(bf16[1,4,96,768]{3,2,1,0:T(8,128)(2,1)S(1)} %bitcast.45), channel_id=1, source_target_pairs={{0,1},{1,0},{2,3},{3,2},{4,6},{5,7},{6,4},{7,5},{8,9},{9,8},{10,11... | collective-permute-start | bytes 1769480 | tf_op jit(solution)/shard_map/ppermute | solution.py:226
  39.9 12.6 %collective-permute-start.13 = (bf16[192,384]{1,0:T(8,128)(2,1)S(1)}, bf16[192,384]{1,0:T(8,128)(2,1)S(1)}, u32[]{:S(2)}, u32[]{:S(2)}) collective-permute-start(bf16[192,384]{1,0:T(8,128)(2,1)S(1)} %bitcast.56), channel_id=1, source_target_pairs={{0,8},{4,12},{8,16},{12,20},{16,24},{20,28},{24,0},{28,4},{1,9},{5... | collective-permute-start | bytes 442376 | tf_op jit(solution)/shard_map/ppermute | solution.py:226
  43.5 10.7 %collective-permute-start.14 = (bf16[192,384]{1,0:T(8,128)(2,1)S(1)}, bf16[192,384]{1,0:T(8,128)(2,1)S(1)}, u32[]{:S(2)}, u32[]{:S(2)}) collective-permute-start(bf16[192,384]{1,0:T(8,128)(2,1)S(1)} %bitcast.57), channel_id=1, source_target_pairs={{0,16},{4,20},{8,24},{12,28},{16,0},{20,4},{24,8},{28,12},{1,17},{... | collective-permute-start | bytes 442376 | tf_op jit(solution)/shard_map/ppermute | solution.py:226
  44.9 9.4 %collective-permute-start.15 = (bf16[192,384]{1,0:T(8,128)(2,1)S(1)}, bf16[192,384]{1,0:T(8,128)(2,1)S(1)}, u32[]{:S(2)}, u32[]{:S(2)}) collective-permute-start(bf16[192,384]{1,0:T(8,128)(2,1)S(1)} %bitcast.58), channel_id=1, source_target_pairs={{0,24},{4,28},{8,0},{12,4},{16,8},{20,12},{24,16},{28,20},{1,25},{... | collective-permute-start | bytes 442376 | tf_op jit(solution)/shard_map/ppermute | solution.py:226
  54.4 7.6 %collective-permute-start.16 = (bf16[400,768]{1,0:T(8,128)(2,1)S(1)}, bf16[400,768]{1,0:T(8,128)(2,1)S(1)}, u32[]{:S(2)}, u32[]{:S(2)}) collective-permute-start(bf16[400,768]{1,0:T(8,128)(2,1)S(1)} %collective-permute-done.11.own), channel_id=1, source_target_pairs={{0,4},{4,0},{8,12},{12,8},{16,20},{20,16},{24,28},{28,24},{1,5},{5... | collective-permute-start | bytes 1843208 | tf_op jit(solution)/shard_map/ppermute | solution.py:1303
  54.6 19.5 %collective-permute-start.19 = (bf16[1,4,192,384]{3,2,1,0:T(8,128)(2,1)S(1)}, bf16[1,4,192,384]{3,2,1,0:T(8,128)(2,1)S(1)}, u32[]{:S(2)}, u32[]{:S(2)}) collective-permute-start(bf16[1,4,192,384]{3,2,1,0:T(8,128)(2,1)S(1)} %maximum_bitcast_fusion), channel_id=1, source_target_pairs={{0,1},{1,0},{2,3},{3,2},{4,6},{5,7},{6,4},{7,5},{8,9},{9,8},{10,11... | collective-permute-start | bytes 1769480 | tf_op jit(solution)/shard_map/ppermute | solution.py:226
  55.2 21.5 %collective-permute-start.17 = (bf16[2,4,96,768]{3,2,1,0:T(8,128)(2,1)S(1)}, bf16[2,4,96,768]{3,2,1,0:T(8,128)(2,1)S(1)}, u32[]{:S(2)}, u32[]{:S(2)}) collective-permute-start(bf16[2,4,96,768]{3,2,1,0:T(8,128)(2,1)S(1)} %pad_maximum_fusion.u0), channel_id=1, source_target_pairs={{0,2},{1,3},{2,0},{3,1},{4,5},{5,4},{6,7},{7,6},{8,10},{9,11},{10,... | collective-permute-start | bytes 3538952 | tf_op jit(solution)/shard_map/ppermute | solution.py:226
  55.7 21.0 %collective-permute-start.18 = (bf16[2,4,96,768]{3,2,1,0:T(8,128)(2,1)S(1)}, bf16[2,4,96,768]{3,2,1,0:T(8,128)(2,1)S(1)}, u32[]{:S(2)}, u32[]{:S(2)}) collective-permute-start(bf16[2,4,96,768]{3,2,1,0:T(8,128)(2,1)S(1)} %pad_maximum_fusion.u0), channel_id=1, source_target_pairs={{0,4},{4,0},{8,12},{12,8},{16,20},{20,16},{24,28},{28,24},{1,5},{5... | collective-permute-start | bytes 3538952 | tf_op jit(solution)/shard_map/ppermute | solution.py:226
  76.7 2.8 %collective-permute-start.20 = (bf16[2,4,96,768]{3,2,1,0:T(8,128)(2,1)S(1)}, bf16[2,4,96,768]{3,2,1,0:T(8,128)(2,1)S(1)}, u32[]{:S(2)}, u32[]{:S(2)}) collective-permute-start(bf16[2,4,96,768]{3,2,1,0:T(8,128)(2,1)S(1)} %collective-permute-done.17.u1), channel_id=1, source_target_pairs={{0,4},{4,0},{8,12},{12,8},{16,20},{20,16},{24,28},{28,24},{1,5},{5... | collective-permute-start | bytes 3538952 | tf_op jit(solution)/shard_map/ppermute | solution.py:1333
  77.0 16.3 %collective-permute-start.21 = (bf16[2,4,192,384]{3,2,1,0:T(8,128)(2,1)S(1)}, bf16[2,4,192,384]{3,2,1,0:T(8,128)(2,1)S(1)}, u32[]{:S(2)}, u32[]{:S(2)}) collective-permute-start(bf16[2,4,192,384]{3,2,1,0:T(8,128)(2,1)S(1)} %pad_maximum_fusion.1.d0), channel_id=1, source_target_pairs={{0,2},{1,3},{2,0},{3,1},{4,5},{5,4},{6,7},{7,6},{8,10},{9,11},{10,... | collective-permute-start | bytes 3538952 | tf_op jit(solution)/shard_map/ppermute | solution.py:226
  77.7 15.5 %collective-permute-start.22 = (bf16[2,4,192,384]{3,2,1,0:T(8,128)(2,1)S(1)}, bf16[2,4,192,384]{3,2,1,0:T(8,128)(2,1)S(1)}, u32[]{:S(2)}, u32[]{:S(2)}) collective-permute-start(bf16[2,4,192,384]{3,2,1,0:T(8,128)(2,1)S(1)} %pad_maximum_fusion.1.d0), channel_id=1, source_target_pairs={{0,4},{4,0},{8,12},{12,8},{16,20},{20,16},{24,28},{28,24},{1,5},{5... | collective-permute-start | bytes 3538952 | tf_op jit(solution)/shard_map/ppermute | solution.py:226
  93.2 2.9 %collective-permute-start.23 = (bf16[2,4,192,384]{3,2,1,0:T(8,128)(2,1)S(1)}, bf16[2,4,192,384]{3,2,1,0:T(8,128)(2,1)S(1)}, u32[]{:S(2)}, u32[]{:S(2)}) collective-permute-start(bf16[2,4,192,384]{3,2,1,0:T(8,128)(2,1)S(1)} %collective-permute-done.21.d1), channel_id=1, source_target_pairs={{0,4},{4,0},{8,12},{12,8},{16,20},{20,16},{24,28},{28,24},{1,5},{5... | collective-permute-start | bytes 3538952 | tf_op jit(solution)/shard_map/ppermute | solution.py:226
  118.3 13.9 %collective-permute-start.24 = (bf16[4,4,96,768]{3,2,1,0:T(8,128)(2,1)}, bf16[4,4,96,768]{3,2,1,0:T(8,128)(2,1)S(1)}, u32[]{:S(2)}, u32[]{:S(2)}) collective-permute-start(bf16[4,4,96,768]{3,2,1,0:T(8,128)(2,1)} %get-tuple-element.292), channel_id=1, source_target_pairs={{0,4},{4,0},{8,12},{12,8},{16,20},{20,16},{24,28},{28,24},{1,5},{5... | collective-permute-start | bytes 7077896 | tf_op jit(solution)/shard_map/ppermute | solution.py:226
  133.0 16.3 %collective-permute-start.25 = (bf16[2,4,96,768]{3,2,1,0:T(8,128)(2,1)S(1)}, bf16[2,4,96,768]{3,2,1,0:T(8,128)(2,1)S(1)}, u32[]{:S(2)}, u32[]{:S(2)}) collective-permute-start(bf16[2,4,96,768]{3,2,1,0:T(8,128)(2,1)S(1)} %get-tuple-element.303), channel_id=1, source_target_pairs={{0,2},{1,3},{2,0},{3,1},{4,5},{5,4},{6,7},{7,6},{8,10},{9,11},{10,... | collective-permute-start | bytes 3538952 | tf_op jit(solution)/shard_map/ppermute | solution.py:226
  150.9 10.3 %collective-permute-start.27 = (bf16[4,4,96,768]{3,2,1,0:T(8,128)(2,1)S(1)}, bf16[4,4,96,768]{3,2,1,0:T(8,128)(2,1)S(1)}, u32[]{:S(2)}, u32[]{:S(2)}) collective-permute-start(bf16[4,4,96,768]{3,2,1,0:T(8,128)(2,1)S(1)} %copy-done.11), channel_id=1, source_target_pairs={{0,4},{4,0},{8,12},{12,8},{16,20},{20,16},{24,28},{28,24},{1,5},{5... | collective-permute-start | bytes 7077896 | tf_op jit(solution)/shard_map/ppermute | solution.py:226
  150.9 10.2 %collective-permute-start.26 = (bf16[1,4,96,768]{3,2,1,0:T(8,128)(2,1)S(1)}, bf16[1,4,96,768]{3,2,1,0:T(8,128)(2,1)S(1)}, u32[]{:S(2)}, u32[]{:S(2)}) collective-permute-start(bf16[1,4,96,768]{3,2,1,0:T(8,128)(2,1)S(1)} %get-tuple-element.309), channel_id=1, source_target_pairs={{0,1},{1,0},{2,3},{3,2},{4,6},{5,7},{6,4},{7,5},{8,9},{9,8},{10,11... | collective-permute-start | bytes 1769480 | tf_op jit(solution)/shard_map/ppermute | solution.py:226
  162.0 19.0 %collective-permute-start.28 = (bf16[2,4,96,768]{3,2,1,0:T(8,128)(2,1)S(1)}, bf16[2,4,96,768]{3,2,1,0:T(8,128)(2,1)S(1)}, u32[]{:S(2)}, u32[]{:S(2)}) collective-permute-start(bf16[2,4,96,768]{3,2,1,0:T(8,128)(2,1)S(1)} %get-tuple-element.325), channel_id=1, source_target_pairs={{0,2},{1,3},{2,0},{3,1},{4,5},{5,4},{6,7},{7,6},{8,10},{9,11},{10,... | collective-permute-start | bytes 3538952 | tf_op jit(solution)/shard_map/ppermute | solution.py:226
  162.8 13.2 %collective-permute-start.29 = (bf16[96,768]{1,0:T(8,128)(2,1)S(1)}, bf16[96,768]{1,0:T(8,128)(2,1)S(1)}, u32[]{:S(2)}, u32[]{:S(2)}) collective-permute-start(bf16[96,768]{1,0:T(8,128)(2,1)S(1)} %get-tuple-element.326), channel_id=1, source_target_pairs={{0,24},{4,28},{8,0},{12,4},{16,8},{20,12},{24,16},{28,20},{1,25},{... | collective-permute-start | bytes 442376 | tf_op jit(solution)/shard_map/ppermute | solution.py:226
  167.5 13.6 %collective-permute-start.30 = (bf16[96,768]{1,0:T(8,128)(2,1)S(1)}, bf16[96,768]{1,0:T(8,128)(2,1)S(1)}, u32[]{:S(2)}, u32[]{:S(2)}) collective-permute-start(bf16[96,768]{1,0:T(8,128)(2,1)S(1)} %get-tuple-element.327), channel_id=1, source_target_pairs={{0,16},{4,20},{8,24},{12,28},{16,0},{20,4},{24,8},{28,12},{1,17},{... | collective-permute-start | bytes 442376 | tf_op jit(solution)/shard_map/ppermute | solution.py:226
  167.9 13.2 %collective-permute-start.31 = (bf16[96,768]{1,0:T(8,128)(2,1)S(1)}, bf16[96,768]{1,0:T(8,128)(2,1)S(1)}, u32[]{:S(2)}, u32[]{:S(2)}) collective-permute-start(bf16[96,768]{1,0:T(8,128)(2,1)S(1)} %get-tuple-element.328), channel_id=1, source_target_pairs={{0,8},{4,12},{8,16},{12,20},{16,24},{20,28},{24,0},{28,4},{1,9},{5... | collective-permute-start | bytes 442376 | tf_op jit(solution)/shard_map/ppermute | solution.py:226
  181.4 9.9 %collective-permute-start.33 = (bf16[1,4,96,768]{3,2,1,0:T(8,128)(2,1)S(1)}, bf16[1,4,96,768]{3,2,1,0:T(8,128)(2,1)S(1)}, u32[]{:S(2)}, u32[]{:S(2)}) collective-permute-start(bf16[1,4,96,768]{3,2,1,0:T(8,128)(2,1)S(1)} %get-tuple-element.336), channel_id=1, source_target_pairs={{0,1},{1,0},{2,3},{3,2},{4,6},{5,7},{6,4},{7,5},{8,9},{9,8},{10,11... | collective-permute-start | bytes 1769480 | tf_op jit(solution)/shard_map/ppermute | solution.py:226
  182.9 8.4 %collective-permute-start.32 = (bf16[400,768]{1,0:T(8,128)(2,1)S(1)}, bf16[400,768]{1,0:T(8,128)(2,1)S(1)}, u32[]{:S(2)}, u32[]{:S(2)}) collective-permute-start(bf16[400,768]{1,0:T(8,128)(2,1)S(1)} %get-tuple-element.335), channel_id=1, source_target_pairs={{0,4},{4,0},{8,12},{12,8},{16,20},{20,16},{24,28},{28,24},{1,5},{5... | collective-permute-start | bytes 1843208 | tf_op jit(solution)/shard_map/ppermute | solution.py:226
  192.0 11.4 %collective-permute-start.35 = (bf16[96,768]{1,0:T(8,128)(2,1)S(1)}, bf16[96,768]{1,0:T(8,128)(2,1)S(1)}, u32[]{:S(2)}, u32[]{:S(2)}) collective-permute-start(bf16[96,768]{1,0:T(8,128)(2,1)S(1)} %get-tuple-element.345), channel_id=1, source_target_pairs={{0,24},{4,28},{8,0},{12,4},{16,8},{20,12},{24,16},{28,20},{1,25},{... | collective-permute-start | bytes 442376 | tf_op jit(solution)/shard_map/ppermute | solution.py:226
  194.0 9.4 %collective-permute-start.36 = (bf16[96,768]{1,0:T(8,128)(2,1)S(1)}, bf16[96,768]{1,0:T(8,128)(2,1)S(1)}, u32[]{:S(2)}, u32[]{:S(2)}) collective-permute-start(bf16[96,768]{1,0:T(8,128)(2,1)S(1)} %get-tuple-element.346), channel_id=1, source_target_pairs={{0,8},{4,12},{8,16},{12,20},{16,24},{20,28},{24,0},{28,4},{1,9},{5... | collective-permute-start | bytes 442376 | tf_op jit(solution)/shard_map/ppermute | solution.py:226
  194.0 10.1 %collective-permute-start.34 = (bf16[400,768]{1,0:T(8,128)(2,1)S(1)}, bf16[400,768]{1,0:T(8,128)(2,1)S(1)}, u32[]{:S(2)}, u32[]{:S(2)}) collective-permute-start(bf16[400,768]{1,0:T(8,128)(2,1)S(1)} %add_convert_fusion.6), channel_id=1, source_target_pairs={{0,1},{1,0},{2,3},{3,2},{4,6},{5,7},{6,4},{7,5},{8,9},{9,8},{10,11... | collective-permute-start | bytes 1843208 | tf_op jit(solution)/shard_map/ppermute | solution.py:226
  195.2 9.0 %collective-permute-start.37 = (bf16[400,768]{1,0:T(8,128)(2,1)S(1)}, bf16[400,768]{1,0:T(8,128)(2,1)S(1)}, u32[]{:S(2)}, u32[]{:S(2)}) collective-permute-start(bf16[400,768]{1,0:T(8,128)(2,1)S(1)} %get-tuple-element.347), channel_id=1, source_target_pairs={{0,4},{4,0},{8,12},{12,8},{16,20},{20,16},{24,28},{28,24},{1,5},{5... | collective-permute-start | bytes 1843208 | tf_op jit(solution)/shard_map/ppermute | solution.py:226
  204.2 2.0 collective-permute-start.38
  206.8 12.3 %collective-permute-start.41 = (bf16[96,768]{1,0:T(8,128)(2,1)S(1)}, bf16[96,768]{1,0:T(8,128)(2,1)S(1)}, u32[]{:S(2)}, u32[]{:S(2)}) collective-permute-start(bf16[96,768]{1,0:T(8,128)(2,1)S(1)} %get-tuple-element.361), channel_id=1, source_target_pairs={{0,16},{4,20},{8,24},{12,28},{16,0},{20,4},{24,8},{28,12},{1,17},{... | collective-permute-start | bytes 442376 | tf_op jit(solution)/shard_map/ppermute | solution.py:226
  208.4 15.6 %collective-permute-start.39 = (bf16[400,768]{1,0:T(8,128)(2,1)S(1)}, bf16[400,768]{1,0:T(8,128)(2,1)S(1)}, u32[]{:S(2)}, u32[]{:S(2)}) collective-permute-start(bf16[400,768]{1,0:T(8,128)(2,1)S(1)} %get-tuple-element.359), channel_id=1, source_target_pairs={{0,1},{1,0},{2,3},{3,2},{4,5},{5,4},{6,7},{7,6},{8,9},{9,8},{10,11... | collective-permute-start | bytes 1843208 | tf_op jit(solution)/shard_map/ppermute | solution.py:226
  209.6 15.3 %collective-permute-start.40 = (bf16[400,768]{1,0:T(8,128)(2,1)S(1)}, bf16[400,768]{1,0:T(8,128)(2,1)S(1)}, u32[]{:S(2)}, u32[]{:S(2)}) collective-permute-start(bf16[400,768]{1,0:T(8,128)(2,1)S(1)} %get-tuple-element.360), channel_id=1, source_target_pairs={{0,2},{1,3},{2,0},{3,1},{4,6},{5,7},{6,4},{7,5},{8,10},{9,11},{10,... | collective-permute-start | bytes 1843208 | tf_op jit(solution)/shard_map/ppermute | solution.py:226
  224.9 2.0 collective-permute-start.42
  227.8 15.0 %collective-permute-start.43 = (bf16[112,768]{1,0:T(8,128)(2,1)S(1)}, bf16[112,768]{1,0:T(8,128)(2,1)S(1)}, u32[]{:S(2)}, u32[]{:S(2)}) collective-permute-start(bf16[112,768]{1,0:T(8,128)(2,1)S(1)} %get-tuple-element.376), channel_id=1, source_target_pairs={{0,24},{4,28},{8,0},{12,4},{16,8},{20,12},{24,16},{28,20},{1,25},{... | collective-permute-start | bytes 516104 | tf_op jit(solution)/shard_map/ppermute | solution.py:226
  230.5 17.1 %collective-permute-start.44 = (bf16[112,768]{1,0:T(8,128)(2,1)S(1)}, bf16[112,768]{1,0:T(8,128)(2,1)S(1)}, u32[]{:S(2)}, u32[]{:S(2)}) collective-permute-start(bf16[112,768]{1,0:T(8,128)(2,1)S(1)} %get-tuple-element.377), channel_id=1, source_target_pairs={{0,16},{4,20},{8,24},{12,28},{16,0},{20,4},{24,8},{28,12},{1,17},{... | collective-permute-start | bytes 516104 | tf_op jit(solution)/shard_map/ppermute | solution.py:226
  232.1 15.5 %collective-permute-start.45 = (bf16[112,768]{1,0:T(8,128)(2,1)S(1)}, bf16[112,768]{1,0:T(8,128)(2,1)S(1)}, u32[]{:S(2)}, u32[]{:S(2)}) collective-permute-start(bf16[112,768]{1,0:T(8,128)(2,1)S(1)} %get-tuple-element.378), channel_id=1, source_target_pairs={{0,8},{4,12},{8,16},{12,20},{16,24},{20,28},{24,0},{28,4},{1,9},{5... | collective-permute-start | bytes 516104 | tf_op jit(solution)/shard_map/ppermute | solution.py:226
  (10 other events, 63.2 us)
